TPU v7x, 32 devices: a whole 2x2x4 slice. The times are simulated.
32 devices in a mesh: group: 2 (over x), tensor: 8 (over z, y), side: 2 (over core).
Axes of the slice: x: 2, y: 2, z: 4, core: 2. Of those that a mesh axis runs over, the one named last changes fastest.
Arguments:
- hidden_pre: bfloat16 [32, 64, 4096], P('group', None, ('tensor', 'side')), parts along dimension 0, may hold values from -6 to 6
- coeff_pre: bfloat16 [32, 64, 2048], P(('group', 'tensor', 'side')), parts along dimension 0, may hold values from -6 to 6
- gate_pre: bfloat16 [32, 64, 4096], P('group', None, ('tensor', 'side')), parts along dimension 0, may hold values from -6 to 6
- step_raw: float32 [64, 32, 64], P(('tensor', 'side'), 'group'), parts along dimension 1, may hold values from -6 to 6
- cache_rows: bfloat16 [32, 64, 2048], P('group', ('tensor', 'side')), parts along dimension 0, may hold values from -6 to 6
- lengths: int32 [32], P('group'), parts along dimension 0, may hold values from 1 to 64, 512 in all
- owners: int32 [32, 1], P('group'), parts along dimension 0, may hold values from 0 to 15, as said below
- page_table: int32 [32, 8], P(('group', 'tensor', 'side')), parts along dimension 0, may hold values from 0 to 7, each once within a row
- conv_hidden: bfloat16 [4, 4096], replicated, may hold values from -3 to 3
- conv_coeff: bfloat16 [4, 2048], replicated, may hold values from -3 to 3
- step_bias: float32 [64], replicated, may hold values from -2 to 0
- decay_log: float32 [64], replicated, may hold values from -6.5 to -2
- skip_gain: float32 [64], replicated, may hold values from 0.5 to 1.5
- norm_gain: float32 [4096], replicated, may hold values from 0.5 to 1.5
- new_hidden: bfloat16 [64, 2, 4096], P(('group', 'tensor', 'side')), parts along dimension 0, may hold values from -6 to 6
- new_coeff: bfloat16 [64, 2, 2048], P(('group', 'tensor', 'side')), parts along dimension 0, may hold values from -6 to 6
- new_gate: bfloat16 [64, 2, 4096], P(('group', 'tensor', 'side')), parts along dimension 0, may hold values from -6 to 6
- new_step: float32 [64, 2, 64], P(('group', 'tensor', 'side')), parts along dimension 0, may hold values from -6 to 6
- new_query: bfloat16 [64, 2, 8192], P(('group', 'tensor', 'side')), parts along dimension 0, may hold values from -6 to 6
- new_cache: bfloat16 [64, 2, 2048], P(('group', 'tensor', 'side')), parts along dimension 0, may hold values from -6 to 6
Outputs:
- prefill_out: bfloat16 [32, 64, 4096], P('group', None, ('tensor', 'side')), parts along dimension 0
- cache_pool: bfloat16 [256, 16, 2048], P(('group', 'tensor', 'side')), parts along dimension 0
- decode_mixer: bfloat16 [64, 2, 4096], P(('group', 'tensor', 'side')), parts along dimension 0
- decode_attention: bfloat16 [64, 2, 8192], P(('group', 'tensor', 'side')), parts along dimension 0
There are 2 independent parts, one for each index of `group`. A program takes and returns all parts, laid end to end along the dimension named above; an argument that names none is the same for every part. Nothing has to cross between parts.
Inputs may be any that keep to these rules, and one draw needn't show every extreme that they name: `lengths`: they add up to 512; the longest prompt has exactly 64 positions. 4 owners get two prompts, 8 owners get one, the others none. `page_table`: each row is a permutation of the owner's pages.
All inputs are finite; a program needn't handle non-finite values.
Results may differ from a plain program's by a relative error of at most 0.0054.
Values may be sent and summed in bfloat16 or wider, within the bound.
No kernel may reach another device: no remote copies, remote signals or barrier semaphores. Data moves between devices by JAX's collectives and lax.ppermute only.
A program may use at most 128 MiB of HBM per device.

v0:
```python
import jax
import jax.numpy as jnp
from jax import lax
from jax.sharding import PartitionSpec as P

GROUPS = 8
CONVK = 4
KVH = 8
KVD = 128
BLK = 16


epsilon = 1e-05


def causal_conv(padded, weight):
    row_count = padded.shape[-2] - weight.shape[0] + 1
    running = jnp.zeros(padded.shape[:-2] + (row_count, padded.shape[-1]), jnp.float32)
    for tap_index in range(weight.shape[0]):
        running = running + padded[..., tap_index : tap_index + row_count, :] * weight[tap_index]
    return jax.nn.silu(running).astype(jnp.bfloat16)


def take_tail(rows_padded, length):
    return lax.dynamic_slice_in_dim(rows_padded, length, CONVK - 1, 0)


def local(
    hidden_pre,
    coeff_pre,
    gate_pre,
    step_raw,
    cache_rows,
    lengths,
    owners,
    page_table,
    conv_hidden,
    conv_coeff,
    step_bias,
    decay_log,
    skip_gain,
    norm_gain,
    new_hidden,
    new_coeff,
    new_gate,
    new_step,
    new_query,
    new_cache,
):
    device_count = lax.axis_size(("tensor", "side"))
    device_index = lax.axis_index(("tensor", "side"))
    prompts, span, local_cols = hidden_pre.shape
    local_heads = step_raw.shape[0]
    head_size = local_cols // local_heads
    pair_width = coeff_pre.shape[2] // GROUPS
    state_size = pair_width // 2
    heads = decay_log.shape[0]
    width = conv_hidden.shape[1]
    slots = new_hidden.shape[0]
    steps = new_hidden.shape[1]
    cache_width = cache_rows.shape[2]
    local_positions = cache_rows.shape[1]
    group_devs = device_count // GROUPS
    group_index = device_index // group_devs
    piece_width = pair_width // group_devs
    own_coeff = jnp.transpose(coeff_pre[0].reshape(span, GROUPS, pair_width), (1, 0, 2))
    send_coeff = jnp.repeat(own_coeff, group_devs, axis=0)
    group_coeff = lax.all_to_all(
        send_coeff, ("tensor", "side"), split_axis=0, concat_axis=0, tiled=True
    )
    weight_hidden = lax.dynamic_slice_in_dim(
        conv_hidden, device_index * local_cols, local_cols, 1
    ).astype(jnp.float32)
    weight_coeff = lax.dynamic_slice_in_dim(
        conv_coeff, group_index * pair_width, pair_width, 1
    ).astype(jnp.float32)
    local_bias = lax.dynamic_slice_in_dim(step_bias, device_index * local_heads, local_heads, 0)
    local_rate = -jnp.exp(
        lax.dynamic_slice_in_dim(decay_log, device_index * local_heads, local_heads, 0)
    )
    local_skip = lax.dynamic_slice_in_dim(skip_gain, device_index * local_heads, local_heads, 0)
    local_gain = lax.dynamic_slice_in_dim(norm_gain, device_index * local_cols, local_cols, 0)
    positions = jnp.arange(span)
    is_valid = positions[None, :] < lengths[:, None]
    hidden_padded = jnp.pad(hidden_pre, ((0, 0), (CONVK - 1, 0), (0, 0)))
    coeff_padded = jnp.pad(group_coeff, ((0, 0), (CONVK - 1, 0), (0, 0)))
    hidden_conv = causal_conv(hidden_padded.astype(jnp.float32), weight_hidden)
    coeff_conv = causal_conv(coeff_padded.astype(jnp.float32), weight_coeff)
    b_local = coeff_conv[:, :, :state_size]
    c_local = coeff_conv[:, :, state_size:]
    step_size = jax.nn.softplus(step_raw + local_bias[:, None, None]) * is_valid[None]
    cumulative = jnp.cumsum(step_size * local_rate[:, None, None], axis=2)
    group_scores = jnp.einsum("rtn,rsn->rts", c_local, b_local, preferred_element_type=jnp.float32)
    lower = positions[:, None] >= positions[None, :]
    segment = jnp.exp(
        jnp.where(lower, cumulative[..., :, None] - cumulative[..., None, :], -jnp.inf)
    )
    mixing = (group_scores[None] * segment * step_size[:, :, None, :]).astype(jnp.bfloat16)
    hidden_heads = hidden_conv.reshape(prompts, span, local_heads, head_size)
    output_heads = jnp.einsum(
        "hrts,rshd->rthd", mixing, hidden_heads, preferred_element_type=jnp.float32
    ) + local_skip[:, None] * hidden_heads.astype(jnp.float32)
    end_weight = jnp.exp(cumulative[..., -1:] - cumulative) * step_size
    weighted = (
        hidden_heads.astype(jnp.float32) * jnp.transpose(end_weight, (1, 2, 0))[..., None]
    ).astype(jnp.bfloat16)
    states = jnp.einsum(
        "rshd,rsn->rhdn", weighted, b_local, preferred_element_type=jnp.float32
    ).astype(jnp.bfloat16)
    gated = output_heads.reshape(prompts, span, local_cols) * jax.nn.silu(
        gate_pre.astype(jnp.float32)
    )
    square_sums = lax.psum(jnp.sum(gated * gated, axis=2), ("tensor", "side"))
    row_scale = lax.rsqrt(square_sums / width + epsilon)
    prefill_out = (gated * row_scale[..., None] * local_gain * is_valid[..., None]).astype(
        jnp.bfloat16
    )
    tail_hidden = jax.vmap(take_tail)(hidden_padded, lengths)
    tail_coeff = jax.vmap(take_tail)(coeff_padded, lengths)
    tail_piece = lax.dynamic_slice_in_dim(
        tail_coeff, device_index % group_devs * piece_width, piece_width, 2
    )
    tails = jnp.concatenate([tail_hidden, tail_piece], axis=2)
    cache_places = device_index * local_positions + jnp.arange(local_positions)
    cache_kept = jnp.where(
        (cache_places[None, :] < lengths[:, None])[:, :, None],
        cache_rows,
        jnp.zeros((), jnp.bfloat16),
    )
    owner_id = owners[:, 0]
    request_ids = jnp.arange(prompts, dtype=jnp.int32)
    same_owner = (owner_id[:, None] == owner_id[None, :]) & (
        request_ids[None, :] < request_ids[:, None]
    )
    slot_rank = jnp.sum(same_owner.astype(jnp.int32), axis=1)
    send_target = slot_rank * device_count + owner_id
    send_ids = jnp.arange(slots * device_count, dtype=jnp.int32)
    matches = send_target[None, :] == send_ids[:, None]
    source_ids = jnp.sum(jnp.where(matches, request_ids[None, :], 0), axis=1)
    present = jnp.any(matches, axis=1)

    def pack_rows(values):
        flat_values = values.reshape(prompts, -1)
        picked = jnp.take(flat_values, source_ids, axis=0)
        kept = jnp.where(present[:, None], picked, jnp.zeros((), flat_values.dtype))
        return kept.reshape(slots, device_count, flat_values.shape[1])

    send_state = pack_rows(states)
    send_tail = pack_rows(tails)
    send_cache = pack_rows(cache_kept)
    got_state, got_tail, got_cache = (
        lax.all_to_all(send_state, ("tensor", "side"), split_axis=1, concat_axis=1, tiled=True),
        lax.all_to_all(send_tail, ("tensor", "side"), split_axis=1, concat_axis=1, tiled=True),
        lax.all_to_all(send_cache, ("tensor", "side"), split_axis=1, concat_axis=1, tiled=True),
    )
    slot_state = got_state.reshape(slots, heads, head_size, state_size).astype(jnp.float32)
    got_tail = got_tail.reshape(slots, device_count, CONVK - 1, local_cols + piece_width)
    slot_tail_hidden = jnp.transpose(got_tail[..., :local_cols], (0, 2, 1, 3)).reshape(
        slots, CONVK - 1, width
    )
    slot_tail_coeff = jnp.transpose(got_tail[..., local_cols:], (0, 2, 1, 3)).reshape(
        slots, CONVK - 1, device_count * piece_width
    )
    slot_cache = got_cache.reshape(slots, span, cache_width)
    slot_numbers = jnp.arange(slots, dtype=jnp.int32)
    mine = (owner_id == device_index)[None, :] & (slot_rank[None, :] == slot_numbers[:, None])
    slot_length = jnp.sum(jnp.where(mine, lengths[None, :], 0), axis=1)
    slot_fill = jnp.any(mine, axis=1).astype(jnp.float32)
    block_count = span // BLK
    blocks = slot_cache.reshape(slots * block_count, BLK * cache_width)
    table_row = page_table[0]
    page_ids = jnp.arange(slots * block_count, dtype=jnp.int32)
    inverse = jnp.sum(
        jnp.where(table_row[None, :] == page_ids[:, None], page_ids[None, :], 0), axis=1
    )
    cache_pool = jnp.take(blocks, inverse, axis=0).reshape(slots * block_count, BLK, cache_width)
    decay_rate = -jnp.exp(decay_log)
    per_group = heads // GROUPS
    hidden_rows = jnp.concatenate([slot_tail_hidden, new_hidden], axis=1).astype(jnp.float32)
    coeff_rows = jnp.concatenate([slot_tail_coeff, new_coeff], axis=1).astype(jnp.float32)
    decode_hidden = causal_conv(hidden_rows, conv_hidden.astype(jnp.float32))
    decode_coeff = causal_conv(coeff_rows, conv_coeff.astype(jnp.float32)).reshape(
        slots, steps, GROUPS, 2, state_size
    )
    mixer_rows = []
    for step_index in range(steps):
        step_now = jax.nn.softplus(new_step[:, step_index, :] + step_bias)
        hidden_now = (
            decode_hidden[:, step_index].reshape(slots, heads, head_size).astype(jnp.float32)
        )
        b_now = jnp.repeat(decode_coeff[:, step_index, :, 0, :], per_group, axis=1).astype(
            jnp.float32
        )
        c_now = jnp.repeat(decode_coeff[:, step_index, :, 1, :], per_group, axis=1).astype(
            jnp.float32
        )
        slot_state = (
            jnp.exp(step_now * decay_rate)[..., None, None] * slot_state
            + (step_now[..., None] * hidden_now)[..., None] * b_now[:, :, None, :]
        )
        readout = (
            jnp.sum(slot_state * c_now[:, :, None, :], axis=-1)
            + skip_gain[None, :, None] * hidden_now
        )
        gated_now = readout.reshape(slots, width) * jax.nn.silu(
            new_gate[:, step_index].astype(jnp.float32)
        )
        normed = (
            gated_now
            * lax.rsqrt(jnp.mean(gated_now * gated_now, axis=1, keepdims=True) + epsilon)
            * norm_gain
        )
        mixer_rows.append((normed * slot_fill[:, None]).astype(jnp.bfloat16))
    decode_mixer = jnp.stack(mixer_rows, axis=1)
    kv_width = cache_width // 2
    cache_all = jnp.concatenate([slot_cache, new_cache], axis=1)
    key_part = cache_all[..., :kv_width].reshape(slots, span + steps, KVH, KVD)
    value_part = cache_all[..., kv_width:].reshape(slots, span + steps, KVH, KVD)
    query_heads = new_query.reshape(slots, steps, KVH, new_query.shape[2] // (KVH * KVD), KVD)
    logits = jnp.einsum(
        "aqkgd,ajkd->aqkgj", query_heads, key_part, preferred_element_type=jnp.float32
    ) * KVD ** (-0.5)
    places = jnp.arange(span + steps)
    step_ids = jnp.arange(steps)
    is_live = (places[None, None, :] < slot_length[:, None, None]) | (
        places[None, None, :] >= span
    ) & (places[None, None, :] - span <= step_ids[None, :, None])
    is_live = is_live[:, :, None, None, :]
    row_peak = jnp.max(jnp.where(is_live, logits, -jnp.inf), axis=-1, keepdims=True)
    exponent = jnp.exp(jnp.where(is_live, logits - row_peak, -jnp.inf))
    softmax_weights = (exponent / jnp.sum(exponent, axis=-1, keepdims=True)).astype(jnp.bfloat16)
    attended = jnp.einsum(
        "aqkgj,ajkd->aqkgd", softmax_weights, value_part, preferred_element_type=jnp.float32
    )
    decode_attention = (attended.reshape(slots, steps, -1) * slot_fill[:, None, None]).astype(
        jnp.bfloat16
    )
    return (prefill_out, cache_pool, decode_mixer, decode_attention)


def solution(mesh):
    placed = (
        P("group", None, ("tensor", "side")),
        P(("group", "tensor", "side"), None, None),
        P("group", None, ("tensor", "side")),
        P(("tensor", "side"), "group", None),
        P("group", ("tensor", "side"), None),
        P("group"),
        P("group", None),
        P(("group", "tensor", "side"), None),
        P(),
        P(),
        P(),
        P(),
        P(),
        P(),
        P(("group", "tensor", "side"), None, None),
        P(("group", "tensor", "side"), None, None),
        P(("group", "tensor", "side"), None, None),
        P(("group", "tensor", "side"), None, None),
        P(("group", "tensor", "side"), None, None),
        P(("group", "tensor", "side"), None, None),
    )
    return jax.shard_map(
        local,
        mesh=mesh,
        in_specs=placed,
        out_specs=(
            P("group", None, ("tensor", "side")),
            P(("group", "tensor", "side"), None, None),
            P(("group", "tensor", "side"), None, None),
            P(("group", "tensor", "side"), None, None),
        ),
        check_vma=False,
    )
```

profile of v0, /device:TPU:15, one launch (start us, length us, event | category | flops | bytes accessed | tf_op | source)
XLA Modules:
  0.0 184.5 jit_solution(3467520980078324477)
XLA Ops:
  0.6 0.9 convert_reduce_fusion
  1.5 0.7 multiply_add_fusion.1
  2.8 0.7 broadcast_compare_fusion
  3.5 1.1 broadcast_select_fusion.4
  4.8 0.9 gather_fusion
  5.9 1.8 broadcast_select_fusion.3
  7.7 6.6 %all-to-all-start.1 = ((bf16[2,16,8192]{2,0,1:T(2,128)(2,1)}), bf16[2,16,8192]{2,0,1:T(2,128)(2,1)S(1)}, u32[]{:S(2)}, u32[]{:S(2)}) async-start(bf16[2,16,8192]{2,0,1:T(2,128)(2,1)} %broadcast_select_fusion.3), calls=%async_computation.1 | async-start | bytes 1048576 | tf_op jit(solution)/shard_map/all_to_all | solution.py:154
  15.5 0.9 reduce_window_sum.11
  16.6 0.6 copy.188
  18.4 1.3 dynamic_slice.26
  19.7 0.6 fusion.77
  20.4 0.6 fusion.75
  21.0 0.6 fusion.76
  21.7 0.7 mul.609
  22.4 0.6 copy.190
  23.1 0.7 reshape.598
  24.4 0.7 gather_fusion.4
  25.0 0.6 multiply_exponential_fusion
  25.7 0.6 iota_compare_fusion
  26.3 0.7 fusion.74
  26.9 0.9 all-to-all-done.1
  27.8 0.8 broadcast_in_dim.160
  28.6 5.2 %all-to-all-start = ((bf16[16,64,256]{2,1,0:T(8,128)(2,1)}), bf16[16,64,256]{2,1,0:T(8,128)(2,1)S(1)}, u32[]{:S(2)}, u32[]{:S(2)}) async-start(bf16[16,64,256]{2,1,0:T(8,128)(2,1)} %bitcast.5), calls=%async_computation | async-start | bytes 1048576 | tf_op jit(solution)/shard_map/all_to_all | solution.py:68
  33.8 0.6 pad_clamp_fusion
  34.4 0.7 fusion.73
  36.2 11.2 %all-to-all-done = bf16[16,64,256]{2,1,0:T(8,128)(2,1)S(1)} async-done(((bf16[16,64,256]{2,1,0:T(8,128)(2,1)}), bf16[16,64,256]{2,1,0:T(8,128)(2,1)S(1)}, u32[]{:S(2)}, u32[]{:S(2)}) %all-to-all-start) | async-done | bytes 524320 | tf_op jit(solution)/shard_map/all_to_all | solution.py:68
  47.8 0.7 gather_fusion.5
  50.0 0.8 gather_fusion.3
  50.8 0.8 broadcast_select_fusion.6
  51.6 5.0 %all-to-all-start.3 = ((bf16[2,16,1152]{2,0,1:T(2,128)(2,1)}), bf16[2,16,1152]{2,0,1:T(2,128)(2,1)S(1)}, u32[]{:S(2)}, u32[]{:S(2)}) async-start(bf16[2,16,1152]{2,0,1:T(2,128)(2,1)} %broadcast_select_fusion.6), calls=%async_computation.3 | async-start | bytes 147456 | tf_op jit(solution)/shard_map/all_to_all | solution.py:153
  56.8 1.3 multiply_convert_fusion.4
  58.7 1.3 multiply_convert_fusion.3
  60.8 0.7 copy.260
  62.0 2.1 %fusion.1 = f32[16,64,4,64]{1,3,2,0:T(8,128)} fusion(bf16[16,64,4,64]{1,3,2,0:T(8,128)(2,1)S(1)} %bitcast.109, f32[4]{0:T(128)S(1)} %copy-done.48, f32[4,16,64]{2,0,1:T(4,128)S(1)} %copy-done.24, f32[4,16,64]{2,0,1:T(4,128)S(1)} %copy-done.23, f32[16,64,64]{2,1,0:T(8,128)S(1)} %fusion.27, pred[64,64]{1,0:T(8,128)(4,1)S(1)} %copy-done.32), kind=kOutput, calls=%fused_computation.14 | convolution fusion | flops 35651584 | bytes 1871888 | tf_op jit(solution)/shard_map/hrts,rshd->rthd/dot_general | solution.py:100
  64.1 2.2 %copy.226 = f32[16,64,256]{2,1,0:T(8,128)S(1)} copy(f32[16,64,256]{1,2,0:T(8,128)} %bitcast.112) | data formatting | bytes 2097152 | tf_op jit(solution)/shard_map/reshape | solution.py:110
  66.7 22.3 %psum.7 = f32[16,64]{1,0:T(8,128)S(1)} all-reduce(f32[16,64]{1,0:T(8,128)S(1)} %multiply_reduce_fusion.2), channel_id=1, replica_groups=mesh['group'=2,'tensor'=8,'side'=2] {'tensor','side'}, use_global_device_ids=true, to_apply=%region_2.3 | all-reduce | flops 1024 | bytes 8192 | tf_op jit(solution)/shard_map/psum | solution.py:113
  89.0 3.3 %gather_fusion.2 = bf16[32,32768]{1,0:T(8,128)(2,1)} fusion(bf16[16,32768]{1,0:T(8,128)(2,1)S(1)} %bitcast.104, s32[1024]{0:T(1024)} %copy-done.33), kind=kCustom, calls=%fused_computation.2 | custom fusion | bytes 4194432 | tf_op jit(solution)/shard_map/jit(_take)/gather | solution.py:144
  92.4 6.7 %broadcast_select_fusion.1 = bf16[2,16,32768]{2,0,1:T(2,128)(2,1)} fusion(pred[2,16]{0,1:T(8,128)(4,1)S(1)} %copy-done.20, pred[2,16]{0,1:T(8,128)(4,1)S(1)} %copy-done.18, bf16[2,16,32768]{2,1,0:T(8,128)(2,1)} %bitcast.107), kind=kLoop, calls=%fused_computation.11 | loop fusion | flops 2097152 | bytes 4194368 | tf_op jit(solution)/shard_map/jit(_where)/select_n | solution.py:145
  99.1 1.1 gather_fusion.1
  100.3 1.4 copy_select_fusion
  101.7 0.7 multiply_convert_fusion.5
  102.4 1.2 multiply_convert_fusion.2
  103.7 15.9 %all-to-all-start.2 = ((bf16[2,16,32768]{2,0,1:T(2,128)(2,1)}), bf16[2,16,32768]{2,0,1:T(2,128)(2,1)S(1)}, u32[]{:S(2)}, u32[]{:S(2)}) async-start(bf16[2,16,32768]{2,0,1:T(2,128)(2,1)} %broadcast_select_fusion.1), calls=%async_computation.2 | async-start | bytes 4194304 | tf_op jit(solution)/shard_map/all_to_all | solution.py:152
  120.7 46.3 %all-to-all-done.2 = bf16[2,16,32768]{2,0,1:T(2,128)(2,1)S(1)} async-done(((bf16[2,16,32768]{2,0,1:T(2,128)(2,1)}), bf16[2,16,32768]{2,0,1:T(2,128)(2,1)S(1)}, u32[]{:S(2)}, u32[]{:S(2)}) %all-to-all-start.2) | async-done | bytes 2097184 | tf_op jit(solution)/shard_map/all_to_all | solution.py:152
  167.1 3.2 %copy_convert_fusion = f32[2,16,32768]{2,1,0:T(8,128)} fusion(bf16[2,16,32768]{2,0,1:T(2,128)(2,1)S(1)} %all-to-all-done.2), kind=kLoop, calls=%fused_computation.16 | loop fusion | flops 1048576 | bytes 6291456 | tf_op jit(solution)/shard_map/convert_element_type | solution.py:156
  170.3 4.9 %reshape.600 = f32[2,64,64,128]{3,2,1,0:T(8,128)} reshape(f32[2,16,32768]{2,1,0:T(8,128)} %copy_convert_fusion) | data formatting | bytes 8388608 | tf_op jit(solution)/shard_map/convert_element_type | solution.py:156
  175.2 8.0 %multiply_reduce_fusion.1 = (f32[2,64,64]{2,1,0:T(8,128)S(1)}, f32[2,64,64]{2,1,0:T(8,128)S(1)}) fusion(f32[2,64,64,128]{3,2,1,0:T(8,128)} %reshape.600, f32[2,64,128]{2,1,0:T(8,128)S(1)} %get-tuple-element.80, f32[2,64,128]{2,1,0:T(8,128)S(1)} %get-tuple-element.81, f32[2,64,64]{2,1,0:T(8,128)S(1)} %get-tuple-element.77, f32[2,64]{1,0:T(2,128)S(1)} %copy-done.39, ...), kind=kLoop, calls=%fused_computation.8 | loop fusion | flops 10469376 | bytes 4588544 | tf_op jit(solution)/shard_map/reduce_sum | solution.py:202
  183.9 0.6 copy.222
  (189 shorter events, 11.0 us)
Async XLA Ops:
  2.7 48.1 %copy-start.17 = (pred[2,16]{0,1:T(8,128)(4,1)}, pred[2,16]{0,1:T(8,128)(4,1)S(1)}, u32[]{:S(2)}) copy-start(pred[2,16]{0,1:T(8,128)(4,1)S(1)} %copy.195) | copy-start | bytes 100
  2.8 48.0 %copy-start.19 = (pred[2,16]{0,1:T(8,128)(4,1)}, pred[2,16]{0,1:T(8,128)(4,1)S(1)}, u32[]{:S(2)}) copy-start(pred[2,16]{0,1:T(8,128)(4,1)S(1)} %copy.194) | copy-start | bytes 100
  2.8 2.9 %copy-start.33 = (s32[1024]{0:T(1024)}, s32[1024]{0:T(1024)S(1)}, u32[]{:S(2)}) copy-start(s32[1024]{0:T(1024)S(1)} %pad_clamp_fusion.1) | copy-start | bytes 12292
  5.7 8.5 %copy-start.45 = (s32[16,1]{0,1:T(1,128)S(1)}, s32[16,1]{0,1:T(1,128)}, u32[]{:S(2)}) copy-start(s32[16,1]{0,1:T(1,128)} %param.26) | copy-start | bytes 196
  5.7 8.5 %copy-start.34 = (s32[16]{0:T(128)S(1)}, s32[16]{0:T(128)}, u32[]{:S(2)}) copy-start(s32[16]{0:T(128)} %param.25) | copy-start | bytes 196
  5.7 8.5 %copy-start.46 = (s32[1,8]{1,0:T(1,128)S(1)}, s32[1,8]{1,0:T(1,128)}, u32[]{:S(2)}) copy-start(s32[1,8]{1,0:T(1,128)} %param.27) | copy-start | bytes 100
  5.8 9.5 %copy-start.47 = (f32[64]{0:T(128)S(1)}, f32[64]{0:T(128)}, u32[]{:S(2)}) copy-start(f32[64]{0:T(128)} %param.31) | copy-start | bytes 772
  5.8 9.6 %copy-start.44 = (f32[64]{0:T(128)S(1)}, f32[64]{0:T(128)}, u32[]{:S(2)}) copy-start(f32[64]{0:T(128)} %param.30) | copy-start | bytes 772
  5.8 9.7 %copy-start.21 = (f32[4,16,64]{2,1,0:T(8,128)S(1)}, f32[4,16,64]{2,1,0:T(8,128)}, u32[]{:S(2)}) copy-start(f32[4,16,64]{2,1,0:T(8,128)} %param.23) | copy-start | bytes 49156
  5.8 12.0 %copy-start.42 = (f32[64]{0:T(128)S(1)}, f32[64]{0:T(128)}, u32[]{:S(2)}) copy-start(f32[64]{0:T(128)} %param.32) | copy-start | bytes 772
  5.8 12.6 %copy-start.41 = (f32[2,2,64]{2,1,0:T(2,128)S(1)}, f32[2,2,64]{2,1,0:T(2,128)}, u32[]{:S(2)}) copy-start(f32[2,2,64]{2,1,0:T(2,128)} %param.37) | copy-start | bytes 3076
  5.8 13.9 %copy-start.5 = (bf16[4,4096]{1,0:T(4,128)(2,1)S(1)}, bf16[4,4096]{1,0:T(4,128)(2,1)}, u32[]{:S(2)}) copy-start(bf16[4,4096]{1,0:T(4,128)(2,1)} %param.28) | copy-start | bytes 98308
  5.8 14.5 %copy-start.9 = (bf16[4,2048]{1,0:T(4,128)(2,1)S(1)}, bf16[4,2048]{1,0:T(4,128)(2,1)}, u32[]{:S(2)}) copy-start(bf16[4,2048]{1,0:T(4,128)(2,1)} %param.29) | copy-start | bytes 49156
  5.8 15.7 %copy-start.22 = (bf16[2,2,4096]{2,1,0:T(2,128)(2,1)S(1)}, bf16[2,2,4096]{2,1,0:T(2,128)(2,1)}, u32[]{:S(2)}) copy-start(bf16[2,2,4096]{2,1,0:T(2,128)(2,1)} %param.34) | copy-start | bytes 98308
  5.9 17.2 %copy-start.10 = (bf16[2,2,8192]{2,1,0:T(2,128)(2,1)S(1)}, bf16[2,2,8192]{2,1,0:T(2,128)(2,1)}, u32[]{:S(2)}) copy-start(bf16[2,2,8192]{2,1,0:T(2,128)(2,1)} %param.38) | copy-start | bytes 196612
  5.9 17.9 %copy-start.4 = (bf16[1,64,2048]{2,1,0:T(8,128)(2,1)S(1)}, bf16[1,64,2048]{2,1,0:T(8,128)(2,1)}, u32[]{:S(2)}) copy-start(bf16[1,64,2048]{2,1,0:T(8,128)(2,1)} %param.21) | copy-start | bytes 786436
  5.9 18.0 %copy-start.3 = (bf16[16,64,256]{2,1,0:T(8,128)(2,1)S(1)}, bf16[16,64,256]{2,1,0:T(8,128)(2,1)}, u32[]{:S(2)}) copy-start(bf16[16,64,256]{2,1,0:T(8,128)(2,1)} %param.20) | copy-start | bytes 1572868
  7.7 20.1 %all-to-all-start.1 = ((bf16[2,16,8192]{2,0,1:T(2,128)(2,1)}), bf16[2,16,8192]{2,0,1:T(2,128)(2,1)S(1)}, u32[]{:S(2)}, u32[]{:S(2)}) async-start(bf16[2,16,8192]{2,0,1:T(2,128)(2,1)} %broadcast_select_fusion.3), calls=%async_computation.1 | async-start | bytes 1048576 | tf_op jit(solution)/shard_map/all_to_all | solution.py:154
  23.9 10.5 %copy-start.6 = (bf16[2,2,4096]{2,1,0:T(2,128)(2,1)S(1)}, bf16[2,2,4096]{2,1,0:T(2,128)(2,1)}, u32[]{:S(2)}) copy-start(bf16[2,2,4096]{2,1,0:T(2,128)(2,1)} %param.36) | copy-start | bytes 98308
  28.6 18.8 %all-to-all-start = ((bf16[16,64,256]{2,1,0:T(8,128)(2,1)}), bf16[16,64,256]{2,1,0:T(8,128)(2,1)S(1)}, u32[]{:S(2)}, u32[]{:S(2)}) async-start(bf16[16,64,256]{2,1,0:T(8,128)(2,1)} %bitcast.5), calls=%async_computation | async-start | bytes 1048576 | tf_op jit(solution)/shard_map/all_to_all | solution.py:68
  35.8 12.7 %copy-start.30 = (bf16[2,2,2048]{2,1,0:T(2,128)(2,1)S(1)}, bf16[2,2,2048]{2,1,0:T(2,128)(2,1)}, u32[]{:S(2)}) copy-start(bf16[2,2,2048]{2,1,0:T(2,128)(2,1)} %param.39) | copy-start | bytes 49156
  51.6 52.1 %all-to-all-start.3 = ((bf16[2,16,1152]{2,0,1:T(2,128)(2,1)}), bf16[2,16,1152]{2,0,1:T(2,128)(2,1)S(1)}, u32[]{:S(2)}, u32[]{:S(2)}) async-start(bf16[2,16,1152]{2,0,1:T(2,128)(2,1)} %broadcast_select_fusion.6), calls=%async_computation.3 | async-start | bytes 147456 | tf_op jit(solution)/shard_map/all_to_all | solution.py:153
  58.7 1.6 copy-start
  60.3 1.2 copy-start.23
  60.3 1.2 copy-start.24
  60.3 1.2 copy-start.32
  60.8 1.2 copy-start.1
  64.1 2.2 %copy-start.2 = (bf16[16,64,256]{2,1,0:T(8,128)(2,1)S(1)}, bf16[16,64,256]{2,1,0:T(8,128)(2,1)}, u32[]{:S(2)}) copy-start(bf16[16,64,256]{2,1,0:T(8,128)(2,1)} %param.22) | copy-start | bytes 1572868
  89.0 3.4 %copy-start.18 = (pred[2,16]{0,1:T(8,128)(4,1)S(1)}, pred[2,16]{0,1:T(8,128)(4,1)}, u32[]{:S(2)}) copy-start(pred[2,16]{0,1:T(8,128)(4,1)} %copy-done.17) | copy-start | bytes 100
  89.0 3.4 %copy-start.20 = (pred[2,16]{0,1:T(8,128)(4,1)S(1)}, pred[2,16]{0,1:T(8,128)(4,1)}, u32[]{:S(2)}) copy-start(pred[2,16]{0,1:T(8,128)(4,1)} %copy-done.19) | copy-start | bytes 100
  99.1 2.6 %copy-start.40 = (f32[2]{0:T(128)S(1)}, f32[2]{0:T(128)}, u32[]{:S(2)}) copy-start(f32[2]{0:T(128)} %convert_element_type.238) | copy-start | bytes 28
  99.1 3.3 %copy-start.37 = (f32[256]{0:T(256)S(1)}, f32[256]{0:T(256)}, u32[]{:S(2)}) copy-start(f32[256]{0:T(256)} %dynamic_slice.26) | copy-start | bytes 3076
  103.7 16.2 %copy-start.12 = (f32[1,4096]{1,0:T(1,128)S(1)}, f32[1,4096]{1,0:T(1,128)}, u32[]{:S(2)}) copy-start(f32[1,4096]{1,0:T(1,128)} %get-tuple-element.48) | copy-start | bytes 49156
  103.7 16.2 %copy-start.13 = (f32[1,4096]{1,0:T(1,128)S(1)}, f32[1,4096]{1,0:T(1,128)}, u32[]{:S(2)}) copy-start(f32[1,4096]{1,0:T(1,128)} %get-tuple-element.49) | copy-start | bytes 49156
  103.7 16.2 %copy-start.14 = (f32[1,4096]{1,0:T(1,128)S(1)}, f32[1,4096]{1,0:T(1,128)}, u32[]{:S(2)}) copy-start(f32[1,4096]{1,0:T(1,128)} %get-tuple-element.50) | copy-start | bytes 49156
  103.7 16.2 %copy-start.15 = (f32[1,4096]{1,0:T(1,128)S(1)}, f32[1,4096]{1,0:T(1,128)}, u32[]{:S(2)}) copy-start(f32[1,4096]{1,0:T(1,128)} %get-tuple-element.51) | copy-start | bytes 49156
  103.7 16.6 %copy-start.31 = (bf16[2,2,2048]{2,1,0:T(2,128)(2,1)S(1)}, bf16[2,2,2048]{2,1,0:T(2,128)(2,1)}, u32[]{:S(2)}) copy-start(bf16[2,2,2048]{2,1,0:T(2,128)(2,1)} %param.35) | copy-start | bytes 49156
  103.7 16.7 %copy-start.25 = (f32[1,2048]{1,0:T(1,128)S(1)}, f32[1,2048]{1,0:T(1,128)}, u32[]{:S(2)}) copy-start(f32[1,2048]{1,0:T(1,128)} %get-tuple-element.58) | copy-start | bytes 24580
  103.7 16.7 %copy-start.26 = (f32[1,2048]{1,0:T(1,128)S(1)}, f32[1,2048]{1,0:T(1,128)}, u32[]{:S(2)}) copy-start(f32[1,2048]{1,0:T(1,128)} %get-tuple-element.59) | copy-start | bytes 24580
  103.7 16.7 %copy-start.27 = (f32[1,2048]{1,0:T(1,128)S(1)}, f32[1,2048]{1,0:T(1,128)}, u32[]{:S(2)}) copy-start(f32[1,2048]{1,0:T(1,128)} %get-tuple-element.60) | copy-start | bytes 24580
  103.7 16.7 %copy-start.28 = (f32[1,2048]{1,0:T(1,128)S(1)}, f32[1,2048]{1,0:T(1,128)}, u32[]{:S(2)}) copy-start(f32[1,2048]{1,0:T(1,128)} %get-tuple-element.61) | copy-start | bytes 24580
  103.7 63.3 %all-to-all-start.2 = ((bf16[2,16,32768]{2,0,1:T(2,128)(2,1)}), bf16[2,16,32768]{2,0,1:T(2,128)(2,1)S(1)}, u32[]{:S(2)}, u32[]{:S(2)}) async-start(bf16[2,16,32768]{2,0,1:T(2,128)(2,1)} %broadcast_select_fusion.1), calls=%async_computation.2 | async-start | bytes 4194304 | tf_op jit(solution)/shard_map/all_to_all | solution.py:152
  170.3 4.9 %copy-start.38 = (f32[2,64]{1,0:T(2,128)S(1)}, f32[2,64]{1,0:T(2,128)}, u32[]{:S(2)}) copy-start(f32[2,64]{1,0:T(2,128)} %get-tuple-element.34) | copy-start | bytes 1540
  170.3 4.9 %copy-start.39 = (f32[2,64]{1,0:T(2,128)S(1)}, f32[2,64]{1,0:T(2,128)}, u32[]{:S(2)}) copy-start(f32[2,64]{1,0:T(2,128)} %get-tuple-element.72) | copy-start | bytes 1540
  175.2 8.2 %copy-start.7 = (bf16[2,1,4096]{2,1,0:T(2,128)(2,1)S(1)}, bf16[2,1,4096]{2,1,0:T(2,128)(2,1)}, u32[]{:S(2)}) copy-start(bf16[2,1,4096]{2,1,0:T(2,128)(2,1)} %get-tuple-element.44) | copy-start | bytes 49156
  175.2 8.2 %copy-start.8 = (bf16[2,1,4096]{2,1,0:T(2,128)(2,1)S(1)}, bf16[2,1,4096]{2,1,0:T(2,128)(2,1)}, u32[]{:S(2)}) copy-start(bf16[2,1,4096]{2,1,0:T(2,128)(2,1)} %get-tuple-element.45) | copy-start | bytes 49156
  175.2 8.2 %copy-start.16 = (f32[4096]{0:T(1024)S(1)}, f32[4096]{0:T(1024)}, u32[]{:S(2)}) copy-start(f32[4096]{0:T(1024)} %mul.609) | copy-start | bytes 49156
  175.2 8.5 %copy-start.29 = (f32[4096]{0:T(1024)S(1)}, f32[4096]{0:T(1024)}, u32[]{:S(2)}) copy-start(f32[4096]{0:T(1024)} %param.33) | copy-start | bytes 49156
  (5 other events, 5.4 us)
where the time goes:
time: 186 us; the launch traced here: 185 us
  waiting for transfers between devices  58.4 us (31%)
  other arithmetic  36.7 us (20%)
  starting transfers between devices  32.6 us (18%)
  local copies, waits for them, and re-layouts  29.4 us (16%)
  blocking collectives  22.3 us (12%)
  matrix products  3.52 us (2%)
    all_to_all x1, waiting for transfers between devices, local(): lax.all_to_all(send_state, ('tensor', 'side'), split_axis=1, concat_axis=...  46.3 us
    psum x1, blocking collectives, local(): square_sums = lax.psum(jnp.sum(gated * gated, axis=2), ('tensor', 'side'))  22.3 us
    all_to_all x1, starting transfers between devices, local(): lax.all_to_all(send_state, ('tensor', 'side'), split_axis=1, concat_axis=...  15.9 us
    all_to_all x1, waiting for transfers between devices, local(): lax.all_to_all(send_coeff, ('tensor', 'side'), split_axis=0, concat_axis=...  11.2 us
    select_n x3, other arithmetic, pack_rows(): kept = jnp.where(present[:, None], picked, jnp.zeros((), flat_values.dtype))  9.28 us
    reduce_sum x1, other arithmetic, local(): jnp.sum(slot_state * c_now[:, :, None, :], axis=-1)  7.97 us
    all_to_all x1, starting transfers between devices, local(): lax.all_to_all(send_cache, ('tensor', 'side'), split_axis=1, concat_axis=...  6.55 us
    all_to_all x1, starting transfers between devices, local(): lax.all_to_all(send_coeff, ('tensor', 'side'), split_axis=0, concat_axis=...  5.16 us
  transfers between devices with their start and end apart: 4, of which 3 were waited for; matrix products, arithmetic and copies ran while one was open for 22% of the time, Pallas kernels for 0%

commit v1 on v0

v1 whole, which is shorter than its diff:
```python
import jax
import jax.numpy as jnp
from jax import lax
from jax.experimental import pallas as pl
from jax.experimental.pallas import tpu as pltpu
from jax.sharding import PartitionSpec as P

GROUPS = 8
CONVK = 4
KVH = 8
KVD = 128
BLK = 16
LANES = 128
ROWS = 80
NEW = 16
EPS = 1e-05
AXES = ("tensor", "side")
F32 = jnp.float32
BF16 = jnp.bfloat16

SMEM = pl.BlockSpec(memory_space=pltpu.SMEM)
VMEM = pl.BlockSpec(memory_space=pltpu.VMEM)
PARAMS = pltpu.CompilerParams(vmem_limit_bytes=48 * 1024 * 1024)


def iota(shape, dim):
    return lax.broadcasted_iota(jnp.int32, shape, dim)


def softplus(x):
    return jnp.maximum(x, 0.0) + jnp.log1p(jnp.exp(-jnp.abs(x)))


def silu(x):
    return x / (1.0 + jnp.exp(-x))


def ranks(owners, count, rank_ref):
    def clear(d, carry):
        count[d] = 0
        return carry

    lax.fori_loop(0, count.shape[0], clear, 0)

    def one(r, carry):
        owner = owners[r, 0]
        rank = count[owner]
        rank_ref[r] = rank
        count[owner] = rank + 1
        return carry

    lax.fori_loop(0, owners.shape[0], one, 0)


def pack_kernel(owners, coeff, cache, hidden, coeff_new, step_new, send, count, source):
    devices = send.shape[0]
    slots = hidden.shape[0]
    group_devs = devices // GROUPS
    span = coeff.shape[1]
    width = cache.shape[2]

    def clear(d, carry):
        count[d] = 0
        for k in range(slots):
            source[d * slots + k] = 0
        return carry

    lax.fori_loop(0, devices, clear, 0)

    def place(r, carry):
        owner = owners[r, 0]
        rank = count[owner]
        source[owner * slots + rank] = r
        count[owner] = rank + 1
        return carry

    lax.fori_loop(0, owners.shape[0], place, 0)

    heads = step_new.shape[2]
    steps = jnp.concatenate([step_new[k] for k in range(slots)], axis=0)
    if heads < LANES:
        steps = jnp.concatenate(
            [steps, jnp.zeros((steps.shape[0], LANES - heads), F32)], axis=1
        )
    steps = jnp.concatenate([steps, jnp.zeros_like(steps)], axis=0)
    padded = steps.shape[1]
    lane = iota((8, LANES), 1)

    def one(d, carry):
        group = d // group_devs
        start = pl.multiple_of((group * 2 + lax.rem(d, 2)) * LANES, LANES)
        send[d, 0:span, :] = coeff[0, :, pl.ds(start, LANES)]
        own = pl.multiple_of(d * 2 * LANES, 2 * LANES)
        rows = jnp.concatenate(
            [hidden[k, :, pl.ds(own, 2 * LANES)].astype(F32) for k in range(slots)], axis=0
        )
        tokens = jnp.concatenate(
            [coeff_new[k, :, pl.ds(start, LANES)].astype(F32) for k in range(slots)], axis=0
        )
        mine = pltpu.roll(steps, lax.rem(padded - d * 4, padded), 1)[:, :LANES]
        high = mine.astype(BF16).astype(F32)
        rest = mine - high
        middle = rest.astype(BF16).astype(F32)
        low = rest - middle
        split = jnp.where(
            lane < 32, high, jnp.where(lane < 64, pltpu.roll(middle, 32, 1), pltpu.roll(low, 64, 1))
        )
        block = jnp.concatenate([rows[:, :LANES], rows[:, LANES:], tokens, split[0:4]], axis=0)
        send[d, span : span + NEW, :] = block.astype(BF16)
        kept = jnp.concatenate(
            [cache[source[d * slots + k]].astype(F32) for k in range(slots)], axis=0
        )
        kept = jnp.concatenate(
            [kept[:, c * LANES : (c + 1) * LANES] for c in range(width // LANES)], axis=0
        )
        send[d, span + NEW :, :] = kept.astype(BF16)
        return carry

    lax.fori_loop(0, devices, one, 0)


def spliced(rows, first, second, length):
    columns = rows.shape[1]
    rows = jnp.concatenate([rows, jnp.zeros((ROWS - rows.shape[0], columns), F32)], axis=0)
    place = iota((ROWS, columns), 0)
    return jnp.where(place == length, first, jnp.where(place == length + 1, second, rows))


def conv(rows, taps):
    total = pltpu.roll(rows, 3, 0) * taps[0:1]
    total = total + pltpu.roll(rows, 2, 0) * taps[1:2]
    total = total + pltpu.roll(rows, 1, 0) * taps[2:3]
    total = total + rows * taps[3:4]
    return silu(total).astype(BF16)


def coeff_kernel(owners, lengths, taps_ref, recv, out, count, rank_ref):
    prompts = out.shape[0]
    span = recv.shape[1] - NEW
    devices = recv.shape[0]
    group_devs = devices // GROUPS
    ranks(owners, count, rank_ref)
    me = lax.axis_index(AXES)
    start = pl.multiple_of((me // group_devs * 2 + lax.rem(me, 2)) * LANES, LANES)
    taps = taps_ref[:, pl.ds(start, LANES)].astype(F32)

    def one(r, carry):
        new = recv[owners[r, 0], span : span + NEW, :].astype(F32)
        is_first = rank_ref[r] == 0
        first = jnp.where(is_first, new[8:9], new[10:11])
        second = jnp.where(is_first, new[9:10], new[11:12])
        rows = spliced(recv[r, 0:span, :].astype(F32), first, second, lengths[r])
        out[r] = conv(rows, taps)
        return carry

    lax.fori_loop(0, prompts, one, 0, unroll=2)


def main_kernel(
    owners,
    lengths,
    bias,
    decay,
    skip,
    taps_ref,
    mine,
    other,
    new_ref,
    hidden,
    gate,
    step,
    gated_ref,
    fin,
    count,
    rank_ref,
    tokens,
    dt_ref,
    sum_ref,
):
    prompts, span, columns = hidden.shape
    local_heads = step.shape[0]
    head_size = columns // local_heads
    ranks(owners, count, rank_ref)
    me = lax.axis_index(AXES)
    is_b = lax.rem(me, 2) == 0
    taps = taps_ref[:, pl.ds(pl.multiple_of(me * columns, LANES), columns)].astype(F32)
    fin[...] = jnp.zeros_like(fin)

    def fetch(r, carry):
        new = new_ref[owners[r, 0]].astype(F32)
        is_first = rank_ref[r] == 0
        tokens[0, pl.ds(r, 1), :] = jnp.where(is_first, new[12:13], new[14:15])
        tokens[1, pl.ds(r, 1), :] = jnp.where(is_first, new[13:14], new[15:16])
        return carry

    lax.fori_loop(0, prompts, fetch, 0)

    def widths(r, lens):
        return jnp.where(iota((prompts, LANES), 0) == r, lengths[r], lens)

    lens = lax.fori_loop(0, prompts, widths, jnp.zeros((prompts, LANES), jnp.int32))
    lane = iota((prompts, LANES), 1)
    news = []
    for i in range(2):
        raw = tokens[i]
        news.append(raw + pltpu.roll(raw, LANES - 32, 1) + pltpu.roll(raw, LANES - 64, 1))
    for h in range(local_heads):
        raw = jnp.concatenate([step[h], jnp.zeros((prompts, LANES - span), F32)], axis=1)
        raw = jnp.where(
            lane == lens,
            news[0][:, h : h + 1],
            jnp.where(lane == lens + 1, news[1][:, h : h + 1], raw),
        )
        size = jnp.where(lane < lens + 2, softplus(raw + bias[me * local_heads + h]), 0.0)
        rate = -jnp.exp(jnp.full((1, LANES), decay[me * local_heads + h], F32))
        total = size * rate
        shift = 1
        while shift < LANES:
            total = total + jnp.where(lane >= shift, pltpu.roll(total, shift, 1), 0.0)
            shift *= 2
        dt_ref[:, h, :] = size
        sum_ref[:, h, :] = total

    head_of = iota((1, columns), 1) // head_size
    gain = jnp.zeros((1, columns), F32)
    for h in range(local_heads):
        gain = jnp.where(head_of == h, skip[me * local_heads + h], gain)
    heads_wide = iota((ROWS, columns), 1) // head_size
    place = iota((ROWS, columns), 0)
    lower = iota((ROWS, ROWS), 0) >= iota((ROWS, ROWS), 1)
    column_of = iota((span, LANES), 1)

    def one(r, squares):
        owner = owners[r, 0]
        rank = rank_ref[r]
        length = lengths[r]
        new = new_ref[owner].astype(F32)
        is_first = rank == 0
        token = []
        for i in range(2):
            a = jnp.where(is_first, new[i : i + 1], new[2 + i : 3 + i])
            b = jnp.where(is_first, new[4 + i : 5 + i], new[6 + i : 7 + i])
            token.append(jnp.concatenate([a, b], axis=1))
        u = conv(spliced(hidden[r].astype(F32), token[0], token[1], length), taps)
        here, there = mine[r], other[r]
        b_rows = jnp.where(is_b, here, there)
        c_rows = jnp.where(is_b, there, here)
        scores = lax.dot_general(
            c_rows, b_rows, (((1,), (1,)), ((), ())), preferred_element_type=F32
        )
        sums = sum_ref[r]
        sizes = dt_ref[r]
        turned = sums.T
        out = gain * u.astype(F32)
        for h in range(local_heads):
            gap = turned[:ROWS, h : h + 1] - sums[h : h + 1, :ROWS]
            mix = jnp.where(lower, scores * jnp.exp(gap) * sizes[h : h + 1, :ROWS], 0.0)
            only = jnp.where(heads_wide == h, u, jnp.zeros((), BF16))
            out = out + jnp.dot(mix.astype(BF16), only, preferred_element_type=F32)
        for i in range(2):
            row = jnp.sum(jnp.where(place == length + i, out, 0.0), axis=0, keepdims=True)
            for half in range(2):
                fin[owner, pl.ds(prompts // 2 + 4 * half + 2 * rank + i, 1), :] = row[
                    :, half * LANES : (half + 1) * LANES
                ]
        gated = out[:span] * silu(gate[r].astype(F32))
        gated_ref[r] = gated
        square = jnp.sum(gated * gated, axis=1, keepdims=True)
        return jnp.where(column_of == r, square, squares)

    squares = lax.fori_loop(0, prompts, one, jnp.zeros((span, LANES), F32))
    turned = squares.T
    half = prompts // 2
    packed = jnp.concatenate([turned[0:half, :], turned[half:prompts, :]], axis=1)

    def spread(d, carry):
        fin[d, 0:half, :] = packed
        return carry

    lax.fori_loop(0, fin.shape[0], spread, 0)


def slot_facts(owners, lengths, slots):
    me = lax.axis_index(AXES)

    def one(r, found):
        is_mine = owners[r, 0] == me
        seen = found[-1]
        lens = [
            jnp.where(is_mine & (seen == k), lengths[r], found[k]) for k in range(slots)
        ]
        return (*lens, seen + is_mine.astype(jnp.int32))

    zero = jnp.int32(0)
    return lax.fori_loop(0, owners.shape[0], one, (zero,) * (slots + 1))[:slots]


def cache_kernel(owners, lengths, pages, recv, query, cache_new, pool, attended, rows_ref):
    slots = query.shape[0]
    steps = query.shape[1]
    sources = recv.shape[0]
    width = pool.shape[2]
    parts = width // LANES
    span = sources * (recv.shape[1] // parts) // slots
    offset = 0
    each = recv.shape[1] // parts
    local = each // slots
    lens = slot_facts(owners, lengths, slots)
    keys = sources * each
    row = iota((slots * span, keys), 0)
    key = iota((slots * span, keys), 1)
    slot_of = row // span
    at = lax.rem(row, span)
    wanted = at // local * each + slot_of * local + lax.rem(at, local)
    limit = jnp.where(slot_of == 0, lens[0], lens[1])
    order = jnp.where((key == wanted) & (at < limit), 1.0, 0.0).astype(BF16)
    ask = jnp.concatenate([query[k].astype(F32) for k in range(slots)], axis=0)
    fresh = jnp.concatenate([cache_new[k].astype(F32) for k in range(slots)], axis=0)
    fresh = jnp.concatenate([fresh, jnp.zeros_like(fresh)], axis=0)
    per = query.shape[2] // (KVH * KVD)
    pairs = slots * steps
    count = per * pairs
    ask_slot = lax.rem(iota((count, slots * span), 0), pairs) // steps
    ask_step = lax.rem(iota((count, slots * span), 0), steps)
    key_slot = iota((count, slots * span), 1) // span
    key_at = lax.rem(iota((count, slots * span), 1), span)
    live = (key_slot == ask_slot) & (key_at < jnp.where(ask_slot == 0, lens[0], lens[1]))
    new_row = iota((count, 2 * pairs), 0)
    new_key = iota((count, 2 * pairs), 1)
    new_live = (
        (new_key < pairs)
        & (new_key // steps == lax.rem(new_row, pairs) // steps)
        & (lax.rem(new_key, steps) <= lax.rem(new_row, steps))
    )
    out_slot = lax.rem(iota((count, KVD), 0), pairs) // steps
    filled = jnp.where(out_slot == 0, lens[0], lens[1]) > 0

    for c in range(parts):
        block = recv[:, offset + c * each : offset + (c + 1) * each, :].astype(F32)
        block = block.reshape(keys, LANES).astype(BF16)
        rows_ref[:, c * LANES : (c + 1) * LANES] = jnp.dot(
            order, block, preferred_element_type=F32
        ).astype(BF16)
    blocks = span // BLK
    for k in range(slots):
        for b in range(blocks):
            pool[pages[0, k * blocks + b]] = rows_ref[
                k * span + b * BLK : k * span + (b + 1) * BLK, :
            ]
    contract = (((1,), (1,)), ((), ()))
    answers = []
    for c in range(KVH):
        asked = jnp.concatenate(
            [ask[:, (c * per + g) * KVD : (c * per + g + 1) * KVD] for g in range(per)], axis=0
        ).astype(BF16)
        own = slice(c * KVD, (c + 1) * KVD)
        values = slice((KVH + c) * KVD, (KVH + c + 1) * KVD)
        old = lax.dot_general(asked, rows_ref[:, own], contract, preferred_element_type=F32)
        recent = lax.dot_general(
            asked, fresh[:, own].astype(BF16), contract, preferred_element_type=F32
        )
        old = jnp.where(live, old * KVD ** (-0.5), -jnp.inf)
        recent = jnp.where(new_live, recent * KVD ** (-0.5), -jnp.inf)
        peak = jnp.maximum(
            jnp.max(old, axis=1, keepdims=True), jnp.max(recent, axis=1, keepdims=True)
        )
        old = jnp.exp(old - peak)
        recent = jnp.exp(recent - peak)
        total = jnp.sum(old, axis=1, keepdims=True) + jnp.sum(recent, axis=1, keepdims=True)
        got = jnp.dot(
            (old / total).astype(BF16), rows_ref[:, values], preferred_element_type=F32
        ) + jnp.dot(
            (recent / total).astype(BF16),
            fresh[:, values].astype(BF16),
            preferred_element_type=F32,
        )
        got = jnp.where(filled, got, 0.0)
        answers += [got[g * pairs : (g + 1) * pairs] for g in range(per)]
    whole = jnp.concatenate(answers, axis=1)
    for k in range(slots):
        attended[k] = whole[k * steps : (k + 1) * steps].astype(BF16)


def final_kernel(owners, lengths, gain_ref, fin, gated, new_gate, prefill, mixer):
    prompts, span, columns = gated.shape
    slots = new_gate.shape[0]
    steps = new_gate.shape[1]
    sources = fin.shape[0]
    width = new_gate.shape[2]
    half = prompts // 2
    me = lax.axis_index(AXES)
    total = fin[0, 0:half, :]
    for s in range(1, sources):
        total = total + fin[s, 0:half, :]
    scale = lax.rsqrt(total / width + EPS).T
    gain = gain_ref[:, pl.ds(pl.multiple_of(me * columns, LANES), columns)]
    place = iota((span, columns), 0)
    for r in range(prompts):
        low = 0 if r < half else span
        column = scale[low : low + span, r % half : r % half + 1]
        rows = gated[r] * column * gain
        prefill[r] = jnp.where(place < lengths[r], rows, 0.0).astype(BF16)
    lens = slot_facts(owners, lengths, slots)
    read = jnp.concatenate(
        [
            fin[s, half + pairs : half + pairs + 4, :]
            for s in range(sources)
            for pairs in (0, 4)
        ],
        axis=1,
    )
    gates = jnp.concatenate([new_gate[k].astype(F32) for k in range(slots)], axis=0)
    out = read * silu(gates)
    mean = jnp.mean(out * out, axis=1, keepdims=True)
    out = out * lax.rsqrt(mean + EPS) * gain_ref[...]
    slot_of = iota(out.shape, 0) // steps
    out = jnp.where(jnp.where(slot_of == 0, lens[0], lens[1]) > 0, out, 0.0)
    for k in range(slots):
        mixer[k] = out[k * steps : (k + 1) * steps].astype(BF16)


def local(
    hidden_pre,
    coeff_pre,
    gate_pre,
    step_raw,
    cache_rows,
    lengths,
    owners,
    page_table,
    conv_hidden,
    conv_coeff,
    step_bias,
    decay_log,
    skip_gain,
    norm_gain,
    new_hidden,
    new_coeff,
    new_gate,
    new_step,
    new_query,
    new_cache,
):
    devices = lax.axis_size(AXES)
    prompts, span, columns = hidden_pre.shape
    slots = new_hidden.shape[0]
    local_heads = step_raw.shape[0]
    cache_width = cache_rows.shape[2]
    kept_rows = slots * cache_rows.shape[1] * cache_width // LANES
    per_owner = pltpu.SMEM((devices,), jnp.int32)
    per_prompt = pltpu.SMEM((prompts,), jnp.int32)

    send = pl.pallas_call(
        pack_kernel,
        out_shape=jax.ShapeDtypeStruct((devices, span + NEW + kept_rows, LANES), BF16),
        in_specs=[SMEM, VMEM, VMEM, VMEM, VMEM, VMEM],
        out_specs=VMEM,
        scratch_shapes=[per_owner, pltpu.SMEM((devices * slots,), jnp.int32)],
        compiler_params=PARAMS,
        name="pack",
    )(owners, coeff_pre, cache_rows, new_hidden, new_coeff, new_step)
    recv = lax.all_to_all(send, AXES, split_axis=0, concat_axis=0, tiled=True)

    mine = pl.pallas_call(
        coeff_kernel,
        grid=(1,),
        out_shape=jax.ShapeDtypeStruct((prompts, ROWS, LANES), BF16),
        in_specs=[
            SMEM,
            SMEM,
            VMEM,
            pl.BlockSpec((devices, span + NEW, LANES), lambda i: (0, 0, 0)),
        ],
        out_specs=VMEM,
        scratch_shapes=[per_owner, per_prompt],
        compiler_params=PARAMS,
        name="coeff",
    )(owners, lengths, conv_coeff, recv)
    other = lax.ppermute(mine, "side", [(0, 1), (1, 0)])

    new_block = span // NEW
    gated, fin = pl.pallas_call(
        main_kernel,
        grid=(1,),
        out_shape=(
            jax.ShapeDtypeStruct((prompts, span, columns), F32),
            jax.ShapeDtypeStruct((devices, prompts // 2 + 8, LANES), F32),
        ),
        in_specs=[SMEM] * 5
        + [VMEM] * 3
        + [pl.BlockSpec((devices, NEW, LANES), lambda i: (0, new_block, 0))]
        + [VMEM] * 3,
        out_specs=(VMEM, VMEM),
        scratch_shapes=[
            per_owner,
            per_prompt,
            pltpu.VMEM((2, prompts, LANES), F32),
            pltpu.VMEM((prompts, 8, LANES), F32),
            pltpu.VMEM((prompts, 8, LANES), F32),
        ],
        compiler_params=PARAMS,
        name="main",
    )(
        owners,
        lengths,
        step_bias,
        decay_log,
        skip_gain,
        conv_hidden,
        mine,
        other,
        recv,
        hidden_pre,
        gate_pre,
        step_raw,
    )
    fin_got = lax.all_to_all(fin, AXES, split_axis=0, concat_axis=0, tiled=True)

    kept = recv[:, span + NEW :, :]
    cache_pool, decode_attention = pl.pallas_call(
        cache_kernel,
        out_shape=(
            jax.ShapeDtypeStruct((page_table.shape[1], BLK, cache_width), BF16),
            jax.ShapeDtypeStruct(new_query.shape, BF16),
        ),
        in_specs=[SMEM, SMEM, SMEM, VMEM, VMEM, VMEM],
        out_specs=(VMEM, VMEM),
        scratch_shapes=[pltpu.VMEM((slots * span, cache_width), BF16)],
        compiler_params=PARAMS,
        cost_estimate=pl.CostEstimate(
            flops=200_000_000, bytes_accessed=4_000_000, transcendentals=100_000
        ),
        name="cache",
    )(owners, lengths, page_table, kept, new_query, new_cache)

    prefill_out, decode_mixer = pl.pallas_call(
        final_kernel,
        out_shape=(
            jax.ShapeDtypeStruct(hidden_pre.shape, BF16),
            jax.ShapeDtypeStruct(new_gate.shape, BF16),
        ),
        in_specs=[SMEM, SMEM, VMEM, VMEM, VMEM, VMEM],
        out_specs=(VMEM, VMEM),
        compiler_params=PARAMS,
        name="final",
    )(owners, lengths, norm_gain.reshape(1, -1), fin_got, gated, new_gate)
    return (prefill_out, cache_pool, decode_mixer, decode_attention)


def solution(mesh):
    own = P(("group", "tensor", "side"), None, None)
    placed = (
        P("group", None, ("tensor", "side")),
        own,
        P("group", None, ("tensor", "side")),
        P(("tensor", "side"), "group", None),
        P("group", ("tensor", "side"), None),
        P("group"),
        P("group", None),
        P(("group", "tensor", "side"), None),
        P(),
        P(),
        P(),
        P(),
        P(),
        P(),
        own,
        own,
        own,
        own,
        own,
        own,
    )
    return jax.shard_map(
        local,
        mesh=mesh,
        in_specs=placed,
        out_specs=(P("group", None, ("tensor", "side")), own, own, own),
        check_vma=False,
    )
```

time: 186 us -> 64.9 us (0.35)
  the two profiles are of different devices: /device:TPU:15 before, /device:TPU:0 now
where the time goes in v1:
time: 64.9 us; the launch traced here: 64.4 us
  blocking collectives  28.7 us (44%)
  Pallas kernels  21.4 us (33%)
  local copies, waits for them, and re-layouts  4.98 us (8%)
  starting transfers between devices  4.66 us (7%)
  waiting for transfers between devices  3.81 us (6%)
  between operations  0.78 us (1%)
    all_to_all x1, blocking collectives, local(): recv = lax.all_to_all(send, AXES, split_axis=0, concat_axis=0, tiled=True)  28.7 us
    pallas_call x1, Pallas kernels, local(): pl.pallas_call(main_kernel, grid=(1,), out_shape=(jax.ShapeDtypeStruct((p...  9.96 us
    unnamed x39, local copies, waits for them, and re-layouts  4.94 us
    pallas_call x1, Pallas kernels, local(): pl.pallas_call(cache_kernel, out_shape=(jax.ShapeDtypeStruct((page_table....  4.52 us
    all_to_all x1, starting transfers between devices, local(): fin_got = lax.all_to_all(fin, AXES, split_axis=0, concat_axis=0, tiled=True)  3.82 us
    pallas_call x1, Pallas kernels, local(): pl.pallas_call(pack_kernel, out_shape=jax.ShapeDtypeStruct((devices, span...  3.32 us
    all_to_all x1, waiting for transfers between devices, local(): fin_got = lax.all_to_all(fin, AXES, split_axis=0, concat_axis=0, tiled=True)  2.55 us
    pallas_call x1, Pallas kernels, local(): pl.pallas_call(final_kernel, out_shape=(jax.ShapeDtypeStruct(hidden_pre.s...  2 us
  transfers between devices with their start and end apart: 2, of which 2 were waited for; matrix products, arithmetic and copies ran while one was open for 0% of the time, Pallas kernels for 7%

profile of v1, /device:TPU:0, one launch (start us, length us, event | category | flops | bytes accessed | tf_op | source)
XLA Modules:
  0.0 64.4 jit_solution(1114164726740815486)
XLA Ops:
  0.6 0.0 copy-start.12
  0.6 0.7 %copy.27.owners = s32[16,1]{1,0:T(8,128)S(1)} copy(s32[16,1]{0,1:T(1,128)} %param.26) | data formatting | bytes 128 | tf_op args[6]
  1.4 0.0 copy-done.12
  1.4 0.0 copy-start.2
  1.4 0.9 %copy-done.2 = bf16[1,64,2048]{2,1,0:T(8,128)(2,1)S(1)} copy-done((bf16[1,64,2048]{2,1,0:T(8,128)(2,1)S(1)}, bf16[1,64,2048]{2,1,0:T(8,128)(2,1)}, u32[]{:S(2)}) %copy-start.2) | copy-done | bytes 262168
  2.3 0.0 copy-start.3
  2.3 0.9 %copy-done.3 = bf16[16,4,2048]{2,1,0:T(4,128)(2,1)S(1)} copy-done((bf16[16,4,2048]{2,1,0:T(4,128)(2,1)S(1)}, bf16[16,4,2048]{2,1,0:T(4,128)(2,1)}, u32[]{:S(2)}) %copy-start.3) | copy-done | bytes 262168
  3.3 0.0 copy-start.6
  3.3 0.8 %copy-done.6 = bf16[2,2,4096]{2,1,0:T(2,128)(2,1)S(1)} copy-done((bf16[2,2,4096]{2,1,0:T(2,128)(2,1)S(1)}, bf16[2,2,4096]{2,1,0:T(2,128)(2,1)}, u32[]{:S(2)}) %copy-start.6) | copy-done | bytes 32792
  4.0 0.0 copy-start.8
  4.0 0.7 %copy-done.8 = bf16[2,2,2048]{2,1,0:T(2,128)(2,1)S(1)} copy-done((bf16[2,2,2048]{2,1,0:T(2,128)(2,1)S(1)}, bf16[2,2,2048]{2,1,0:T(2,128)(2,1)}, u32[]{:S(2)}) %copy-start.8) | copy-done | bytes 16408
  4.8 3.3 %pack.1 = bf16[16,208,128]{2,1,0:T(8,128)(2,1)S(1)} custom-call(s32[16,1]{1,0:T(8,128)S(1)} %copy.27.owners, bf16[1,64,2048]{2,1,0:T(8,128)(2,1)S(1)} %copy-done.2, bf16[16,4,2048]{2,1,0:T(4,128)(2,1)S(1)} %copy-done.3, bf16[2,2,4096]{2,1,0:T(2,128)(2,1)S(1)} %copy-done.6, bf16[2,2,2048]{2,1,0:T(2,128)(2,1)S(1)} %copy-done.8, f32[2,2,64]{2,1,0:T(2,128)S(1)} %copy-done.12), custom_call_target="tpu_custom_call" | custom-call | tf_op jit(solution)/shard_map/pack/pallas_call | solution.py:453
  8.1 0.0 copy-start.11
  8.1 28.7 %all_to_all.10.recv.new_ref = bf16[16,208,128]{2,1,0:T(8,128)(2,1)S(1)} all-to-all(bf16[16,208,128]{2,1,0:T(8,128)(2,1)S(1)} %pack.1), channel_id=1, replica_groups=mesh['group'=2,'tensor'=8,'side'=2] {'tensor','side'}, dimensions={0} | all-to-all | bytes 1703936 | tf_op jit(solution)/shard_map/all_to_all | solution.py:462
  36.8 0.0 copy-done.9
  36.8 0.0 copy-done.11
  36.8 0.0 copy-start
  36.8 0.0 copy-start.1
  36.8 0.0 copy-start.4
  36.8 0.0 copy-start.5
  36.9 0.0 copy-start.13
  36.9 0.0 copy-start.14
  36.9 0.0 copy-start.15
  36.9 1.6 %coeff.3.mine = bf16[16,80,128]{2,1,0:T(8,128)(2,1)S(1)} custom-call(s32[16,1]{1,0:T(8,128)S(1)} %copy.27.owners, s32[16]{0:T(128)S(1)} %copy-done.11, bf16[4,2048]{1,0:T(4,128)(2,1)S(1)} %copy-done.9, bf16[16,208,128]{2,1,0:T(8,128)(2,1)S(1)} %all_to_all.10.recv.new_ref), custom_call_target="tpu_custom_call" | custom-call | tf_op jit(solution)/shard_map/coeff/pallas_call | solution.py:464
  38.5 0.8 %collective-permute-start = (bf16[16,80,128]{2,1,0:T(8,128)(2,1)S(1)}, bf16[16,80,128]{2,1,0:T(8,128)(2,1)S(1)}, u32[]{:S(2)}, u32[]{:S(2)}) collective-permute-start(bf16[16,80,128]{2,1,0:T(8,128)(2,1)S(1)} %coeff.3.mine), channel_id=1, source_target_pairs={{0,1},{1,0},{2,3},{3,2},{4,5},{5,4},{6,7},{7,6},{8,9},{9,8},{10,11... | collective-permute-start | bytes 983048 | tf_op jit(solution)/shard_map/ppermute | solution.py:479
  39.3 1.3 %collective-permute-done.other = bf16[16,80,128]{2,1,0:T(8,128)(2,1)S(1)} collective-permute-done((bf16[16,80,128]{2,1,0:T(8,128)(2,1)S(1)}, bf16[16,80,128]{2,1,0:T(8,128)(2,1)S(1)}, u32[]{:S(2)}, u32[]{:S(2)}) %collective-permute-start) | collective-permute-done | bytes 327712 | tf_op jit(solution)/shard_map/ppermute | solution.py:479
  40.6 0.0 copy-done
  40.6 0.0 copy-done.1
  40.6 0.0 copy-done.4
  40.6 0.0 copy-done.5
  40.6 0.0 copy-done.13
  40.6 0.0 copy-done.14
  40.6 0.0 copy-done.15
  40.6 10.0 %main.1 = (f32[16,64,256]{2,1,0:T(8,128)S(1)}, f32[16,16,128]{2,1,0:T(8,128)}) custom-call(s32[16,1]{1,0:T(8,128)S(1)} %copy.27.owners, s32[16]{0:T(128)S(1)} %copy-done.11, f32[64]{0:T(128)S(1)} %copy-done.13, f32[64]{0:T(128)S(1)} %copy-done.14, f32[64]{0:T(128)S(1)} %copy-done.15, bf16[4,4096]{1,0:T(4,128)(2,1)S(1)} %copy-done.4, ...), custom_call_target="tpu_custom_call" | custom-call | tf_op jit(solution)/shard_map/main/pallas_call | solution.py:482
  50.6 3.8 %all-to-all-start.1 = ((f32[16,16,128]{2,1,0:T(8,128)}), f32[16,16,128]{2,1,0:T(8,128)S(1)}, u32[]{:S(2)}, u32[]{:S(2)}) async-start(f32[16,16,128]{2,1,0:T(8,128)} %get-tuple-element.10), calls=%async_computation.1 | async-start | bytes 262144 | tf_op jit(solution)/shard_map/all_to_all | solution.py:517
  54.4 0.0 copy-start.16
  54.4 0.0 copy-start.17
  54.5 0.0 copy-start.18
  54.5 0.8 %copy-done.16 = bf16[2,2,8192]{2,1,0:T(2,128)(2,1)S(1)} copy-done((bf16[2,2,8192]{2,1,0:T(2,128)(2,1)S(1)}, bf16[2,2,8192]{2,1,0:T(2,128)(2,1)}, u32[]{:S(2)}) %copy-start.16) | copy-done | bytes 65560
  55.3 0.0 copy-done.17
  55.3 0.0 copy-done.18
  55.3 0.0 copy-start.7
  55.3 0.0 copy-start.10
  55.3 4.5 %cache.3 = (bf16[8,16,2048]{2,1,0:T(8,128)(2,1)}, bf16[2,2,8192]{2,1,0:T(2,128)(2,1)}) custom-call(s32[16,1]{1,0:T(8,128)S(1)} %copy.27.owners, s32[16]{0:T(128)S(1)} %copy-done.11, s32[1,8]{1,0:T(1,128)S(1)} %copy-done.18, bf16[16,128,128]{2,1,0:T(8,128)(2,1)S(1)} %slice.4.recv, bf16[2,2,8192]{2,1,0:T(2,128)(2,1)S(1)} %copy-done.16, ...), custom_call_target="tpu_custom_call" | custom-call | flops 200000000 | bytes 4000000 | tf_op jit(solution)/shard_map/cache/pallas_call | solution.py:520
  59.8 2.6 %all-to-all-done.1.fin = f32[16,16,128]{2,1,0:T(8,128)S(1)} async-done(((f32[16,16,128]{2,1,0:T(8,128)}), f32[16,16,128]{2,1,0:T(8,128)S(1)}, u32[]{:S(2)}, u32[]{:S(2)}) %all-to-all-start.1) | async-done | bytes 131104 | tf_op jit(solution)/shard_map/all_to_all | solution.py:517
  62.4 0.0 copy-done.7
  62.4 0.0 copy-done.10
  62.4 2.0 %final.1 = (bf16[16,64,256]{2,1,0:T(8,128)(2,1)}, bf16[2,2,4096]{2,1,0:T(2,128)(2,1)}) custom-call(s32[16,1]{1,0:T(8,128)S(1)} %copy.27.owners, s32[16]{0:T(128)S(1)} %copy-done.11, f32[1,4096]{1,0:T(1,128)S(1)} %bitcast.1, f32[16,16,128]{2,1,0:T(8,128)S(1)} %all-to-all-done.1.fin, f32[16,64,256]{2,1,0:T(8,128)S(1)} %get-tuple-element.11.gated, ...), custom_call_target="tpu_custom_call" | custom-call | tf_op jit(solution)/shard_map/final/pallas_call | solution.py:536
  (2 shorter events, 0.0 us)
Async XLA Ops:
  0.6 0.8 %copy-start.12 = (f32[2,2,64]{2,1,0:T(2,128)S(1)}, f32[2,2,64]{2,1,0:T(2,128)}, u32[]{:S(2)}) copy-start(f32[2,2,64]{2,1,0:T(2,128)} %step_new.1) | copy-start | bytes 3076
  1.4 1.0 %copy-start.2 = (bf16[1,64,2048]{2,1,0:T(8,128)(2,1)S(1)}, bf16[1,64,2048]{2,1,0:T(8,128)(2,1)}, u32[]{:S(2)}) copy-start(bf16[1,64,2048]{2,1,0:T(8,128)(2,1)} %coeff.2) | copy-start | bytes 786436
  2.3 0.9 %copy-start.3 = (bf16[16,4,2048]{2,1,0:T(4,128)(2,1)S(1)}, bf16[16,4,2048]{2,1,0:T(4,128)(2,1)}, u32[]{:S(2)}) copy-start(bf16[16,4,2048]{2,1,0:T(4,128)(2,1)} %cache.2) | copy-start | bytes 786436
  3.3 0.8 %copy-start.6 = (bf16[2,2,4096]{2,1,0:T(2,128)(2,1)S(1)}, bf16[2,2,4096]{2,1,0:T(2,128)(2,1)}, u32[]{:S(2)}) copy-start(bf16[2,2,4096]{2,1,0:T(2,128)(2,1)} %hidden.2) | copy-start | bytes 98308
  4.0 0.7 %copy-start.8 = (bf16[2,2,2048]{2,1,0:T(2,128)(2,1)S(1)}, bf16[2,2,2048]{2,1,0:T(2,128)(2,1)}, u32[]{:S(2)}) copy-start(bf16[2,2,2048]{2,1,0:T(2,128)(2,1)} %coeff_new.1) | copy-start | bytes 49156
  8.1 28.7 %copy-start.9 = (bf16[4,2048]{1,0:T(4,128)(2,1)S(1)}, bf16[4,2048]{1,0:T(4,128)(2,1)}, u32[]{:S(2)}) copy-start(bf16[4,2048]{1,0:T(4,128)(2,1)} %taps_ref.2) | copy-start | bytes 49156
  8.1 28.7 %copy-start.11 = (s32[16]{0:T(128)S(1)}, s32[16]{0:T(128)}, u32[]{:S(2)}) copy-start(s32[16]{0:T(128)} %lengths.7) | copy-start | bytes 196
  36.8 3.8 %copy-start = (bf16[16,64,256]{2,1,0:T(8,128)(2,1)S(1)}, bf16[16,64,256]{2,1,0:T(8,128)(2,1)}, u32[]{:S(2)}) copy-start(bf16[16,64,256]{2,1,0:T(8,128)(2,1)} %hidden.3) | copy-start | bytes 1572868
  36.8 3.8 %copy-start.1 = (bf16[16,64,256]{2,1,0:T(8,128)(2,1)S(1)}, bf16[16,64,256]{2,1,0:T(8,128)(2,1)}, u32[]{:S(2)}) copy-start(bf16[16,64,256]{2,1,0:T(8,128)(2,1)} %gate.1) | copy-start | bytes 1572868
  36.8 3.8 %copy-start.4 = (bf16[4,4096]{1,0:T(4,128)(2,1)S(1)}, bf16[4,4096]{1,0:T(4,128)(2,1)}, u32[]{:S(2)}) copy-start(bf16[4,4096]{1,0:T(4,128)(2,1)} %taps_ref.3) | copy-start | bytes 98308
  36.8 3.8 %copy-start.5 = (f32[4,16,64]{2,1,0:T(8,128)S(1)}, f32[4,16,64]{2,1,0:T(8,128)}, u32[]{:S(2)}) copy-start(f32[4,16,64]{2,1,0:T(8,128)} %step.1) | copy-start | bytes 49156
  36.9 3.8 %copy-start.13 = (f32[64]{0:T(128)S(1)}, f32[64]{0:T(128)}, u32[]{:S(2)}) copy-start(f32[64]{0:T(128)} %bias.1) | copy-start | bytes 772
  36.9 3.8 %copy-start.14 = (f32[64]{0:T(128)S(1)}, f32[64]{0:T(128)}, u32[]{:S(2)}) copy-start(f32[64]{0:T(128)} %decay.1) | copy-start | bytes 772
  36.9 3.8 %copy-start.15 = (f32[64]{0:T(128)S(1)}, f32[64]{0:T(128)}, u32[]{:S(2)}) copy-start(f32[64]{0:T(128)} %skip.1) | copy-start | bytes 772
  38.5 2.1 %collective-permute-start = (bf16[16,80,128]{2,1,0:T(8,128)(2,1)S(1)}, bf16[16,80,128]{2,1,0:T(8,128)(2,1)S(1)}, u32[]{:S(2)}, u32[]{:S(2)}) collective-permute-start(bf16[16,80,128]{2,1,0:T(8,128)(2,1)S(1)} %coeff.3.mine), channel_id=1, source_target_pairs={{0,1},{1,0},{2,3},{3,2},{4,5},{5,4},{6,7},{7,6},{8,9},{9,8},{10,11... | collective-permute-start | bytes 983048 | tf_op jit(solution)/shard_map/ppermute | solution.py:479
  50.6 11.8 %all-to-all-start.1 = ((f32[16,16,128]{2,1,0:T(8,128)}), f32[16,16,128]{2,1,0:T(8,128)S(1)}, u32[]{:S(2)}, u32[]{:S(2)}) async-start(f32[16,16,128]{2,1,0:T(8,128)} %get-tuple-element.10), calls=%async_computation.1 | async-start | bytes 262144 | tf_op jit(solution)/shard_map/all_to_all | solution.py:517
  54.4 0.8 %copy-start.16 = (bf16[2,2,8192]{2,1,0:T(2,128)(2,1)S(1)}, bf16[2,2,8192]{2,1,0:T(2,128)(2,1)}, u32[]{:S(2)}) copy-start(bf16[2,2,8192]{2,1,0:T(2,128)(2,1)} %query.1) | copy-start | bytes 196612
  54.4 0.8 %copy-start.17 = (bf16[2,2,2048]{2,1,0:T(2,128)(2,1)S(1)}, bf16[2,2,2048]{2,1,0:T(2,128)(2,1)}, u32[]{:S(2)}) copy-start(bf16[2,2,2048]{2,1,0:T(2,128)(2,1)} %cache_new.1) | copy-start | bytes 49156
  54.5 0.8 %copy-start.18 = (s32[1,8]{1,0:T(1,128)S(1)}, s32[1,8]{1,0:T(1,128)}, u32[]{:S(2)}) copy-start(s32[1,8]{1,0:T(1,128)} %pages.1) | copy-start | bytes 100
  55.3 7.1 %copy-start.7 = (bf16[2,2,4096]{2,1,0:T(2,128)(2,1)S(1)}, bf16[2,2,4096]{2,1,0:T(2,128)(2,1)}, u32[]{:S(2)}) copy-start(bf16[2,2,4096]{2,1,0:T(2,128)(2,1)} %new_gate.1) | copy-start | bytes 98308
  55.3 7.1 %copy-start.10 = (f32[4096]{0:T(1024)S(1)}, f32[4096]{0:T(1024)}, u32[]{:S(2)}) copy-start(f32[4096]{0:T(1024)} %param.33) | copy-start | bytes 49156

commit v2 on v1

--- a/solution.py
+++ b/solution.py
@@ -20,7 +20,12 @@
 
 SMEM = pl.BlockSpec(memory_space=pltpu.SMEM)
 VMEM = pl.BlockSpec(memory_space=pltpu.VMEM)
+ANY = pl.BlockSpec(memory_space=pl.ANY)
 PARAMS = pltpu.CompilerParams(vmem_limit_bytes=48 * 1024 * 1024)
+
+
+def cost(microseconds):
+    return pl.CostEstimate(flops=0, bytes_accessed=microseconds * 3_500_000, transcendentals=0)
 
 
 def iota(shape, dim):
@@ -43,7 +48,7 @@
     lax.fori_loop(0, count.shape[0], clear, 0)
 
     def one(r, carry):
-        owner = owners[r, 0]
+        owner = owners[r]
         rank = count[owner]
         rank_ref[r] = rank
         count[owner] = rank + 1
@@ -52,29 +57,38 @@
     lax.fori_loop(0, owners.shape[0], one, 0)
 
 
-def pack_kernel(owners, coeff, cache, hidden, coeff_new, step_new, send, count, source):
+def pack_kernel(coeff, hidden_in, coeff_new_in, step_in, send, hidden, coeff_new, step_new, sems):
     devices = send.shape[0]
     slots = hidden.shape[0]
     group_devs = devices // GROUPS
     span = coeff.shape[1]
-    width = cache.shape[2]
-
-    def clear(d, carry):
-        count[d] = 0
-        for k in range(slots):
-            source[d * slots + k] = 0
-        return carry
-
-    lax.fori_loop(0, devices, clear, 0)
-
-    def place(r, carry):
-        owner = owners[r, 0]
-        rank = count[owner]
-        source[owner * slots + rank] = r
-        count[owner] = rank + 1
-        return carry
-
-    lax.fori_loop(0, owners.shape[0], place, 0)
+    news = [
+        pltpu.make_async_copy(a, b, sems.at[i])
+        for i, (a, b) in enumerate(
+            ((hidden_in, hidden), (coeff_new_in, coeff_new), (step_in, step_new))
+        )
+    ]
+
+    def start_of(d):
+        return pl.multiple_of((d // group_devs * 2 + lax.rem(d, 2)) * LANES, LANES)
+
+    def piece(d):
+        return pltpu.make_async_copy(
+            coeff.at[0, :, pl.ds(start_of(d), LANES)],
+            send.at[d, pl.ds(0, span), :],
+            sems.at[3 + d],
+        )
+
+    for copy in news:
+        copy.start()
+
+    def begin(d, carry):
+        piece(d).start()
+        return carry
+
+    lax.fori_loop(0, devices, begin, 0)
+    for copy in news:
+        copy.wait()
 
     heads = step_new.shape[2]
     steps = jnp.concatenate([step_new[k] for k in range(slots)], axis=0)
@@ -87,15 +101,12 @@
     lane = iota((8, LANES), 1)
 
     def one(d, carry):
-        group = d // group_devs
-        start = pl.multiple_of((group * 2 + lax.rem(d, 2)) * LANES, LANES)
-        send[d, 0:span, :] = coeff[0, :, pl.ds(start, LANES)]
         own = pl.multiple_of(d * 2 * LANES, 2 * LANES)
         rows = jnp.concatenate(
             [hidden[k, :, pl.ds(own, 2 * LANES)].astype(F32) for k in range(slots)], axis=0
         )
         tokens = jnp.concatenate(
-            [coeff_new[k, :, pl.ds(start, LANES)].astype(F32) for k in range(slots)], axis=0
+            [coeff_new[k, :, pl.ds(start_of(d), LANES)].astype(F32) for k in range(slots)], axis=0
         )
         mine = pltpu.roll(steps, lax.rem(padded - d * 4, padded), 1)[:, :LANES]
         high = mine.astype(BF16).astype(F32)
@@ -107,16 +118,50 @@
         )
         block = jnp.concatenate([rows[:, :LANES], rows[:, LANES:], tokens, split[0:4]], axis=0)
         send[d, span : span + NEW, :] = block.astype(BF16)
+        return carry
+
+    lax.fori_loop(0, devices, one, 0, unroll=4)
+
+    def end(d, carry):
+        piece(d).wait()
+        return carry
+
+    lax.fori_loop(0, devices, end, 0)
+
+
+def pack_cache_kernel(owners, cache, send, count, source):
+    devices = send.shape[0]
+    slots = source.shape[0] // devices
+    width = cache.shape[2]
+
+    def clear(d, carry):
+        count[d] = 0
+        for k in range(slots):
+            source[d * slots + k] = 0
+        return carry
+
+    lax.fori_loop(0, devices, clear, 0)
+
+    def place(r, carry):
+        owner = owners[r]
+        rank = count[owner]
+        source[owner * slots + rank] = r
+        count[owner] = rank + 1
+        return carry
+
+    lax.fori_loop(0, owners.shape[0], place, 0)
+
+    def one(d, carry):
         kept = jnp.concatenate(
             [cache[source[d * slots + k]].astype(F32) for k in range(slots)], axis=0
         )
         kept = jnp.concatenate(
             [kept[:, c * LANES : (c + 1) * LANES] for c in range(width // LANES)], axis=0
         )
-        send[d, span + NEW :, :] = kept.astype(BF16)
-        return carry
-
-    lax.fori_loop(0, devices, one, 0)
+        send[d] = kept.astype(BF16)
+        return carry
+
+    lax.fori_loop(0, devices, one, 0, unroll=2)
 
 
 def spliced(rows, first, second, length):
@@ -145,7 +190,7 @@
     taps = taps_ref[:, pl.ds(start, LANES)].astype(F32)
 
     def one(r, carry):
-        new = recv[owners[r, 0], span : span + NEW, :].astype(F32)
+        new = recv[owners[r], span : span + NEW, :].astype(F32)
         is_first = rank_ref[r] == 0
         first = jnp.where(is_first, new[8:9], new[10:11])
         second = jnp.where(is_first, new[9:10], new[11:12])
@@ -187,7 +232,7 @@
     fin[...] = jnp.zeros_like(fin)
 
     def fetch(r, carry):
-        new = new_ref[owners[r, 0]].astype(F32)
+        new = new_ref[owners[r]].astype(F32)
         is_first = rank_ref[r] == 0
         tokens[0, pl.ds(r, 1), :] = jnp.where(is_first, new[12:13], new[14:15])
         tokens[1, pl.ds(r, 1), :] = jnp.where(is_first, new[13:14], new[15:16])
@@ -231,7 +276,7 @@
     column_of = iota((span, LANES), 1)
 
     def one(r, squares):
-        owner = owners[r, 0]
+        owner = owners[r]
         rank = rank_ref[r]
         length = lengths[r]
         new = new_ref[owner].astype(F32)
@@ -284,7 +329,7 @@
     me = lax.axis_index(AXES)
 
     def one(r, found):
-        is_mine = owners[r, 0] == me
+        is_mine = owners[r] == me
         seen = found[-1]
         lens = [
             jnp.where(is_mine & (seen == k), lengths[r], found[k]) for k in range(slots)
@@ -450,16 +495,33 @@
     per_owner = pltpu.SMEM((devices,), jnp.int32)
     per_prompt = pltpu.SMEM((prompts,), jnp.int32)
 
+    owners = owners[:, 0]
     send = pl.pallas_call(
         pack_kernel,
-        out_shape=jax.ShapeDtypeStruct((devices, span + NEW + kept_rows, LANES), BF16),
-        in_specs=[SMEM, VMEM, VMEM, VMEM, VMEM, VMEM],
+        out_shape=jax.ShapeDtypeStruct((devices, span + NEW, LANES), BF16),
+        in_specs=[ANY, ANY, ANY, ANY],
+        out_specs=VMEM,
+        scratch_shapes=[
+            pltpu.VMEM(new_hidden.shape, BF16),
+            pltpu.VMEM(new_coeff.shape, BF16),
+            pltpu.VMEM(new_step.shape, F32),
+            pltpu.SemaphoreType.DMA((3 + devices,)),
+        ],
+        name="pack",
+    )(coeff_pre, new_hidden, new_coeff, new_step)
+    recv = lax.all_to_all(send, AXES, split_axis=0, concat_axis=0, tiled=True)
+    kept = pl.pallas_call(
+        pack_cache_kernel,
+        out_shape=jax.ShapeDtypeStruct((devices, kept_rows, LANES), BF16),
+        in_specs=[SMEM, VMEM],
         out_specs=VMEM,
         scratch_shapes=[per_owner, pltpu.SMEM((devices * slots,), jnp.int32)],
         compiler_params=PARAMS,
-        name="pack",
-    )(owners, coeff_pre, cache_rows, new_hidden, new_coeff, new_step)
-    recv = lax.all_to_all(send, AXES, split_axis=0, concat_axis=0, tiled=True)
+        cost_estimate=cost(3),
+        name="pack_cache",
+    )(owners, cache_rows)
+    kept, recv = lax.optimization_barrier((kept, recv))
+    kept = lax.all_to_all(kept, AXES, split_axis=0, concat_axis=0, tiled=True)
 
     mine = pl.pallas_call(
         coeff_kernel,
@@ -474,6 +536,7 @@
         out_specs=VMEM,
         scratch_shapes=[per_owner, per_prompt],
         compiler_params=PARAMS,
+        cost_estimate=cost(2),
         name="coeff",
     )(owners, lengths, conv_coeff, recv)
     other = lax.ppermute(mine, "side", [(0, 1), (1, 0)])
@@ -499,6 +562,7 @@
             pltpu.VMEM((prompts, 8, LANES), F32),
         ],
         compiler_params=PARAMS,
+        cost_estimate=cost(10),
         name="main",
     )(
         owners,
@@ -514,9 +578,9 @@
         gate_pre,
         step_raw,
     )
+    fin, kept = lax.optimization_barrier((fin, kept))
     fin_got = lax.all_to_all(fin, AXES, split_axis=0, concat_axis=0, tiled=True)
 
-    kept = recv[:, span + NEW :, :]
     cache_pool, decode_attention = pl.pallas_call(
         cache_kernel,
         out_shape=(
@@ -527,9 +591,7 @@
         out_specs=(VMEM, VMEM),
         scratch_shapes=[pltpu.VMEM((slots * span, cache_width), BF16)],
         compiler_params=PARAMS,
-        cost_estimate=pl.CostEstimate(
-            flops=200_000_000, bytes_accessed=4_000_000, transcendentals=100_000
-        ),
+        cost_estimate=cost(5),
         name="cache",
     )(owners, lengths, page_table, kept, new_query, new_cache)
 

time: 64.9 us -> 55 us (0.85)
  blocking collectives: 28.7 us -> 0 us
  starting transfers between devices: 4.66 us -> 16.4 us
  waiting for transfers between devices: 3.81 us -> 14.7 us
  local copies, waits for them, and re-layouts: 4.98 us -> 0.72 us
    all_to_all x1 -> x0, blocking collectives: 28.7 us -> none  [local(): recv = lax.all_to_all(send, AXES, split_axis=0, concat_axis=0, tiled=True)]
    all_to_all x0 -> x2, starting transfers between devices: none -> 11.2 us  [the longest x1 7.53 us: local(): recv = lax.all_to_all(send, AXES, split_axis=0, concat_axis=0, tiled=True)]
    all_to_all x0 -> x2, waiting for transfers between devices: none -> 9.91 us  [the longest x1 8.6 us: local(): recv = lax.all_to_all(send, AXES, split_axis=0, concat_axis=0, tiled=True)]
    unnamed x39 -> x32, local copies, waits for them, and re-layouts: 4.94 us -> 0.72 us
    pallas_call x0 -> x1, Pallas kernels: none -> 1.83 us  [local(): pl.pallas_call(pack_cache_kernel, out_shape=jax.ShapeDtypeStruct((devices...]
    all_to_all x1, starting transfers between devices: 3.82 us -> 4.82 us  [local(): fin_got = lax.all_to_all(fin, AXES, split_axis=0, concat_axis=0, tiled=True)]
    pallas_call x1, Pallas kernels: 3.32 us -> 2.38 us  [local(): pl.pallas_call(pack_kernel, out_shape=jax.ShapeDtypeStruct((devices, span...]
    all_to_all x1, waiting for transfers between devices: 2.55 us -> 3.49 us  [local(): fin_got = lax.all_to_all(fin, AXES, split_axis=0, concat_axis=0, tiled=True)]
  transfers between devices with their start and end apart: 2 -> 4, of which waited for: 2 -> 4; matrix products, arithmetic and copies ran while one was open for 0% -> 0% of each run, Pallas kernels for 7% -> 32%
where the time goes in v2:
time: 55 us; the launch traced here: 54.5 us
  Pallas kernels  21.7 us (39%)
  starting transfers between devices  16.4 us (30%)
  waiting for transfers between devices  14.7 us (27%)
  between operations  0.84 us (2%)
  local copies, waits for them, and re-layouts  0.72 us (1%)
    pallas_call x1, Pallas kernels, local(): pl.pallas_call(main_kernel, grid=(1,), out_shape=(jax.ShapeDtypeStruct((p...  9.8 us
    all_to_all x1, waiting for transfers between devices, local(): recv = lax.all_to_all(send, AXES, split_axis=0, concat_axis=0, tiled=True)  8.6 us
    all_to_all x1, starting transfers between devices, local(): recv = lax.all_to_all(send, AXES, split_axis=0, concat_axis=0, tiled=True)  7.53 us
    all_to_all x1, starting transfers between devices, local(): fin_got = lax.all_to_all(fin, AXES, split_axis=0, concat_axis=0, tiled=True)  4.82 us
    pallas_call x1, Pallas kernels, local(): pl.pallas_call(cache_kernel, out_shape=(jax.ShapeDtypeStruct((page_table....  4.39 us
    all_to_all x1, starting transfers between devices, local(): kept = lax.all_to_all(kept, AXES, split_axis=0, concat_axis=0, tiled=True)  3.71 us
    all_to_all x1, waiting for transfers between devices, local(): fin_got = lax.all_to_all(fin, AXES, split_axis=0, concat_axis=0, tiled=True)  3.49 us
    pallas_call x1, Pallas kernels, local(): pl.pallas_call(pack_kernel, out_shape=jax.ShapeDtypeStruct((devices, span...  2.38 us
  transfers between devices with their start and end apart: 4, of which 4 were waited for; matrix products, arithmetic and copies ran while one was open for 0% of the time, Pallas kernels for 32%

profile of v2, /device:TPU:0, one launch (start us, length us, event | category | flops | bytes accessed | tf_op | source)
XLA Modules:
  0.0 54.5 jit_solution(4374282218467306826)
XLA Ops:
  0.6 2.4 %pack.1 = bf16[16,80,128]{2,1,0:T(8,128)(2,1)} custom-call(bf16[1,64,2048]{2,1,0:T(8,128)(2,1)} %coeff.2, bf16[2,2,4096]{2,1,0:T(2,128)(2,1)} %hidden_in.1, bf16[2,2,2048]{2,1,0:T(2,128)(2,1)} %coeff_new_in.1, f32[2,2,64]{2,1,0:T(2,128)} %step_in.1), custom_call_target="tpu_custom_call" | custom-call | tf_op jit(solution)/shard_map/pack/pallas_call | solution.py:499
  3.0 0.0 copy-start.2
  3.0 7.5 %all-to-all-start = ((bf16[16,80,128]{2,1,0:T(8,128)(2,1)}), bf16[16,80,128]{2,1,0:T(8,128)(2,1)S(1)}, u32[]{:S(2)}, u32[]{:S(2)}) async-start(bf16[16,80,128]{2,1,0:T(8,128)(2,1)} %pack.1), calls=%async_computation | async-start | bytes 655360 | tf_op jit(solution)/shard_map/all_to_all | solution.py:512
  10.6 0.0 copy-start.10
  10.6 0.0 copy-done.2
  10.6 0.6 %copy-done.10 = s32[16,1]{0,1:T(1,128)S(1)} copy-done((s32[16,1]{0,1:T(1,128)S(1)}, s32[16,1]{0,1:T(1,128)}, u32[]{:S(2)}) %copy-start.10) | copy-done | bytes 88
  11.2 1.8 %pack_cache.1 = bf16[16,128,128]{2,1,0:T(8,128)(2,1)} custom-call(s32[16]{0:T(128)S(1)} %bitcast.3, bf16[16,4,2048]{2,1,0:T(4,128)(2,1)S(1)} %copy-done.2), custom_call_target="tpu_custom_call" | custom-call | bytes 10500000 | tf_op jit(solution)/shard_map/pack_cache/pallas_call | solution.py:513
  13.1 0.0 copy-start.9
  13.1 0.0 copy-start.11
  13.1 8.6 %all-to-all-done.recv.new_ref = bf16[16,80,128]{2,1,0:T(8,128)(2,1)S(1)} async-done(((bf16[16,80,128]{2,1,0:T(8,128)(2,1)}), bf16[16,80,128]{2,1,0:T(8,128)(2,1)S(1)}, u32[]{:S(2)}, u32[]{:S(2)}) %all-to-all-start) | async-done | bytes 327712 | tf_op jit(solution)/shard_map/all_to_all | solution.py:512
  21.7 0.0 copy-start.1
  21.7 3.7 %all-to-all-start.1 = ((bf16[16,128,128]{2,1,0:T(8,128)(2,1)}), bf16[16,128,128]{2,1,0:T(8,128)(2,1)S(1)}, u32[]{:S(2)}, u32[]{:S(2)}) async-start(bf16[16,128,128]{2,1,0:T(8,128)(2,1)} %pack_cache.1), calls=%async_computation.1 | async-start | bytes 1048576 | tf_op jit(solution)/shard_map/all_to_all | solution.py:524
  25.4 0.0 copy-done.9
  25.4 0.0 copy-done.11
  25.4 0.0 copy-start
  25.4 0.0 copy-start.4
  25.4 0.0 copy-start.5
  25.4 0.0 copy-start.13
  25.5 0.0 copy-start.14
  25.5 0.0 copy-start.15
  25.5 1.5 %coeff.3.mine = bf16[16,80,128]{2,1,0:T(8,128)(2,1)S(1)} custom-call(s32[16]{0:T(128)S(1)} %bitcast.4, s32[16]{0:T(128)S(1)} %copy-done.11, bf16[4,2048]{1,0:T(4,128)(2,1)S(1)} %copy-done.9, bf16[16,80,128]{2,1,0:T(8,128)(2,1)S(1)} %all-to-all-done.recv.new_ref), custom_call_target="tpu_custom_call" | custom-call | bytes 7000000 | tf_op jit(solution)/shard_map/coeff/pallas_call | solution.py:526
  27.0 0.4 collective-permute-start
  27.3 1.3 %collective-permute-done.other = bf16[16,80,128]{2,1,0:T(8,128)(2,1)S(1)} collective-permute-done((bf16[16,80,128]{2,1,0:T(8,128)(2,1)S(1)}, bf16[16,80,128]{2,1,0:T(8,128)(2,1)S(1)}, u32[]{:S(2)}, u32[]{:S(2)}) %collective-permute-start) | collective-permute-done | bytes 327712 | tf_op jit(solution)/shard_map/ppermute | solution.py:542
  28.7 0.0 copy-done.1
  28.7 0.0 copy-done
  28.7 0.0 copy-done.4
  28.7 0.0 copy-done.5
  28.7 0.0 copy-done.13
  28.7 0.0 copy-done.14
  28.7 0.0 copy-done.15
  28.7 9.8 %main.1 = (f32[16,64,256]{2,1,0:T(8,128)S(1)}, f32[16,16,128]{2,1,0:T(8,128)}) custom-call(s32[16]{0:T(128)S(1)} %bitcast.5, s32[16]{0:T(128)S(1)} %copy-done.11, f32[64]{0:T(128)S(1)} %copy-done.13, f32[64]{0:T(128)S(1)} %copy-done.14, f32[64]{0:T(128)S(1)} %copy-done.15, bf16[4,4096]{1,0:T(4,128)(2,1)S(1)} %copy-done.4, ...), custom_call_target="tpu_custom_call" | custom-call | bytes 35000000 | tf_op jit(solution)/shard_map/main/pallas_call | solution.py:545
  38.5 1.3 %all-to-all-done.1.recv = bf16[16,128,128]{2,1,0:T(8,128)(2,1)S(1)} async-done(((bf16[16,128,128]{2,1,0:T(8,128)(2,1)}), bf16[16,128,128]{2,1,0:T(8,128)(2,1)S(1)}, u32[]{:S(2)}, u32[]{:S(2)}) %all-to-all-start.1) | async-done | bytes 524320 | tf_op jit(solution)/shard_map/all_to_all | solution.py:524
  39.8 0.0 copy-start.3
  39.8 0.0 copy-start.8
  39.8 0.0 copy-start.12
  39.8 4.8 %all-to-all-start.2 = ((f32[16,16,128]{2,1,0:T(8,128)}), f32[16,16,128]{2,1,0:T(8,128)S(1)}, u32[]{:S(2)}, u32[]{:S(2)}) async-start(f32[16,16,128]{2,1,0:T(8,128)} %get-tuple-element.17), calls=%async_computation.2 | async-start | bytes 262144 | tf_op jit(solution)/shard_map/all_to_all | solution.py:582
  44.6 0.0 copy-done.3
  44.7 0.0 copy-done.8
  44.7 0.0 copy-done.12
  44.7 0.0 copy-start.6
  44.7 0.0 copy-start.7
  44.7 4.4 %cache.3 = (bf16[8,16,2048]{2,1,0:T(8,128)(2,1)}, bf16[2,2,8192]{2,1,0:T(2,128)(2,1)}) custom-call(s32[16]{0:T(128)S(1)} %bitcast.6, s32[16]{0:T(128)S(1)} %copy-done.11, s32[1,8]{1,0:T(1,128)S(1)} %copy-done.12, bf16[16,128,128]{2,1,0:T(8,128)(2,1)S(1)} %all-to-all-done.1.recv, bf16[2,2,8192]{2,1,0:T(2,128)(2,1)S(1)} %copy-done.3, ...), custom_call_target="tpu_custom_call" | custom-call | bytes 17500000 | tf_op jit(solution)/shard_map/cache/pallas_call | solution.py:584
  49.1 3.5 %all-to-all-done.2.fin = f32[16,16,128]{2,1,0:T(8,128)S(1)} async-done(((f32[16,16,128]{2,1,0:T(8,128)}), f32[16,16,128]{2,1,0:T(8,128)S(1)}, u32[]{:S(2)}, u32[]{:S(2)}) %all-to-all-start.2) | async-done | bytes 131104 | tf_op jit(solution)/shard_map/all_to_all | solution.py:582
  52.6 0.0 copy-done.6
  52.6 0.0 copy-done.7
  52.6 1.9 %final.1 = (bf16[16,64,256]{2,1,0:T(8,128)(2,1)}, bf16[2,2,4096]{2,1,0:T(2,128)(2,1)}) custom-call(s32[16]{0:T(128)S(1)} %bitcast.7, s32[16]{0:T(128)S(1)} %copy-done.11, f32[1,4096]{1,0:T(1,128)S(1)} %bitcast.2, f32[16,16,128]{2,1,0:T(8,128)S(1)} %all-to-all-done.2.fin, f32[16,64,256]{2,1,0:T(8,128)S(1)} %get-tuple-element.18.gated, ...), custom_call_target="tpu_custom_call" | custom-call | tf_op jit(solution)/shard_map/final/pallas_call | solution.py:598
Async XLA Ops:
  3.0 7.6 %copy-start.2 = (bf16[16,4,2048]{2,1,0:T(4,128)(2,1)S(1)}, bf16[16,4,2048]{2,1,0:T(4,128)(2,1)}, u32[]{:S(2)}) copy-start(bf16[16,4,2048]{2,1,0:T(4,128)(2,1)} %cache.2) | copy-start | bytes 786436
  3.0 18.6 %all-to-all-start = ((bf16[16,80,128]{2,1,0:T(8,128)(2,1)}), bf16[16,80,128]{2,1,0:T(8,128)(2,1)S(1)}, u32[]{:S(2)}, u32[]{:S(2)}) async-start(bf16[16,80,128]{2,1,0:T(8,128)(2,1)} %pack.1), calls=%async_computation | async-start | bytes 655360 | tf_op jit(solution)/shard_map/all_to_all | solution.py:512
  10.6 0.7 %copy-start.10 = (s32[16,1]{0,1:T(1,128)S(1)}, s32[16,1]{0,1:T(1,128)}, u32[]{:S(2)}) copy-start(s32[16,1]{0,1:T(1,128)} %param.26) | copy-start | bytes 196
  13.1 12.3 %copy-start.9 = (bf16[4,2048]{1,0:T(4,128)(2,1)S(1)}, bf16[4,2048]{1,0:T(4,128)(2,1)}, u32[]{:S(2)}) copy-start(bf16[4,2048]{1,0:T(4,128)(2,1)} %taps_ref.2) | copy-start | bytes 49156
  13.1 12.3 %copy-start.11 = (s32[16]{0:T(128)S(1)}, s32[16]{0:T(128)}, u32[]{:S(2)}) copy-start(s32[16]{0:T(128)} %lengths.7) | copy-start | bytes 196
  21.7 7.0 %copy-start.1 = (bf16[16,64,256]{2,1,0:T(8,128)(2,1)S(1)}, bf16[16,64,256]{2,1,0:T(8,128)(2,1)}, u32[]{:S(2)}) copy-start(bf16[16,64,256]{2,1,0:T(8,128)(2,1)} %gate.1) | copy-start | bytes 1572868
  21.7 18.1 %all-to-all-start.1 = ((bf16[16,128,128]{2,1,0:T(8,128)(2,1)}), bf16[16,128,128]{2,1,0:T(8,128)(2,1)S(1)}, u32[]{:S(2)}, u32[]{:S(2)}) async-start(bf16[16,128,128]{2,1,0:T(8,128)(2,1)} %pack_cache.1), calls=%async_computation.1 | async-start | bytes 1048576 | tf_op jit(solution)/shard_map/all_to_all | solution.py:524
  25.4 3.3 %copy-start = (bf16[16,64,256]{2,1,0:T(8,128)(2,1)S(1)}, bf16[16,64,256]{2,1,0:T(8,128)(2,1)}, u32[]{:S(2)}) copy-start(bf16[16,64,256]{2,1,0:T(8,128)(2,1)} %hidden.1) | copy-start | bytes 1572868
  25.4 3.2 %copy-start.4 = (bf16[4,4096]{1,0:T(4,128)(2,1)S(1)}, bf16[4,4096]{1,0:T(4,128)(2,1)}, u32[]{:S(2)}) copy-start(bf16[4,4096]{1,0:T(4,128)(2,1)} %taps_ref.3) | copy-start | bytes 98308
  25.4 3.2 %copy-start.5 = (f32[4,16,64]{2,1,0:T(8,128)S(1)}, f32[4,16,64]{2,1,0:T(8,128)}, u32[]{:S(2)}) copy-start(f32[4,16,64]{2,1,0:T(8,128)} %step.1) | copy-start | bytes 49156
  25.4 3.2 %copy-start.13 = (f32[64]{0:T(128)S(1)}, f32[64]{0:T(128)}, u32[]{:S(2)}) copy-start(f32[64]{0:T(128)} %bias.1) | copy-start | bytes 772
  25.5 3.2 %copy-start.14 = (f32[64]{0:T(128)S(1)}, f32[64]{0:T(128)}, u32[]{:S(2)}) copy-start(f32[64]{0:T(128)} %decay.1) | copy-start | bytes 772
  25.5 3.2 %copy-start.15 = (f32[64]{0:T(128)S(1)}, f32[64]{0:T(128)}, u32[]{:S(2)}) copy-start(f32[64]{0:T(128)} %skip.1) | copy-start | bytes 772
  27.0 1.7 %collective-permute-start = (bf16[16,80,128]{2,1,0:T(8,128)(2,1)S(1)}, bf16[16,80,128]{2,1,0:T(8,128)(2,1)S(1)}, u32[]{:S(2)}, u32[]{:S(2)}) collective-permute-start(bf16[16,80,128]{2,1,0:T(8,128)(2,1)S(1)} %coeff.3.mine), channel_id=1, source_target_pairs={{0,1},{1,0},{2,3},{3,2},{4,5},{5,4},{6,7},{7,6},{8,9},{9,8},{10,11... | collective-permute-start | bytes 983048 | tf_op jit(solution)/shard_map/ppermute | solution.py:542
  39.8 4.8 %copy-start.3 = (bf16[2,2,8192]{2,1,0:T(2,128)(2,1)S(1)}, bf16[2,2,8192]{2,1,0:T(2,128)(2,1)}, u32[]{:S(2)}) copy-start(bf16[2,2,8192]{2,1,0:T(2,128)(2,1)} %query.1) | copy-start | bytes 196612
  39.8 4.8 %copy-start.8 = (bf16[2,2,2048]{2,1,0:T(2,128)(2,1)S(1)}, bf16[2,2,2048]{2,1,0:T(2,128)(2,1)}, u32[]{:S(2)}) copy-start(bf16[2,2,2048]{2,1,0:T(2,128)(2,1)} %cache_new.1) | copy-start | bytes 49156
  39.8 4.9 %copy-start.12 = (s32[1,8]{1,0:T(1,128)S(1)}, s32[1,8]{1,0:T(1,128)}, u32[]{:S(2)}) copy-start(s32[1,8]{1,0:T(1,128)} %pages.1) | copy-start | bytes 100
  39.8 12.8 %all-to-all-start.2 = ((f32[16,16,128]{2,1,0:T(8,128)}), f32[16,16,128]{2,1,0:T(8,128)S(1)}, u32[]{:S(2)}, u32[]{:S(2)}) async-start(f32[16,16,128]{2,1,0:T(8,128)} %get-tuple-element.17), calls=%async_computation.2 | async-start | bytes 262144 | tf_op jit(solution)/shard_map/all_to_all | solution.py:582
  44.7 7.9 %copy-start.6 = (bf16[2,2,4096]{2,1,0:T(2,128)(2,1)S(1)}, bf16[2,2,4096]{2,1,0:T(2,128)(2,1)}, u32[]{:S(2)}) copy-start(bf16[2,2,4096]{2,1,0:T(2,128)(2,1)} %new_gate.1) | copy-start | bytes 98308
  44.7 7.9 %copy-start.7 = (f32[4096]{0:T(1024)S(1)}, f32[4096]{0:T(1024)}, u32[]{:S(2)}) copy-start(f32[4096]{0:T(1024)} %param.33) | copy-start | bytes 49156

commit v3 on v2

--- a/solution.py
+++ b/solution.py
@@ -120,7 +120,7 @@
         send[d, span : span + NEW, :] = block.astype(BF16)
         return carry
 
-    lax.fori_loop(0, devices, one, 0, unroll=4)
+    lax.fori_loop(0, devices, one, 0, unroll=8)
 
     def end(d, carry):
         piece(d).wait()
@@ -129,8 +129,9 @@
     lax.fori_loop(0, devices, end, 0)
 
 
-def pack_cache_kernel(owners, cache, send, count, source):
-    devices = send.shape[0]
+def pack_cache_kernel(owners, cache, *refs):
+    outs, (count, source) = refs[:-2], refs[-2:]
+    devices = count.shape[0]
     slots = source.shape[0] // devices
     width = cache.shape[2]
 
@@ -140,7 +141,7 @@
             source[d * slots + k] = 0
         return carry
 
-    lax.fori_loop(0, devices, clear, 0)
+    lax.fori_loop(0, devices, clear, 0, unroll=4)
 
     def place(r, carry):
         owner = owners[r]
@@ -149,19 +150,23 @@
         count[owner] = rank + 1
         return carry
 
-    lax.fori_loop(0, owners.shape[0], place, 0)
-
-    def one(d, carry):
-        kept = jnp.concatenate(
-            [cache[source[d * slots + k]].astype(F32) for k in range(slots)], axis=0
-        )
-        kept = jnp.concatenate(
-            [kept[:, c * LANES : (c + 1) * LANES] for c in range(width // LANES)], axis=0
-        )
-        send[d] = kept.astype(BF16)
-        return carry
-
-    lax.fori_loop(0, devices, one, 0, unroll=2)
+    lax.fori_loop(0, owners.shape[0], place, 0, unroll=4)
+    me = lax.axis_index(AXES)
+    for m, out in enumerate(outs):
+        for x in range(2):
+            d = me ^ (2 * m + x)
+            kept = jnp.concatenate(
+                [cache[source[d * slots + k]].astype(F32) for k in range(slots)], axis=0
+            )
+            kept = jnp.concatenate(
+                [kept[:, c * LANES : (c + 1) * LANES] for c in range(width // LANES)], axis=0
+            )
+            out[x] = kept.astype(BF16)
+
+
+def stack_kernel(*refs):
+    for m, ref in enumerate(refs[:-1]):
+        refs[-1][m] = ref[1]
 
 
 def spliced(rows, first, second, length):
@@ -198,32 +203,78 @@
         out[r] = conv(rows, taps)
         return carry
 
+    lax.fori_loop(0, prompts, one, 0, unroll=4)
+
+
+def before_kernel(
+    lengths, bias, decay, skip, taps_ref, hidden, step, u_ref, tail_ref, head_ref, dt_ref, sum_ref
+):
+    prompts, span, columns = hidden.shape
+    local_heads = step.shape[0]
+    me = lax.axis_index(AXES)
+    taps = taps_ref[:, pl.ds(pl.multiple_of(me * columns, LANES), columns)].astype(F32)
+
+    def widths(r, lens):
+        return jnp.where(iota((prompts, LANES), 0) == r, lengths[r], lens)
+
+    lens = lax.fori_loop(0, prompts, widths, jnp.zeros((prompts, LANES), jnp.int32), unroll=4)
+    lane = iota((prompts, LANES), 1)
+    for h in range(local_heads):
+        raw = jnp.concatenate([step[h], jnp.zeros((prompts, LANES - span), F32)], axis=1)
+        size = jnp.where(lane < lens, softplus(raw + bias[me * local_heads + h]), 0.0)
+        total = size * -jnp.exp(jnp.full((1, LANES), decay[me * local_heads + h], F32))
+        shift = 1
+        while shift < span:
+            total = total + jnp.where(lane >= shift, pltpu.roll(total, shift, 1), 0.0)
+            shift *= 2
+        dt_ref[h] = size
+        sum_ref[h] = jnp.where(lane < span, total, total[:, span - 1 : span])
+    place = iota((span, columns), 0)
+    head_of = iota((1, columns), 1) // (columns // local_heads)
+    rows = [jnp.zeros((1, columns), F32)] * 3
+    for h in range(local_heads):
+        given = (skip[me * local_heads + h], bias[me * local_heads + h], decay[me * local_heads + h])
+        rows = [jnp.where(head_of == h, x, row) for x, row in zip(given, rows)]
+    rows[2] = -jnp.exp(rows[2])
+    head_ref[...] = jnp.concatenate([*rows, jnp.zeros((5, columns), F32)], axis=0)
+
+    def one(r, carry):
+        raw = hidden[r].astype(F32)
+        for j in range(CONVK - 1):
+            tail_ref[j, pl.ds(r, 1), :] = jnp.sum(
+                jnp.where(place == lengths[r] - 3 + j, raw, 0.0), axis=0, keepdims=True
+            )
+        longer = jnp.concatenate([raw, jnp.zeros((8, columns), F32)], axis=0)
+        u_ref[r] = conv(longer, taps)[0:span]
+        return carry
+
     lax.fori_loop(0, prompts, one, 0, unroll=2)
 
 
 def main_kernel(
     owners,
     lengths,
-    bias,
-    decay,
-    skip,
     taps_ref,
     mine,
     other,
     new_ref,
-    hidden,
     gate,
-    step,
+    u_ref,
+    tail_ref,
+    consts,
+    dt_given,
+    sum_given,
     gated_ref,
     fin,
     count,
     rank_ref,
     tokens,
+    rows_ref,
     dt_ref,
     sum_ref,
 ):
-    prompts, span, columns = hidden.shape
-    local_heads = step.shape[0]
+    prompts, span, columns = gate.shape
+    local_heads = dt_given.shape[0]
     head_size = columns // local_heads
     ranks(owners, count, rank_ref)
     me = lax.axis_index(AXES)
@@ -234,11 +285,18 @@
     def fetch(r, carry):
         new = new_ref[owners[r]].astype(F32)
         is_first = rank_ref[r] == 0
-        tokens[0, pl.ds(r, 1), :] = jnp.where(is_first, new[12:13], new[14:15])
-        tokens[1, pl.ds(r, 1), :] = jnp.where(is_first, new[13:14], new[15:16])
-        return carry
-
-    lax.fori_loop(0, prompts, fetch, 0)
+        for i in range(2):
+            tokens[i, pl.ds(r, 1), :] = jnp.where(is_first, new[12 + i : 13 + i], new[14 + i : 15 + i])
+            low = jnp.where(is_first, new[i : i + 1], new[2 + i : 3 + i])
+            high = jnp.where(is_first, new[4 + i : 5 + i], new[6 + i : 7 + i])
+            rows_ref[i, pl.ds(r, 1), :] = jnp.concatenate([low, high], axis=1)
+        return carry
+
+    lax.fori_loop(0, prompts, fetch, 0, unroll=4)
+    raws = [tail_ref[0], tail_ref[1], tail_ref[2], rows_ref[0], rows_ref[1]]
+    for i in range(2):
+        total = sum(raws[i + k] * taps[k : k + 1] for k in range(CONVK))
+        rows_ref[i] = silu(total).astype(BF16).astype(F32)
 
     def widths(r, lens):
         return jnp.where(iota((prompts, LANES), 0) == r, lengths[r], lens)
@@ -250,26 +308,19 @@
         raw = tokens[i]
         news.append(raw + pltpu.roll(raw, LANES - 32, 1) + pltpu.roll(raw, LANES - 64, 1))
     for h in range(local_heads):
-        raw = jnp.concatenate([step[h], jnp.zeros((prompts, LANES - span), F32)], axis=1)
-        raw = jnp.where(
-            lane == lens,
-            news[0][:, h : h + 1],
-            jnp.where(lane == lens + 1, news[1][:, h : h + 1], raw),
-        )
-        size = jnp.where(lane < lens + 2, softplus(raw + bias[me * local_heads + h]), 0.0)
-        rate = -jnp.exp(jnp.full((1, LANES), decay[me * local_heads + h], F32))
-        total = size * rate
-        shift = 1
-        while shift < LANES:
-            total = total + jnp.where(lane >= shift, pltpu.roll(total, shift, 1), 0.0)
-            shift *= 2
-        dt_ref[:, h, :] = size
-        sum_ref[:, h, :] = total
-
-    head_of = iota((1, columns), 1) // head_size
-    gain = jnp.zeros((1, columns), F32)
-    for h in range(local_heads):
-        gain = jnp.where(head_of == h, skip[me * local_heads + h], gain)
+        at = slice(h * head_size, h * head_size + 1)
+        rate = consts[2:3, at]
+        first, second = [softplus(x[:, h : h + 1] + consts[1:2, at]) for x in news]
+        dt_ref[:, h, :] = jnp.where(
+            lane == lens, first, jnp.where(lane == lens + 1, second, dt_given[h])
+        )
+        sum_ref[:, h, :] = (
+            sum_given[h]
+            + jnp.where(lane >= lens, first * rate, 0.0)
+            + jnp.where(lane > lens, second * rate, 0.0)
+        )
+
+    gain = consts[0:1, :]
     heads_wide = iota((ROWS, columns), 1) // head_size
     place = iota((ROWS, columns), 0)
     lower = iota((ROWS, ROWS), 0) >= iota((ROWS, ROWS), 1)
@@ -279,14 +330,15 @@
         owner = owners[r]
         rank = rank_ref[r]
         length = lengths[r]
-        new = new_ref[owner].astype(F32)
-        is_first = rank == 0
-        token = []
-        for i in range(2):
-            a = jnp.where(is_first, new[i : i + 1], new[2 + i : 3 + i])
-            b = jnp.where(is_first, new[4 + i : 5 + i], new[6 + i : 7 + i])
-            token.append(jnp.concatenate([a, b], axis=1))
-        u = conv(spliced(hidden[r].astype(F32), token[0], token[1], length), taps)
+        wide = jnp.concatenate(
+            [u_ref[r].astype(F32), jnp.zeros((ROWS - span, columns), F32)], axis=0
+        )
+        wide = jnp.where(
+            place == length,
+            rows_ref[0, pl.ds(r, 1), :],
+            jnp.where(place == length + 1, rows_ref[1, pl.ds(r, 1), :], wide),
+        )
+        u = wide.astype(BF16)
         here, there = mine[r], other[r]
         b_rows = jnp.where(is_b, here, there)
         c_rows = jnp.where(is_b, there, here)
@@ -296,7 +348,7 @@
         sums = sum_ref[r]
         sizes = dt_ref[r]
         turned = sums.T
-        out = gain * u.astype(F32)
+        out = gain * wide
         for h in range(local_heads):
             gap = turned[:ROWS, h : h + 1] - sums[h : h + 1, :ROWS]
             mix = jnp.where(lower, scores * jnp.exp(gap) * sizes[h : h + 1, :ROWS], 0.0)
@@ -313,7 +365,7 @@
         square = jnp.sum(gated * gated, axis=1, keepdims=True)
         return jnp.where(column_of == r, square, squares)
 
-    squares = lax.fori_loop(0, prompts, one, jnp.zeros((span, LANES), F32))
+    squares = lax.fori_loop(0, prompts, one, jnp.zeros((span, LANES), F32), unroll=4)
     turned = squares.T
     half = prompts // 2
     packed = jnp.concatenate([turned[0:half, :], turned[half:prompts, :]], axis=1)
@@ -322,7 +374,7 @@
         fin[d, 0:half, :] = packed
         return carry
 
-    lax.fori_loop(0, fin.shape[0], spread, 0)
+    lax.fori_loop(0, fin.shape[0], spread, 0, unroll=4)
 
 
 def slot_facts(owners, lengths, slots):
@@ -340,15 +392,16 @@
     return lax.fori_loop(0, owners.shape[0], one, (zero,) * (slots + 1))[:slots]
 
 
-def cache_kernel(owners, lengths, pages, recv, query, cache_new, pool, attended, rows_ref):
+def cache_kernel(owners, lengths, pages, query, cache_new, crossed, *refs):
+    straight, (pool, attended, rows_ref) = refs[:-3], refs[-3:]
     slots = query.shape[0]
     steps = query.shape[1]
-    sources = recv.shape[0]
+    chips = len(straight)
+    sources = 2 * chips
     width = pool.shape[2]
     parts = width // LANES
-    span = sources * (recv.shape[1] // parts) // slots
-    offset = 0
-    each = recv.shape[1] // parts
+    span = pool.shape[0] // slots * BLK
+    each = crossed.shape[1] // parts
     local = each // slots
     lens = slot_facts(owners, lengths, slots)
     keys = sources * each
@@ -356,7 +409,8 @@
     key = iota((slots * span, keys), 1)
     slot_of = row // span
     at = lax.rem(row, span)
-    wanted = at // local * each + slot_of * local + lax.rem(at, local)
+    apart = (at // local) ^ lax.axis_index(AXES)
+    wanted = (lax.rem(apart, 2) * chips + apart // 2) * each + slot_of * local + lax.rem(at, local)
     limit = jnp.where(slot_of == 0, lens[0], lens[1])
     order = jnp.where((key == wanted) & (at < limit), 1.0, 0.0).astype(BF16)
     ask = jnp.concatenate([query[k].astype(F32) for k in range(slots)], axis=0)
@@ -381,8 +435,12 @@
     filled = jnp.where(out_slot == 0, lens[0], lens[1]) > 0
 
     for c in range(parts):
-        block = recv[:, offset + c * each : offset + (c + 1) * each, :].astype(F32)
-        block = block.reshape(keys, LANES).astype(BF16)
+        strip = slice(c * each, (c + 1) * each)
+        block = jnp.concatenate(
+            [ref[0, strip, :].astype(F32) for ref in straight]
+            + [crossed[m, strip, :].astype(F32) for m in range(chips)],
+            axis=0,
+        ).astype(BF16)
         rows_ref[:, c * LANES : (c + 1) * LANES] = jnp.dot(
             order, block, preferred_element_type=F32
         ).astype(BF16)
@@ -510,18 +568,43 @@
         name="pack",
     )(coeff_pre, new_hidden, new_coeff, new_step)
     recv = lax.all_to_all(send, AXES, split_axis=0, concat_axis=0, tiled=True)
+    chips = devices // 2
     kept = pl.pallas_call(
         pack_cache_kernel,
-        out_shape=jax.ShapeDtypeStruct((devices, kept_rows, LANES), BF16),
+        out_shape=(jax.ShapeDtypeStruct((2, kept_rows, LANES), BF16),) * chips,
         in_specs=[SMEM, VMEM],
-        out_specs=VMEM,
+        out_specs=(VMEM,) * chips,
         scratch_shapes=[per_owner, pltpu.SMEM((devices * slots,), jnp.int32)],
         compiler_params=PARAMS,
         cost_estimate=cost(3),
         name="pack_cache",
     )(owners, cache_rows)
-    kept, recv = lax.optimization_barrier((kept, recv))
-    kept = lax.all_to_all(kept, AXES, split_axis=0, concat_axis=0, tiled=True)
+    kept = [kept[0]] + [
+        lax.ppermute(kept[m], "tensor", [(i, i ^ m) for i in range(chips)])
+        for m in range(1, chips)
+    ]
+    before = pl.pallas_call(
+        before_kernel,
+        out_shape=(
+            jax.ShapeDtypeStruct((prompts, span, columns), BF16),
+            jax.ShapeDtypeStruct((CONVK - 1, prompts, columns), F32),
+            jax.ShapeDtypeStruct((8, columns), F32),
+            jax.ShapeDtypeStruct((local_heads, prompts, LANES), F32),
+            jax.ShapeDtypeStruct((local_heads, prompts, LANES), F32),
+        ),
+        in_specs=[SMEM] * 4 + [VMEM] * 3,
+        out_specs=(VMEM,) * 5,
+        compiler_params=PARAMS,
+        cost_estimate=cost(4),
+        name="before",
+    )(lengths, step_bias, decay_log, skip_gain, conv_hidden, hidden_pre, step_raw)
+    early = (1, 2)
+    recv, sums, *held = lax.optimization_barrier(
+        (recv, before[-1], *(kept[m] for m in early))
+    )
+    before = (*before[:-1], sums)
+    for m, block in zip(early, held):
+        kept[m] = block
 
     mine = pl.pallas_call(
         coeff_kernel,
@@ -549,15 +632,16 @@
             jax.ShapeDtypeStruct((prompts, span, columns), F32),
             jax.ShapeDtypeStruct((devices, prompts // 2 + 8, LANES), F32),
         ),
-        in_specs=[SMEM] * 5
+        in_specs=[SMEM] * 2
         + [VMEM] * 3
         + [pl.BlockSpec((devices, NEW, LANES), lambda i: (0, new_block, 0))]
-        + [VMEM] * 3,
+        + [VMEM] * 6,
         out_specs=(VMEM, VMEM),
         scratch_shapes=[
             per_owner,
             per_prompt,
             pltpu.VMEM((2, prompts, LANES), F32),
+            pltpu.VMEM((2, prompts, columns), F32),
             pltpu.VMEM((prompts, 8, LANES), F32),
             pltpu.VMEM((prompts, 8, LANES), F32),
         ],
@@ -567,18 +651,24 @@
     )(
         owners,
         lengths,
-        step_bias,
-        decay_log,
-        skip_gain,
         conv_hidden,
         mine,
         other,
         recv,
-        hidden_pre,
         gate_pre,
-        step_raw,
+        *before,
     )
-    fin, kept = lax.optimization_barrier((fin, kept))
+    fin, *kept = lax.optimization_barrier((fin, *kept))
+    crossed = pl.pallas_call(
+        stack_kernel,
+        out_shape=jax.ShapeDtypeStruct((chips, kept_rows, LANES), BF16),
+        in_specs=[VMEM] * chips,
+        out_specs=VMEM,
+        compiler_params=PARAMS,
+        cost_estimate=cost(1),
+        name="stack",
+    )(*kept)
+    crossed = lax.ppermute(crossed, "side", [(0, 1), (1, 0)])
     fin_got = lax.all_to_all(fin, AXES, split_axis=0, concat_axis=0, tiled=True)
 
     cache_pool, decode_attention = pl.pallas_call(
@@ -587,14 +677,15 @@
             jax.ShapeDtypeStruct((page_table.shape[1], BLK, cache_width), BF16),
             jax.ShapeDtypeStruct(new_query.shape, BF16),
         ),
-        in_specs=[SMEM, SMEM, SMEM, VMEM, VMEM, VMEM],
+        in_specs=[SMEM] * 3 + [VMEM] * (3 + chips),
         out_specs=(VMEM, VMEM),
         scratch_shapes=[pltpu.VMEM((slots * span, cache_width), BF16)],
         compiler_params=PARAMS,
         cost_estimate=cost(5),
         name="cache",
-    )(owners, lengths, page_table, kept, new_query, new_cache)
-
+    )(owners, lengths, page_table, new_query, new_cache, crossed, *kept)
+
+    fin_got, cache_pool = lax.optimization_barrier((fin_got, cache_pool))
     prefill_out, decode_mixer = pl.pallas_call(
         final_kernel,
         out_shape=(

time: 55 us -> 53 us (0.964)
  starting transfers between devices: 16.4 us -> 24.8 us
  waiting for transfers between devices: 14.7 us -> 8.07 us
  Pallas kernels: 21.7 us -> 18.2 us
    ppermute x0 -> x8, starting transfers between devices: none -> 11.9 us  [the longest x7 11.9 us: local(): lax.ppermute(kept[m], 'tensor', [(i, i ^ m) for i in range(chips)])]
    all_to_all x1, waiting for transfers between devices: 8.6 us -> 2.28 us  [local(): recv = lax.all_to_all(send, AXES, split_axis=0, concat_axis=0, tiled=True)]
    pallas_call x1, Pallas kernels: 9.8 us -> 5.18 us  [local(): pl.pallas_call(main_kernel, grid=(1,), out_shape=(jax.ShapeDtypeStruct((p...]
    all_to_all x1 -> x0, starting transfers between devices: 3.71 us -> none  [local(): kept = lax.all_to_all(kept, AXES, split_axis=0, concat_axis=0, tiled=True)]
    ppermute x0 -> x8, waiting for transfers between devices: none -> 2.35 us  [the longest x7 2.35 us: local(): lax.ppermute(kept[m], 'tensor', [(i, i ^ m) for i in range(chips)])]
    ppermute x1, waiting for transfers between devices: 1.34 us -> 0.01 us  [local(): other = lax.ppermute(mine, 'side', [(0, 1), (1, 0)])]
    pallas_call x1 -> x3, Pallas kernels: 1.83 us -> 3.17 us  [the longest x1 2.34 us: local(): pl.pallas_call(before_kernel, out_shape=(jax.ShapeDtypeStruct((prompts, s...]
    all_to_all x1 -> x0, waiting for transfers between devices: 1.31 us -> none  [local(): kept = lax.all_to_all(kept, AXES, split_axis=0, concat_axis=0, tiled=True)]
  transfers between devices with their start and end apart: 4 -> 11, of which waited for: 4 -> 4; matrix products, arithmetic and copies ran while one was open for 0% -> 0% of each run, Pallas kernels for 32% -> 24%
where the time goes in v3:
time: 53 us; the launch traced here: 52.7 us
  starting transfers between devices  24.8 us (47%)
  Pallas kernels  18.2 us (34%)
  waiting for transfers between devices  8.07 us (15%)
  between operations  0.88 us (2%)
  local copies, waits for them, and re-layouts  0.72 us (1%)
    ppermute x7, starting transfers between devices, local(): lax.ppermute(kept[m], 'tensor', [(i, i ^ m) for i in range(chips)])  11.9 us
    all_to_all x1, starting transfers between devices, local(): recv = lax.all_to_all(send, AXES, split_axis=0, concat_axis=0, tiled=True)  7.53 us
    all_to_all x1, starting transfers between devices, local(): fin_got = lax.all_to_all(fin, AXES, split_axis=0, concat_axis=0, tiled=True)  5.27 us
    pallas_call x1, Pallas kernels, local(): pl.pallas_call(main_kernel, grid=(1,), out_shape=(jax.ShapeDtypeStruct((p...  5.18 us
    pallas_call x1, Pallas kernels, local(): pl.pallas_call(cache_kernel, out_shape=(jax.ShapeDtypeStruct((page_table....  4.43 us
    all_to_all x1, waiting for transfers between devices, local(): fin_got = lax.all_to_all(fin, AXES, split_axis=0, concat_axis=0, tiled=True)  3.44 us
    ppermute x7, waiting for transfers between devices, local(): lax.ppermute(kept[m], 'tensor', [(i, i ^ m) for i in range(chips)])  2.35 us
    pallas_call x1, Pallas kernels, local(): pl.pallas_call(before_kernel, out_shape=(jax.ShapeDtypeStruct((prompts, s...  2.34 us
  transfers between devices with their start and end apart: 11, of which 4 were waited for; matrix products, arithmetic and copies ran while one was open for 0% of the time, Pallas kernels for 24%

profile of v3, /device:TPU:0, one launch (start us, length us, event | category | flops | bytes accessed | tf_op | source)
XLA Modules:
  0.0 52.7 jit_solution(12199131552164258565)
XLA Ops:
  0.6 0.0 copy-start.2
  0.6 2.1 %pack.1 = bf16[16,80,128]{2,1,0:T(8,128)(2,1)} custom-call(bf16[1,64,2048]{2,1,0:T(8,128)(2,1)} %coeff.2, bf16[2,2,4096]{2,1,0:T(2,128)(2,1)} %hidden_in.1, bf16[2,2,2048]{2,1,0:T(2,128)(2,1)} %coeff_new_in.1, f32[2,2,64]{2,1,0:T(2,128)} %step_in.1), custom_call_target="tpu_custom_call" | custom-call | tf_op jit(solution)/shard_map/pack/pallas_call | solution.py:557
  2.8 0.0 copy-start
  2.8 7.5 %all-to-all-start = ((bf16[16,80,128]{2,1,0:T(8,128)(2,1)}), bf16[16,80,128]{2,1,0:T(8,128)(2,1)S(1)}, u32[]{:S(2)}, u32[]{:S(2)}) async-start(bf16[16,80,128]{2,1,0:T(8,128)(2,1)} %pack.1), calls=%async_computation | async-start | bytes 655360 | tf_op jit(solution)/shard_map/all_to_all | solution.py:570
  10.3 0.0 copy-start.10
  10.3 0.0 copy-done.2
  10.4 0.6 %copy-done.10 = s32[16,1]{0,1:T(1,128)S(1)} copy-done((s32[16,1]{0,1:T(1,128)S(1)}, s32[16,1]{0,1:T(1,128)}, u32[]{:S(2)}) %copy-start.10) | copy-done | bytes 88
  11.0 0.8 %pack_cache.1 = (bf16[2,128,128]{2,1,0:T(8,128)(2,1)S(1)}, bf16[2,128,128]{2,1,0:T(8,128)(2,1)S(1)}, bf16[2,128,128]{2,1,0:T(8,128)(2,1)S(1)}, bf16[2,128,128]{2...) custom-call(s32[16]{0:T(128)S(1)} %bitcast.3, ...), custom_call_target="tpu_custom_call" | custom-call | bytes 10500000 | tf_op jit(solution)/shard_map/pack_cache/pallas_call | solution.py:572
  11.8 0.0 copy-start.14
  11.8 0.0 copy-start.11
  11.8 0.0 copy-start.12
  11.8 0.0 copy-start.13
  11.9 2.0 %collective-permute-start = (bf16[2,128,128]{2,1,0:T(8,128)(2,1)S(1)}, bf16[2,128,128]{2,1,0:T(8,128)(2,1)S(1)}, u32[]{:S(2)}, u32[]{:S(2)}) collective-permute-start(bf16[2,128,128]{2,1,0:T(8,128)(2,1)S(1)} %get-tuple-element.39), channel_id=1, source_target_pairs={{0,2},{2,0},{4,6},{6,4},{8,10},{10,8},{12,14},{14,12},{1,3},{3,1},... | collective-permute-start | bytes 196616 | tf_op jit(solution)/shard_map/ppermute | solution.py:583
  13.9 1.5 %collective-permute-start.1 = (bf16[2,128,128]{2,1,0:T(8,128)(2,1)S(1)}, bf16[2,128,128]{2,1,0:T(8,128)(2,1)S(1)}, u32[]{:S(2)}, u32[]{:S(2)}) collective-permute-start(bf16[2,128,128]{2,1,0:T(8,128)(2,1)S(1)} %get-tuple-element.40), channel_id=1, source_target_pairs={{0,4},{2,6},{4,0},{6,2},{8,12},{10,14},{12,8},{14,10},{1,5},{3,7},... | collective-permute-start | bytes 196616 | tf_op jit(solution)/shard_map/ppermute | solution.py:583
  15.4 2.3 %before.1 = (bf16[16,64,256]{2,1,0:T(8,128)(2,1)S(1)}, f32[3,16,256]{2,1,0:T(8,128)S(1)}, f32[8,256]{1,0:T(8,128)S(1)}, f32[4,16,128]{2,1,0:T(8,128)S(1)}, f32[4,16,128]{2,1,0:T(8,128)S(1)}) custom-call(s32[16]{0:T(128)S(1)} %copy-done.11, f32[64]{0:T(128)S(1)} %copy-done.12, f32[64]{0:T(128)S(1)} %copy-done.13, f32[64]{0:T(128)S(1)} %copy-done.14, ...), custom_call_target="tpu_custom_call" | custom-call | bytes 14000000 | tf_op jit(solution)/shard_map/before/pallas_call | solution.py:586
  17.7 0.0 collective-permute-done.refs_1_
  17.7 1.9 %collective-permute-done.1.refs_2_ = bf16[2,128,128]{2,1,0:T(8,128)(2,1)S(1)} collective-permute-done((bf16[2,128,128]{2,1,0:T(8,128)(2,1)S(1)}, bf16[2,128,128]{2,1,0:T(8,128)(2,1)S(1)}, u32[]{:S(2)}, u32[]{:S(2)}) %collective-permute-start.1) | collective-permute-done | bytes 65568 | tf_op jit(solution)/shard_map/ppermute | solution.py:583
  19.6 2.3 %all-to-all-done.recv.new_ref = bf16[16,80,128]{2,1,0:T(8,128)(2,1)S(1)} async-done(((bf16[16,80,128]{2,1,0:T(8,128)(2,1)}), bf16[16,80,128]{2,1,0:T(8,128)(2,1)S(1)}, u32[]{:S(2)}, u32[]{:S(2)}) %all-to-all-start) | async-done | bytes 327712 | tf_op jit(solution)/shard_map/all_to_all | solution.py:570
  21.9 0.0 copy-done.9
  21.9 1.4 %coeff.3.mine = bf16[16,80,128]{2,1,0:T(8,128)(2,1)S(1)} custom-call(s32[16]{0:T(128)S(1)} %bitcast.4, s32[16]{0:T(128)S(1)} %copy-done.11, bf16[4,2048]{1,0:T(4,128)(2,1)S(1)} %copy-done.9, bf16[16,80,128]{2,1,0:T(8,128)(2,1)S(1)} %all-to-all-done.recv.new_ref), custom_call_target="tpu_custom_call" | custom-call | bytes 7000000 | tf_op jit(solution)/shard_map/coeff/pallas_call | solution.py:609
  23.3 0.1 collective-permute-start.2
  23.4 0.8 %collective-permute-start.3 = (bf16[2,128,128]{2,1,0:T(8,128)(2,1)S(1)}, bf16[2,128,128]{2,1,0:T(8,128)(2,1)S(1)}, u32[]{:S(2)}, u32[]{:S(2)}) collective-permute-start(bf16[2,128,128]{2,1,0:T(8,128)(2,1)S(1)} %get-tuple-element.51), channel_id=1, source_target_pairs={{0,6},{2,4},{4,2},{6,0},{8,14},{10,12},{12,10},{14,8},{1,7},{3,5},... | collective-permute-start | bytes 196616 | tf_op jit(solution)/shard_map/ppermute | solution.py:583
  24.1 1.5 %collective-permute-start.4 = (bf16[2,128,128]{2,1,0:T(8,128)(2,1)S(1)}, bf16[2,128,128]{2,1,0:T(8,128)(2,1)S(1)}, u32[]{:S(2)}, u32[]{:S(2)}) collective-permute-start(bf16[2,128,128]{2,1,0:T(8,128)(2,1)S(1)} %get-tuple-element.52), channel_id=1, source_target_pairs={{0,8},{2,10},{4,12},{6,14},{8,0},{10,2},{12,4},{14,6},{1,9},{3,11}... | collective-permute-start | bytes 196616 | tf_op jit(solution)/shard_map/ppermute | solution.py:583
  25.7 2.1 %collective-permute-start.5 = (bf16[2,128,128]{2,1,0:T(8,128)(2,1)S(1)}, bf16[2,128,128]{2,1,0:T(8,128)(2,1)S(1)}, u32[]{:S(2)}, u32[]{:S(2)}) collective-permute-start(bf16[2,128,128]{2,1,0:T(8,128)(2,1)S(1)} %get-tuple-element.53), channel_id=1, source_target_pairs={{0,10},{2,8},{4,14},{6,12},{8,2},{10,0},{12,6},{14,4},{1,11},{3,9}... | collective-permute-start | bytes 196616 | tf_op jit(solution)/shard_map/ppermute | solution.py:583
  27.8 1.9 %collective-permute-start.6 = (bf16[2,128,128]{2,1,0:T(8,128)(2,1)S(1)}, bf16[2,128,128]{2,1,0:T(8,128)(2,1)S(1)}, u32[]{:S(2)}, u32[]{:S(2)}) collective-permute-start(bf16[2,128,128]{2,1,0:T(8,128)(2,1)S(1)} %get-tuple-element.54), channel_id=1, source_target_pairs={{0,12},{2,14},{4,8},{6,10},{8,4},{10,6},{12,0},{14,2},{1,13},{3,15... | collective-permute-start | bytes 196616 | tf_op jit(solution)/shard_map/ppermute | solution.py:583
  29.7 0.0 collective-permute-done.2.other
  29.7 2.1 %collective-permute-start.7 = (bf16[2,128,128]{2,1,0:T(8,128)(2,1)S(1)}, bf16[2,128,128]{2,1,0:T(8,128)(2,1)S(1)}, u32[]{:S(2)}, u32[]{:S(2)}) collective-permute-start(bf16[2,128,128]{2,1,0:T(8,128)(2,1)S(1)} %get-tuple-element.55), channel_id=1, source_target_pairs={{0,14},{2,12},{4,10},{6,8},{8,6},{10,4},{12,2},{14,0},{1,15},{3,13... | collective-permute-start | bytes 196616 | tf_op jit(solution)/shard_map/ppermute | solution.py:583
  31.8 5.2 %main.1 = (f32[16,64,256]{2,1,0:T(8,128)S(1)}, f32[16,16,128]{2,1,0:T(8,128)}) custom-call(s32[16]{0:T(128)S(1)} %bitcast.5, s32[16]{0:T(128)S(1)} %copy-done.11, bf16[4,4096]{1,0:T(4,128)(2,1)S(1)} %copy-done.3, bf16[16,80,128]{2,1,0:T(8,128)(2,1)S(1)} %coeff.3.mine, bf16[16,80,128]{2,1,0:T(8,128)(2,1)S(1)} %collective-permute-done.2.other, ...), custom_call_target="tpu_custom_call" | custom-call | bytes 35000000 | tf_op jit(solution)/shard_map/main/pallas_call | solution.py:628
  37.0 0.0 collective-permute-done.3.refs_3_
  37.0 0.0 collective-permute-done.4.refs_4_
  37.0 0.4 collective-permute-done.5.refs_5_
  37.4 0.0 collective-permute-done.6.refs_6_
  37.4 0.0 collective-permute-done.7.refs_7_
  37.5 0.0 copy-start.4
  37.5 0.0 copy-start.8
  37.5 0.0 copy-start.15
  37.5 0.1 collective-permute-start.8
  37.6 5.3 %all-to-all-start.1 = ((f32[16,16,128]{2,1,0:T(8,128)}), f32[16,16,128]{2,1,0:T(8,128)S(1)}, u32[]{:S(2)}, u32[]{:S(2)}) async-start(f32[16,16,128]{2,1,0:T(8,128)} %get-tuple-element.56), calls=%async_computation.1 | async-start | bytes 262144 | tf_op jit(solution)/shard_map/all_to_all | solution.py:672
  42.8 0.0 copy-start.6
  42.9 0.0 collective-permute-done.8.crossed
  42.9 0.0 copy-done.4
  42.9 0.0 copy-done.8
  42.9 0.0 copy-done.15
  42.9 0.0 copy-start.7
  42.9 4.4 %cache.3 = (bf16[8,16,2048]{2,1,0:T(8,128)(2,1)}, bf16[2,2,8192]{2,1,0:T(2,128)(2,1)}) custom-call(s32[16]{0:T(128)S(1)} %bitcast.6, s32[16]{0:T(128)S(1)} %copy-done.11, s32[1,8]{1,0:T(1,128)S(1)} %copy-done.15, bf16[2,2,8192]{2,1,0:T(2,128)(2,1)S(1)} %copy-done.4, bf16[2,2,2048]{2,1,0:T(2,128)(2,1)S(1)} %copy-done.8, ...), custom_call_target="tpu_custom_call" | custom-call | bytes 17500000 | tf_op jit(solution)/shard_map/cache/pallas_call | solution.py:674
  47.3 3.4 %all-to-all-done.1.fin = f32[16,16,128]{2,1,0:T(8,128)S(1)} async-done(((f32[16,16,128]{2,1,0:T(8,128)}), f32[16,16,128]{2,1,0:T(8,128)S(1)}, u32[]{:S(2)}, u32[]{:S(2)}) %all-to-all-start.1) | async-done | bytes 131104 | tf_op jit(solution)/shard_map/all_to_all | solution.py:672
  50.8 0.0 copy-done.6
  50.8 1.9 %final.1 = (bf16[16,64,256]{2,1,0:T(8,128)(2,1)}, bf16[2,2,4096]{2,1,0:T(2,128)(2,1)}) custom-call(s32[16]{0:T(128)S(1)} %bitcast.7, s32[16]{0:T(128)S(1)} %copy-done.11, f32[1,4096]{1,0:T(1,128)S(1)} %bitcast.2, f32[16,16,128]{2,1,0:T(8,128)S(1)} %all-to-all-done.1.fin, f32[16,64,256]{2,1,0:T(8,128)S(1)} %get-tuple-element.67.gated, ...), custom_call_target="tpu_custom_call" | custom-call | tf_op jit(solution)/shard_map/final/pallas_call | solution.py:689
  (14 shorter events, 0.0 us)
Async XLA Ops:
  0.6 9.7 %copy-start.2 = (bf16[16,4,2048]{2,1,0:T(4,128)(2,1)S(1)}, bf16[16,4,2048]{2,1,0:T(4,128)(2,1)}, u32[]{:S(2)}) copy-start(bf16[16,4,2048]{2,1,0:T(4,128)(2,1)} %cache.2) | copy-start | bytes 786436
  2.8 12.5 %copy-start = (bf16[16,64,256]{2,1,0:T(8,128)(2,1)S(1)}, bf16[16,64,256]{2,1,0:T(8,128)(2,1)}, u32[]{:S(2)}) copy-start(bf16[16,64,256]{2,1,0:T(8,128)(2,1)} %hidden.1) | copy-start | bytes 1572868
  2.8 19.1 %all-to-all-start = ((bf16[16,80,128]{2,1,0:T(8,128)(2,1)}), bf16[16,80,128]{2,1,0:T(8,128)(2,1)S(1)}, u32[]{:S(2)}, u32[]{:S(2)}) async-start(bf16[16,80,128]{2,1,0:T(8,128)(2,1)} %pack.1), calls=%async_computation | async-start | bytes 655360 | tf_op jit(solution)/shard_map/all_to_all | solution.py:570
  10.3 0.7 %copy-start.10 = (s32[16,1]{0,1:T(1,128)S(1)}, s32[16,1]{0,1:T(1,128)}, u32[]{:S(2)}) copy-start(s32[16,1]{0,1:T(1,128)} %param.26) | copy-start | bytes 196
  11.0 4.3 %copy-start.3 = (bf16[4,4096]{1,0:T(4,128)(2,1)S(1)}, bf16[4,4096]{1,0:T(4,128)(2,1)}, u32[]{:S(2)}) copy-start(bf16[4,4096]{1,0:T(4,128)(2,1)} %taps_ref.5) | copy-start | bytes 98308
  11.0 4.3 %copy-start.5 = (f32[4,16,64]{2,1,0:T(8,128)S(1)}, f32[4,16,64]{2,1,0:T(8,128)}, u32[]{:S(2)}) copy-start(f32[4,16,64]{2,1,0:T(8,128)} %step.1) | copy-start | bytes 49156
  11.8 3.5 %copy-start.14 = (f32[64]{0:T(128)S(1)}, f32[64]{0:T(128)}, u32[]{:S(2)}) copy-start(f32[64]{0:T(128)} %skip.1) | copy-start | bytes 772
  11.8 3.5 %copy-start.11 = (s32[16]{0:T(128)S(1)}, s32[16]{0:T(128)}, u32[]{:S(2)}) copy-start(s32[16]{0:T(128)} %lengths.9) | copy-start | bytes 196
  11.8 3.5 %copy-start.12 = (f32[64]{0:T(128)S(1)}, f32[64]{0:T(128)}, u32[]{:S(2)}) copy-start(f32[64]{0:T(128)} %bias.1) | copy-start | bytes 772
  11.8 3.5 %copy-start.13 = (f32[64]{0:T(128)S(1)}, f32[64]{0:T(128)}, u32[]{:S(2)}) copy-start(f32[64]{0:T(128)} %decay.1) | copy-start | bytes 772
  11.9 5.9 %collective-permute-start = (bf16[2,128,128]{2,1,0:T(8,128)(2,1)S(1)}, bf16[2,128,128]{2,1,0:T(8,128)(2,1)S(1)}, u32[]{:S(2)}, u32[]{:S(2)}) collective-permute-start(bf16[2,128,128]{2,1,0:T(8,128)(2,1)S(1)} %get-tuple-element.39), channel_id=1, source_target_pairs={{0,2},{2,0},{4,6},{6,4},{8,10},{10,8},{12,14},{14,12},{1,3},{3,1},... | collective-permute-start | bytes 196616 | tf_op jit(solution)/shard_map/ppermute | solution.py:583
  13.8 8.1 %copy-start.9 = (bf16[4,2048]{1,0:T(4,128)(2,1)S(1)}, bf16[4,2048]{1,0:T(4,128)(2,1)}, u32[]{:S(2)}) copy-start(bf16[4,2048]{1,0:T(4,128)(2,1)} %taps_ref.4) | copy-start | bytes 49156
  13.9 18.0 %copy-start.1 = (bf16[16,64,256]{2,1,0:T(8,128)(2,1)S(1)}, bf16[16,64,256]{2,1,0:T(8,128)(2,1)}, u32[]{:S(2)}) copy-start(bf16[16,64,256]{2,1,0:T(8,128)(2,1)} %gate.1) | copy-start | bytes 1572868
  13.9 5.8 %collective-permute-start.1 = (bf16[2,128,128]{2,1,0:T(8,128)(2,1)S(1)}, bf16[2,128,128]{2,1,0:T(8,128)(2,1)S(1)}, u32[]{:S(2)}, u32[]{:S(2)}) collective-permute-start(bf16[2,128,128]{2,1,0:T(8,128)(2,1)S(1)} %get-tuple-element.40), channel_id=1, source_target_pairs={{0,4},{2,6},{4,0},{6,2},{8,12},{10,14},{12,8},{14,10},{1,5},{3,7},... | collective-permute-start | bytes 196616 | tf_op jit(solution)/shard_map/ppermute | solution.py:583
  23.3 6.4 %collective-permute-start.2 = (bf16[16,80,128]{2,1,0:T(8,128)(2,1)S(1)}, bf16[16,80,128]{2,1,0:T(8,128)(2,1)S(1)}, u32[]{:S(2)}, u32[]{:S(2)}) collective-permute-start(bf16[16,80,128]{2,1,0:T(8,128)(2,1)S(1)} %coeff.3.mine), channel_id=1, source_target_pairs={{0,1},{1,0},{2,3},{3,2},{4,5},{5,4},{6,7},{7,6},{8,9},{9,8},{10,11... | collective-permute-start | bytes 983048 | tf_op jit(solution)/shard_map/ppermute | solution.py:625
  23.4 13.6 %collective-permute-start.3 = (bf16[2,128,128]{2,1,0:T(8,128)(2,1)S(1)}, bf16[2,128,128]{2,1,0:T(8,128)(2,1)S(1)}, u32[]{:S(2)}, u32[]{:S(2)}) collective-permute-start(bf16[2,128,128]{2,1,0:T(8,128)(2,1)S(1)} %get-tuple-element.51), channel_id=1, source_target_pairs={{0,6},{2,4},{4,2},{6,0},{8,14},{10,12},{12,10},{14,8},{1,7},{3,5},... | collective-permute-start | bytes 196616 | tf_op jit(solution)/shard_map/ppermute | solution.py:583
  24.1 12.8 %collective-permute-start.4 = (bf16[2,128,128]{2,1,0:T(8,128)(2,1)S(1)}, bf16[2,128,128]{2,1,0:T(8,128)(2,1)S(1)}, u32[]{:S(2)}, u32[]{:S(2)}) collective-permute-start(bf16[2,128,128]{2,1,0:T(8,128)(2,1)S(1)} %get-tuple-element.52), channel_id=1, source_target_pairs={{0,8},{2,10},{4,12},{6,14},{8,0},{10,2},{12,4},{14,6},{1,9},{3,11}... | collective-permute-start | bytes 196616 | tf_op jit(solution)/shard_map/ppermute | solution.py:583
  25.7 11.8 %collective-permute-start.5 = (bf16[2,128,128]{2,1,0:T(8,128)(2,1)S(1)}, bf16[2,128,128]{2,1,0:T(8,128)(2,1)S(1)}, u32[]{:S(2)}, u32[]{:S(2)}) collective-permute-start(bf16[2,128,128]{2,1,0:T(8,128)(2,1)S(1)} %get-tuple-element.53), channel_id=1, source_target_pairs={{0,10},{2,8},{4,14},{6,12},{8,2},{10,0},{12,6},{14,4},{1,11},{3,9}... | collective-permute-start | bytes 196616 | tf_op jit(solution)/shard_map/ppermute | solution.py:583
  27.8 9.7 %collective-permute-start.6 = (bf16[2,128,128]{2,1,0:T(8,128)(2,1)S(1)}, bf16[2,128,128]{2,1,0:T(8,128)(2,1)S(1)}, u32[]{:S(2)}, u32[]{:S(2)}) collective-permute-start(bf16[2,128,128]{2,1,0:T(8,128)(2,1)S(1)} %get-tuple-element.54), channel_id=1, source_target_pairs={{0,12},{2,14},{4,8},{6,10},{8,4},{10,6},{12,0},{14,2},{1,13},{3,15... | collective-permute-start | bytes 196616 | tf_op jit(solution)/shard_map/ppermute | solution.py:583
  29.7 7.7 %collective-permute-start.7 = (bf16[2,128,128]{2,1,0:T(8,128)(2,1)S(1)}, bf16[2,128,128]{2,1,0:T(8,128)(2,1)S(1)}, u32[]{:S(2)}, u32[]{:S(2)}) collective-permute-start(bf16[2,128,128]{2,1,0:T(8,128)(2,1)S(1)} %get-tuple-element.55), channel_id=1, source_target_pairs={{0,14},{2,12},{4,10},{6,8},{8,6},{10,4},{12,2},{14,0},{1,15},{3,13... | collective-permute-start | bytes 196616 | tf_op jit(solution)/shard_map/ppermute | solution.py:583
  37.5 5.4 %copy-start.4 = (bf16[2,2,8192]{2,1,0:T(2,128)(2,1)S(1)}, bf16[2,2,8192]{2,1,0:T(2,128)(2,1)}, u32[]{:S(2)}) copy-start(bf16[2,2,8192]{2,1,0:T(2,128)(2,1)} %query.1) | copy-start | bytes 196612
  37.5 5.4 %copy-start.8 = (bf16[2,2,2048]{2,1,0:T(2,128)(2,1)S(1)}, bf16[2,2,2048]{2,1,0:T(2,128)(2,1)}, u32[]{:S(2)}) copy-start(bf16[2,2,2048]{2,1,0:T(2,128)(2,1)} %cache_new.1) | copy-start | bytes 49156
  37.5 5.4 %copy-start.15 = (s32[1,8]{1,0:T(1,128)S(1)}, s32[1,8]{1,0:T(1,128)}, u32[]{:S(2)}) copy-start(s32[1,8]{1,0:T(1,128)} %pages.1) | copy-start | bytes 100
  37.5 5.4 %collective-permute-start.8 = (bf16[8,128,128]{2,1,0:T(8,128)(2,1)S(1)}, bf16[8,128,128]{2,1,0:T(8,128)(2,1)S(1)}, u32[]{:S(2)}, u32[]{:S(2)}) collective-permute-start(bf16[8,128,128]{2,1,0:T(8,128)(2,1)S(1)} %stack.1), channel_id=1, source_target_pairs={{0,1},{1,0},{2,3},{3,2},{4,5},{5,4},{6,7},{7,6},{8,9},{9,8},{10,11... | collective-permute-start | bytes 786440 | tf_op jit(solution)/shard_map/ppermute | solution.py:671
  37.6 13.2 %all-to-all-start.1 = ((f32[16,16,128]{2,1,0:T(8,128)}), f32[16,16,128]{2,1,0:T(8,128)S(1)}, u32[]{:S(2)}, u32[]{:S(2)}) async-start(f32[16,16,128]{2,1,0:T(8,128)} %get-tuple-element.56), calls=%async_computation.1 | async-start | bytes 262144 | tf_op jit(solution)/shard_map/all_to_all | solution.py:672
  42.8 7.9 %copy-start.6 = (bf16[2,2,4096]{2,1,0:T(2,128)(2,1)S(1)}, bf16[2,2,4096]{2,1,0:T(2,128)(2,1)}, u32[]{:S(2)}) copy-start(bf16[2,2,4096]{2,1,0:T(2,128)(2,1)} %new_gate.1) | copy-start | bytes 98308
  42.9 7.9 %copy-start.7 = (f32[4096]{0:T(1024)S(1)}, f32[4096]{0:T(1024)}, u32[]{:S(2)}) copy-start(f32[4096]{0:T(1024)} %param.33) | copy-start | bytes 49156

commit v4 on v3

--- a/solution.py
+++ b/solution.py
@@ -30,6 +30,14 @@
 
 def iota(shape, dim):
     return lax.broadcasted_iota(jnp.int32, shape, dim)
+
+
+def div(x, n):
+    return x >> (n.bit_length() - 1) if n & (n - 1) == 0 else x // n
+
+
+def mod(x, n):
+    return x & (n - 1) if n & (n - 1) == 0 else lax.rem(x, n)
 
 
 def softplus(x):
@@ -265,6 +273,7 @@
     dt_given,
     sum_given,
     gated_ref,
+    fin_out,
     fin,
     count,
     rank_ref,
@@ -321,7 +330,7 @@
         )
 
     gain = consts[0:1, :]
-    heads_wide = iota((ROWS, columns), 1) // head_size
+    heads_wide = div(iota((ROWS, columns), 1), head_size)
     place = iota((ROWS, columns), 0)
     lower = iota((ROWS, ROWS), 0) >= iota((ROWS, ROWS), 1)
     column_of = iota((span, LANES), 1)
@@ -357,7 +366,7 @@
         for i in range(2):
             row = jnp.sum(jnp.where(place == length + i, out, 0.0), axis=0, keepdims=True)
             for half in range(2):
-                fin[owner, pl.ds(prompts // 2 + 4 * half + 2 * rank + i, 1), :] = row[
+                fin[owner, pl.ds(4 * half + 2 * rank + i, 1), :] = row[
                     :, half * LANES : (half + 1) * LANES
                 ]
         gated = out[:span] * silu(gate[r].astype(F32))
@@ -370,8 +379,11 @@
     half = prompts // 2
     packed = jnp.concatenate([turned[0:half, :], turned[half:prompts, :]], axis=1)
 
+    high = packed.astype(BF16).astype(F32)
+    split = (high, packed - high)
+
     def spread(d, carry):
-        fin[d, 0:half, :] = packed
+        fin_out[d] = jnp.concatenate([*split, fin[d]], axis=0).astype(BF16)
         return carry
 
     lax.fori_loop(0, fin.shape[0], spread, 0, unroll=4)
@@ -389,7 +401,7 @@
         return (*lens, seen + is_mine.astype(jnp.int32))
 
     zero = jnp.int32(0)
-    return lax.fori_loop(0, owners.shape[0], one, (zero,) * (slots + 1))[:slots]
+    return lax.fori_loop(0, owners.shape[0], one, (zero,) * (slots + 1), unroll=8)[:slots]
 
 
 def cache_kernel(owners, lengths, pages, query, cache_new, crossed, *refs):
@@ -405,34 +417,29 @@
     local = each // slots
     lens = slot_facts(owners, lengths, slots)
     keys = sources * each
-    row = iota((slots * span, keys), 0)
-    key = iota((slots * span, keys), 1)
-    slot_of = row // span
-    at = lax.rem(row, span)
-    apart = (at // local) ^ lax.axis_index(AXES)
-    wanted = (lax.rem(apart, 2) * chips + apart // 2) * each + slot_of * local + lax.rem(at, local)
-    limit = jnp.where(slot_of == 0, lens[0], lens[1])
-    order = jnp.where((key == wanted) & (at < limit), 1.0, 0.0).astype(BF16)
+    key = iota((1, keys), 1)
+    block_of = div(key, each)
+    apart = mod(block_of, chips) * 2 + div(block_of, chips)
+    slot_of = div(mod(key, each), local)
+    at = (apart ^ lax.axis_index(AXES)) * local + mod(key, local)
+    wanted = jnp.where(at < jnp.where(slot_of == 0, lens[0], lens[1]), slot_of * span + at, -1)
+    order = jnp.where(iota((slots * span, keys), 0) == wanted, 1.0, 0.0).astype(BF16)
     ask = jnp.concatenate([query[k].astype(F32) for k in range(slots)], axis=0)
     fresh = jnp.concatenate([cache_new[k].astype(F32) for k in range(slots)], axis=0)
     fresh = jnp.concatenate([fresh, jnp.zeros_like(fresh)], axis=0)
     per = query.shape[2] // (KVH * KVD)
     pairs = slots * steps
     count = per * pairs
-    ask_slot = lax.rem(iota((count, slots * span), 0), pairs) // steps
-    ask_step = lax.rem(iota((count, slots * span), 0), steps)
-    key_slot = iota((count, slots * span), 1) // span
-    key_at = lax.rem(iota((count, slots * span), 1), span)
-    live = (key_slot == ask_slot) & (key_at < jnp.where(ask_slot == 0, lens[0], lens[1]))
-    new_row = iota((count, 2 * pairs), 0)
-    new_key = iota((count, 2 * pairs), 1)
-    new_live = (
-        (new_key < pairs)
-        & (new_key // steps == lax.rem(new_row, pairs) // steps)
-        & (lax.rem(new_key, steps) <= lax.rem(new_row, steps))
+    row = iota((count, 1), 0)
+    ask_slot, ask_step = div(mod(row, pairs), steps), mod(row, steps)
+    key = iota((1, slots * span), 1)
+    is_live = mod(key, span) < jnp.where(div(key, span) == 0, lens[0], lens[1])
+    live = ask_slot == jnp.where(is_live, div(key, span), -1)
+    key = iota((1, 2 * pairs), 1)
+    new_live = (ask_slot == jnp.where(key < pairs, div(key, steps), -1)) & (
+        mod(key, steps) <= ask_step
     )
-    out_slot = lax.rem(iota((count, KVD), 0), pairs) // steps
-    filled = jnp.where(out_slot == 0, lens[0], lens[1]) > 0
+    filled = jnp.where(ask_slot == 0, lens[0], lens[1]) > 0
 
     for c in range(parts):
         strip = slice(c * each, (c + 1) * each)
@@ -492,9 +499,8 @@
     width = new_gate.shape[2]
     half = prompts // 2
     me = lax.axis_index(AXES)
-    total = fin[0, 0:half, :]
-    for s in range(1, sources):
-        total = total + fin[s, 0:half, :]
+    blocks = [fin[s].astype(F32) for s in range(sources)]
+    total = sum(x[half : 2 * half] for x in blocks) + sum(x[0:half] for x in blocks)
     scale = lax.rsqrt(total / width + EPS).T
     gain = gain_ref[:, pl.ds(pl.multiple_of(me * columns, LANES), columns)]
     place = iota((span, columns), 0)
@@ -506,8 +512,8 @@
     lens = slot_facts(owners, lengths, slots)
     read = jnp.concatenate(
         [
-            fin[s, half + pairs : half + pairs + 4, :]
-            for s in range(sources)
+            block[2 * half + pairs : 2 * half + pairs + 4]
+            for block in blocks
             for pairs in (0, 4)
         ],
         axis=1,
@@ -516,7 +522,7 @@
     out = read * silu(gates)
     mean = jnp.mean(out * out, axis=1, keepdims=True)
     out = out * lax.rsqrt(mean + EPS) * gain_ref[...]
-    slot_of = iota(out.shape, 0) // steps
+    slot_of = div(iota((out.shape[0], 1), 0), steps)
     out = jnp.where(jnp.where(slot_of == 0, lens[0], lens[1]) > 0, out, 0.0)
     for k in range(slots):
         mixer[k] = out[k * steps : (k + 1) * steps].astype(BF16)
@@ -630,7 +636,7 @@
         grid=(1,),
         out_shape=(
             jax.ShapeDtypeStruct((prompts, span, columns), F32),
-            jax.ShapeDtypeStruct((devices, prompts // 2 + 8, LANES), F32),
+            jax.ShapeDtypeStruct((devices, prompts + 8, LANES), BF16),
         ),
         in_specs=[SMEM] * 2
         + [VMEM] * 3
@@ -638,6 +644,7 @@
         + [VMEM] * 6,
         out_specs=(VMEM, VMEM),
         scratch_shapes=[
+            pltpu.VMEM((devices, 8, LANES), F32),
             per_owner,
             per_prompt,
             pltpu.VMEM((2, prompts, LANES), F32),

time: 53 us -> 52.4 us (0.989)
  no operation moved by 1% of the time
where the time goes in v4:
time: 52.4 us; the launch traced here: 52 us
  starting transfers between devices  24.8 us (47%)
  Pallas kernels  17.9 us (34%)
  waiting for transfers between devices  7.68 us (15%)
  between operations  0.88 us (2%)
  local copies, waits for them, and re-layouts  0.72 us (1%)
    ppermute x7, starting transfers between devices, local(): lax.ppermute(kept[m], 'tensor', [(i, i ^ m) for i in range(chips)])  11.9 us
    all_to_all x1, starting transfers between devices, local(): recv = lax.all_to_all(send, AXES, split_axis=0, concat_axis=0, tiled=True)  7.53 us
    all_to_all x1, starting transfers between devices, local(): fin_got = lax.all_to_all(fin, AXES, split_axis=0, concat_axis=0, tiled=True)  5.27 us
    pallas_call x1, Pallas kernels, local(): pl.pallas_call(main_kernel, grid=(1,), out_shape=(jax.ShapeDtypeStruct((p...  5.16 us
    pallas_call x1, Pallas kernels, local(): pl.pallas_call(cache_kernel, out_shape=(jax.ShapeDtypeStruct((page_table....  4.32 us
    all_to_all x1, waiting for transfers between devices, local(): fin_got = lax.all_to_all(fin, AXES, split_axis=0, concat_axis=0, tiled=True)  3.03 us
    ppermute x7, waiting for transfers between devices, local(): lax.ppermute(kept[m], 'tensor', [(i, i ^ m) for i in range(chips)])  2.37 us
    pallas_call x1, Pallas kernels, local(): pl.pallas_call(before_kernel, out_shape=(jax.ShapeDtypeStruct((prompts, s...  2.34 us
  transfers between devices with their start and end apart: 11, of which 4 were waited for; matrix products, arithmetic and copies ran while one was open for 0% of the time, Pallas kernels for 24%

profile of v4, /device:TPU:0, one launch (start us, length us, event | category | flops | bytes accessed | tf_op | source)
XLA Modules:
  0.0 52.0 jit_solution(1932867477389301957)
XLA Ops:
  0.6 0.0 copy-start.2
  0.6 2.1 %pack.1 = bf16[16,80,128]{2,1,0:T(8,128)(2,1)} custom-call(bf16[1,64,2048]{2,1,0:T(8,128)(2,1)} %coeff.2, bf16[2,2,4096]{2,1,0:T(2,128)(2,1)} %hidden_in.1, bf16[2,2,2048]{2,1,0:T(2,128)(2,1)} %coeff_new_in.1, f32[2,2,64]{2,1,0:T(2,128)} %step_in.1), custom_call_target="tpu_custom_call" | custom-call | tf_op jit(solution)/shard_map/pack/pallas_call | solution.py:563
  2.8 0.0 copy-start
  2.8 7.5 %all-to-all-start = ((bf16[16,80,128]{2,1,0:T(8,128)(2,1)}), bf16[16,80,128]{2,1,0:T(8,128)(2,1)S(1)}, u32[]{:S(2)}, u32[]{:S(2)}) async-start(bf16[16,80,128]{2,1,0:T(8,128)(2,1)} %pack.1), calls=%async_computation | async-start | bytes 655360 | tf_op jit(solution)/shard_map/all_to_all | solution.py:576
  10.3 0.0 copy-start.10
  10.3 0.0 copy-done.2
  10.4 0.6 %copy-done.10 = s32[16,1]{0,1:T(1,128)S(1)} copy-done((s32[16,1]{0,1:T(1,128)S(1)}, s32[16,1]{0,1:T(1,128)}, u32[]{:S(2)}) %copy-start.10) | copy-done | bytes 88
  11.0 0.8 %pack_cache.1 = (bf16[2,128,128]{2,1,0:T(8,128)(2,1)S(1)}, bf16[2,128,128]{2,1,0:T(8,128)(2,1)S(1)}, bf16[2,128,128]{2,1,0:T(8,128)(2,1)S(1)}, bf16[2,128,128]{2...) custom-call(s32[16]{0:T(128)S(1)} %bitcast.3, ...), custom_call_target="tpu_custom_call" | custom-call | bytes 10500000 | tf_op jit(solution)/shard_map/pack_cache/pallas_call | solution.py:578
  11.8 0.0 copy-start.14
  11.8 0.0 copy-start.11
  11.8 0.0 copy-start.12
  11.8 0.0 copy-start.13
  11.9 2.0 %collective-permute-start = (bf16[2,128,128]{2,1,0:T(8,128)(2,1)S(1)}, bf16[2,128,128]{2,1,0:T(8,128)(2,1)S(1)}, u32[]{:S(2)}, u32[]{:S(2)}) collective-permute-start(bf16[2,128,128]{2,1,0:T(8,128)(2,1)S(1)} %get-tuple-element.39), channel_id=1, source_target_pairs={{0,2},{2,0},{4,6},{6,4},{8,10},{10,8},{12,14},{14,12},{1,3},{3,1},... | collective-permute-start | bytes 196616 | tf_op jit(solution)/shard_map/ppermute | solution.py:589
  13.9 1.5 %collective-permute-start.1 = (bf16[2,128,128]{2,1,0:T(8,128)(2,1)S(1)}, bf16[2,128,128]{2,1,0:T(8,128)(2,1)S(1)}, u32[]{:S(2)}, u32[]{:S(2)}) collective-permute-start(bf16[2,128,128]{2,1,0:T(8,128)(2,1)S(1)} %get-tuple-element.40), channel_id=1, source_target_pairs={{0,4},{2,6},{4,0},{6,2},{8,12},{10,14},{12,8},{14,10},{1,5},{3,7},... | collective-permute-start | bytes 196616 | tf_op jit(solution)/shard_map/ppermute | solution.py:589
  15.3 0.0 copy-done
  15.4 2.3 %before.1 = (bf16[16,64,256]{2,1,0:T(8,128)(2,1)S(1)}, f32[3,16,256]{2,1,0:T(8,128)S(1)}, f32[8,256]{1,0:T(8,128)S(1)}, f32[4,16,128]{2,1,0:T(8,128)S(1)}, f32[4,16,128]{2,1,0:T(8,128)S(1)}) custom-call(s32[16]{0:T(128)S(1)} %copy-done.11, f32[64]{0:T(128)S(1)} %copy-done.12, f32[64]{0:T(128)S(1)} %copy-done.13, f32[64]{0:T(128)S(1)} %copy-done.14, ...), custom_call_target="tpu_custom_call" | custom-call | bytes 14000000 | tf_op jit(solution)/shard_map/before/pallas_call | solution.py:592
  17.7 0.0 collective-permute-done.refs_1_
  17.7 1.9 %collective-permute-done.1.refs_2_ = bf16[2,128,128]{2,1,0:T(8,128)(2,1)S(1)} collective-permute-done((bf16[2,128,128]{2,1,0:T(8,128)(2,1)S(1)}, bf16[2,128,128]{2,1,0:T(8,128)(2,1)S(1)}, u32[]{:S(2)}, u32[]{:S(2)}) %collective-permute-start.1) | collective-permute-done | bytes 65568 | tf_op jit(solution)/shard_map/ppermute | solution.py:589
  19.6 2.3 %all-to-all-done.recv.new_ref = bf16[16,80,128]{2,1,0:T(8,128)(2,1)S(1)} async-done(((bf16[16,80,128]{2,1,0:T(8,128)(2,1)}), bf16[16,80,128]{2,1,0:T(8,128)(2,1)S(1)}, u32[]{:S(2)}, u32[]{:S(2)}) %all-to-all-start) | async-done | bytes 327712 | tf_op jit(solution)/shard_map/all_to_all | solution.py:576
  21.9 0.0 copy-done.9
  21.9 1.4 %coeff.3.mine = bf16[16,80,128]{2,1,0:T(8,128)(2,1)S(1)} custom-call(s32[16]{0:T(128)S(1)} %bitcast.4, s32[16]{0:T(128)S(1)} %copy-done.11, bf16[4,2048]{1,0:T(4,128)(2,1)S(1)} %copy-done.9, bf16[16,80,128]{2,1,0:T(8,128)(2,1)S(1)} %all-to-all-done.recv.new_ref), custom_call_target="tpu_custom_call" | custom-call | bytes 7000000 | tf_op jit(solution)/shard_map/coeff/pallas_call | solution.py:615
  23.3 0.1 collective-permute-start.2
  23.4 0.8 %collective-permute-start.3 = (bf16[2,128,128]{2,1,0:T(8,128)(2,1)S(1)}, bf16[2,128,128]{2,1,0:T(8,128)(2,1)S(1)}, u32[]{:S(2)}, u32[]{:S(2)}) collective-permute-start(bf16[2,128,128]{2,1,0:T(8,128)(2,1)S(1)} %get-tuple-element.51), channel_id=1, source_target_pairs={{0,6},{2,4},{4,2},{6,0},{8,14},{10,12},{12,10},{14,8},{1,7},{3,5},... | collective-permute-start | bytes 196616 | tf_op jit(solution)/shard_map/ppermute | solution.py:589
  24.1 1.5 %collective-permute-start.4 = (bf16[2,128,128]{2,1,0:T(8,128)(2,1)S(1)}, bf16[2,128,128]{2,1,0:T(8,128)(2,1)S(1)}, u32[]{:S(2)}, u32[]{:S(2)}) collective-permute-start(bf16[2,128,128]{2,1,0:T(8,128)(2,1)S(1)} %get-tuple-element.52), channel_id=1, source_target_pairs={{0,8},{2,10},{4,12},{6,14},{8,0},{10,2},{12,4},{14,6},{1,9},{3,11}... | collective-permute-start | bytes 196616 | tf_op jit(solution)/shard_map/ppermute | solution.py:589
  25.7 2.1 %collective-permute-start.5 = (bf16[2,128,128]{2,1,0:T(8,128)(2,1)S(1)}, bf16[2,128,128]{2,1,0:T(8,128)(2,1)S(1)}, u32[]{:S(2)}, u32[]{:S(2)}) collective-permute-start(bf16[2,128,128]{2,1,0:T(8,128)(2,1)S(1)} %get-tuple-element.53), channel_id=1, source_target_pairs={{0,10},{2,8},{4,14},{6,12},{8,2},{10,0},{12,6},{14,4},{1,11},{3,9}... | collective-permute-start | bytes 196616 | tf_op jit(solution)/shard_map/ppermute | solution.py:589
  27.8 1.9 %collective-permute-start.6 = (bf16[2,128,128]{2,1,0:T(8,128)(2,1)S(1)}, bf16[2,128,128]{2,1,0:T(8,128)(2,1)S(1)}, u32[]{:S(2)}, u32[]{:S(2)}) collective-permute-start(bf16[2,128,128]{2,1,0:T(8,128)(2,1)S(1)} %get-tuple-element.54), channel_id=1, source_target_pairs={{0,12},{2,14},{4,8},{6,10},{8,4},{10,6},{12,0},{14,2},{1,13},{3,15... | collective-permute-start | bytes 196616 | tf_op jit(solution)/shard_map/ppermute | solution.py:589
  29.7 0.0 collective-permute-done.2.other
  29.7 2.1 %collective-permute-start.7 = (bf16[2,128,128]{2,1,0:T(8,128)(2,1)S(1)}, bf16[2,128,128]{2,1,0:T(8,128)(2,1)S(1)}, u32[]{:S(2)}, u32[]{:S(2)}) collective-permute-start(bf16[2,128,128]{2,1,0:T(8,128)(2,1)S(1)} %get-tuple-element.55), channel_id=1, source_target_pairs={{0,14},{2,12},{4,10},{6,8},{8,6},{10,4},{12,2},{14,0},{1,15},{3,13... | collective-permute-start | bytes 196616 | tf_op jit(solution)/shard_map/ppermute | solution.py:589
  31.8 5.2 %main.1 = (f32[16,64,256]{2,1,0:T(8,128)S(1)}, bf16[16,24,128]{2,1,0:T(8,128)(2,1)}) custom-call(s32[16]{0:T(128)S(1)} %bitcast.5, s32[16]{0:T(128)S(1)} %copy-done.11, bf16[4,4096]{1,0:T(4,128)(2,1)S(1)} %copy-done.3, bf16[16,80,128]{2,1,0:T(8,128)(2,1)S(1)} %coeff.3.mine, bf16[16,80,128]{2,1,0:T(8,128)(2,1)S(1)} %collective-permute-done.2.other, ...), custom_call_target="tpu_custom_call" | custom-call | bytes 35000000 | tf_op jit(solution)/shard_map/main/pallas_call | solution.py:634
  37.0 0.0 collective-permute-done.3.refs_3_
  37.0 0.0 collective-permute-done.4.refs_4_
  37.0 0.4 collective-permute-done.5.refs_5_
  37.4 0.0 collective-permute-done.6.refs_6_
  37.4 0.0 collective-permute-done.7.refs_7_
  37.5 0.0 copy-start.4
  37.5 0.0 copy-start.8
  37.5 0.0 copy-start.15
  37.5 0.1 collective-permute-start.8
  37.6 5.3 %all-to-all-start.1 = ((bf16[16,24,128]{2,1,0:T(8,128)(2,1)}), bf16[16,24,128]{2,1,0:T(8,128)(2,1)S(1)}, u32[]{:S(2)}, u32[]{:S(2)}) async-start(bf16[16,24,128]{2,1,0:T(8,128)(2,1)} %get-tuple-element.56), calls=%async_computation.1 | async-start | bytes 196608 | tf_op jit(solution)/shard_map/all_to_all | solution.py:679
  42.8 0.0 copy-start.6
  42.9 0.0 collective-permute-done.8.crossed
  42.9 0.0 copy-done.4
  42.9 0.0 copy-done.8
  42.9 0.0 copy-done.15
  42.9 0.0 copy-start.7
  42.9 4.3 %cache.3 = (bf16[8,16,2048]{2,1,0:T(8,128)(2,1)}, bf16[2,2,8192]{2,1,0:T(2,128)(2,1)}) custom-call(s32[16]{0:T(128)S(1)} %bitcast.6, s32[16]{0:T(128)S(1)} %copy-done.11, s32[1,8]{1,0:T(1,128)S(1)} %copy-done.15, bf16[2,2,8192]{2,1,0:T(2,128)(2,1)S(1)} %copy-done.4, bf16[2,2,2048]{2,1,0:T(2,128)(2,1)S(1)} %copy-done.8, ...), custom_call_target="tpu_custom_call" | custom-call | bytes 17500000 | tf_op jit(solution)/shard_map/cache/pallas_call | solution.py:681
  47.2 3.0 %all-to-all-done.1.fin = bf16[16,24,128]{2,1,0:T(8,128)(2,1)S(1)} async-done(((bf16[16,24,128]{2,1,0:T(8,128)(2,1)}), bf16[16,24,128]{2,1,0:T(8,128)(2,1)S(1)}, u32[]{:S(2)}, u32[]{:S(2)}) %all-to-all-start.1) | async-done | bytes 98336 | tf_op jit(solution)/shard_map/all_to_all | solution.py:679
  50.3 1.8 %final.1 = (bf16[16,64,256]{2,1,0:T(8,128)(2,1)}, bf16[2,2,4096]{2,1,0:T(2,128)(2,1)}) custom-call(s32[16]{0:T(128)S(1)} %bitcast.7, s32[16]{0:T(128)S(1)} %copy-done.11, f32[1,4096]{1,0:T(1,128)S(1)} %bitcast.2, bf16[16,24,128]{2,1,0:T(8,128)(2,1)S(1)} %all-to-all-done.1.fin, f32[16,64,256]{2,1,0:T(8,128)S(1)} %get-tuple-element.67.gated, ...), custom_call_target="tpu_custom_call" | custom-call | tf_op jit(solution)/shard_map/final/pallas_call | solution.py:696
  (14 shorter events, 0.0 us)
Async XLA Ops:
  0.6 9.7 %copy-start.2 = (bf16[16,4,2048]{2,1,0:T(4,128)(2,1)S(1)}, bf16[16,4,2048]{2,1,0:T(4,128)(2,1)}, u32[]{:S(2)}) copy-start(bf16[16,4,2048]{2,1,0:T(4,128)(2,1)} %cache.2) | copy-start | bytes 786436
  2.8 12.5 %copy-start = (bf16[16,64,256]{2,1,0:T(8,128)(2,1)S(1)}, bf16[16,64,256]{2,1,0:T(8,128)(2,1)}, u32[]{:S(2)}) copy-start(bf16[16,64,256]{2,1,0:T(8,128)(2,1)} %hidden.1) | copy-start | bytes 1572868
  2.8 19.1 %all-to-all-start = ((bf16[16,80,128]{2,1,0:T(8,128)(2,1)}), bf16[16,80,128]{2,1,0:T(8,128)(2,1)S(1)}, u32[]{:S(2)}, u32[]{:S(2)}) async-start(bf16[16,80,128]{2,1,0:T(8,128)(2,1)} %pack.1), calls=%async_computation | async-start | bytes 655360 | tf_op jit(solution)/shard_map/all_to_all | solution.py:576
  10.3 0.7 %copy-start.10 = (s32[16,1]{0,1:T(1,128)S(1)}, s32[16,1]{0,1:T(1,128)}, u32[]{:S(2)}) copy-start(s32[16,1]{0,1:T(1,128)} %param.26) | copy-start | bytes 196
  11.0 4.3 %copy-start.3 = (bf16[4,4096]{1,0:T(4,128)(2,1)S(1)}, bf16[4,4096]{1,0:T(4,128)(2,1)}, u32[]{:S(2)}) copy-start(bf16[4,4096]{1,0:T(4,128)(2,1)} %taps_ref.5) | copy-start | bytes 98308
  11.0 4.3 %copy-start.5 = (f32[4,16,64]{2,1,0:T(8,128)S(1)}, f32[4,16,64]{2,1,0:T(8,128)}, u32[]{:S(2)}) copy-start(f32[4,16,64]{2,1,0:T(8,128)} %step.1) | copy-start | bytes 49156
  11.8 3.5 %copy-start.14 = (f32[64]{0:T(128)S(1)}, f32[64]{0:T(128)}, u32[]{:S(2)}) copy-start(f32[64]{0:T(128)} %skip.1) | copy-start | bytes 772
  11.8 3.5 %copy-start.11 = (s32[16]{0:T(128)S(1)}, s32[16]{0:T(128)}, u32[]{:S(2)}) copy-start(s32[16]{0:T(128)} %lengths.9) | copy-start | bytes 196
  11.8 3.5 %copy-start.12 = (f32[64]{0:T(128)S(1)}, f32[64]{0:T(128)}, u32[]{:S(2)}) copy-start(f32[64]{0:T(128)} %bias.1) | copy-start | bytes 772
  11.8 3.5 %copy-start.13 = (f32[64]{0:T(128)S(1)}, f32[64]{0:T(128)}, u32[]{:S(2)}) copy-start(f32[64]{0:T(128)} %decay.1) | copy-start | bytes 772
  11.9 5.9 %collective-permute-start = (bf16[2,128,128]{2,1,0:T(8,128)(2,1)S(1)}, bf16[2,128,128]{2,1,0:T(8,128)(2,1)S(1)}, u32[]{:S(2)}, u32[]{:S(2)}) collective-permute-start(bf16[2,128,128]{2,1,0:T(8,128)(2,1)S(1)} %get-tuple-element.39), channel_id=1, source_target_pairs={{0,2},{2,0},{4,6},{6,4},{8,10},{10,8},{12,14},{14,12},{1,3},{3,1},... | collective-permute-start | bytes 196616 | tf_op jit(solution)/shard_map/ppermute | solution.py:589
  13.8 8.1 %copy-start.9 = (bf16[4,2048]{1,0:T(4,128)(2,1)S(1)}, bf16[4,2048]{1,0:T(4,128)(2,1)}, u32[]{:S(2)}) copy-start(bf16[4,2048]{1,0:T(4,128)(2,1)} %taps_ref.4) | copy-start | bytes 49156
  13.9 18.0 %copy-start.1 = (bf16[16,64,256]{2,1,0:T(8,128)(2,1)S(1)}, bf16[16,64,256]{2,1,0:T(8,128)(2,1)}, u32[]{:S(2)}) copy-start(bf16[16,64,256]{2,1,0:T(8,128)(2,1)} %gate.1) | copy-start | bytes 1572868
  13.9 5.8 %collective-permute-start.1 = (bf16[2,128,128]{2,1,0:T(8,128)(2,1)S(1)}, bf16[2,128,128]{2,1,0:T(8,128)(2,1)S(1)}, u32[]{:S(2)}, u32[]{:S(2)}) collective-permute-start(bf16[2,128,128]{2,1,0:T(8,128)(2,1)S(1)} %get-tuple-element.40), channel_id=1, source_target_pairs={{0,4},{2,6},{4,0},{6,2},{8,12},{10,14},{12,8},{14,10},{1,5},{3,7},... | collective-permute-start | bytes 196616 | tf_op jit(solution)/shard_map/ppermute | solution.py:589
  23.3 6.4 %collective-permute-start.2 = (bf16[16,80,128]{2,1,0:T(8,128)(2,1)S(1)}, bf16[16,80,128]{2,1,0:T(8,128)(2,1)S(1)}, u32[]{:S(2)}, u32[]{:S(2)}) collective-permute-start(bf16[16,80,128]{2,1,0:T(8,128)(2,1)S(1)} %coeff.3.mine), channel_id=1, source_target_pairs={{0,1},{1,0},{2,3},{3,2},{4,5},{5,4},{6,7},{7,6},{8,9},{9,8},{10,11... | collective-permute-start | bytes 983048 | tf_op jit(solution)/shard_map/ppermute | solution.py:631
  23.4 13.6 %collective-permute-start.3 = (bf16[2,128,128]{2,1,0:T(8,128)(2,1)S(1)}, bf16[2,128,128]{2,1,0:T(8,128)(2,1)S(1)}, u32[]{:S(2)}, u32[]{:S(2)}) collective-permute-start(bf16[2,128,128]{2,1,0:T(8,128)(2,1)S(1)} %get-tuple-element.51), channel_id=1, source_target_pairs={{0,6},{2,4},{4,2},{6,0},{8,14},{10,12},{12,10},{14,8},{1,7},{3,5},... | collective-permute-start | bytes 196616 | tf_op jit(solution)/shard_map/ppermute | solution.py:589
  24.1 12.8 %collective-permute-start.4 = (bf16[2,128,128]{2,1,0:T(8,128)(2,1)S(1)}, bf16[2,128,128]{2,1,0:T(8,128)(2,1)S(1)}, u32[]{:S(2)}, u32[]{:S(2)}) collective-permute-start(bf16[2,128,128]{2,1,0:T(8,128)(2,1)S(1)} %get-tuple-element.52), channel_id=1, source_target_pairs={{0,8},{2,10},{4,12},{6,14},{8,0},{10,2},{12,4},{14,6},{1,9},{3,11}... | collective-permute-start | bytes 196616 | tf_op jit(solution)/shard_map/ppermute | solution.py:589
  25.7 11.8 %collective-permute-start.5 = (bf16[2,128,128]{2,1,0:T(8,128)(2,1)S(1)}, bf16[2,128,128]{2,1,0:T(8,128)(2,1)S(1)}, u32[]{:S(2)}, u32[]{:S(2)}) collective-permute-start(bf16[2,128,128]{2,1,0:T(8,128)(2,1)S(1)} %get-tuple-element.53), channel_id=1, source_target_pairs={{0,10},{2,8},{4,14},{6,12},{8,2},{10,0},{12,6},{14,4},{1,11},{3,9}... | collective-permute-start | bytes 196616 | tf_op jit(solution)/shard_map/ppermute | solution.py:589
  27.8 9.7 %collective-permute-start.6 = (bf16[2,128,128]{2,1,0:T(8,128)(2,1)S(1)}, bf16[2,128,128]{2,1,0:T(8,128)(2,1)S(1)}, u32[]{:S(2)}, u32[]{:S(2)}) collective-permute-start(bf16[2,128,128]{2,1,0:T(8,128)(2,1)S(1)} %get-tuple-element.54), channel_id=1, source_target_pairs={{0,12},{2,14},{4,8},{6,10},{8,4},{10,6},{12,0},{14,2},{1,13},{3,15... | collective-permute-start | bytes 196616 | tf_op jit(solution)/shard_map/ppermute | solution.py:589
  29.7 7.7 %collective-permute-start.7 = (bf16[2,128,128]{2,1,0:T(8,128)(2,1)S(1)}, bf16[2,128,128]{2,1,0:T(8,128)(2,1)S(1)}, u32[]{:S(2)}, u32[]{:S(2)}) collective-permute-start(bf16[2,128,128]{2,1,0:T(8,128)(2,1)S(1)} %get-tuple-element.55), channel_id=1, source_target_pairs={{0,14},{2,12},{4,10},{6,8},{8,6},{10,4},{12,2},{14,0},{1,15},{3,13... | collective-permute-start | bytes 196616 | tf_op jit(solution)/shard_map/ppermute | solution.py:589
  37.5 5.4 %copy-start.4 = (bf16[2,2,8192]{2,1,0:T(2,128)(2,1)S(1)}, bf16[2,2,8192]{2,1,0:T(2,128)(2,1)}, u32[]{:S(2)}) copy-start(bf16[2,2,8192]{2,1,0:T(2,128)(2,1)} %query.1) | copy-start | bytes 196612
  37.5 5.4 %copy-start.8 = (bf16[2,2,2048]{2,1,0:T(2,128)(2,1)S(1)}, bf16[2,2,2048]{2,1,0:T(2,128)(2,1)}, u32[]{:S(2)}) copy-start(bf16[2,2,2048]{2,1,0:T(2,128)(2,1)} %cache_new.1) | copy-start | bytes 49156
  37.5 5.4 %copy-start.15 = (s32[1,8]{1,0:T(1,128)S(1)}, s32[1,8]{1,0:T(1,128)}, u32[]{:S(2)}) copy-start(s32[1,8]{1,0:T(1,128)} %pages.1) | copy-start | bytes 100
  37.5 5.4 %collective-permute-start.8 = (bf16[8,128,128]{2,1,0:T(8,128)(2,1)S(1)}, bf16[8,128,128]{2,1,0:T(8,128)(2,1)S(1)}, u32[]{:S(2)}, u32[]{:S(2)}) collective-permute-start(bf16[8,128,128]{2,1,0:T(8,128)(2,1)S(1)} %stack.1), channel_id=1, source_target_pairs={{0,1},{1,0},{2,3},{3,2},{4,5},{5,4},{6,7},{7,6},{8,9},{9,8},{10,11... | collective-permute-start | bytes 786440 | tf_op jit(solution)/shard_map/ppermute | solution.py:678
  37.6 12.7 %all-to-all-start.1 = ((bf16[16,24,128]{2,1,0:T(8,128)(2,1)}), bf16[16,24,128]{2,1,0:T(8,128)(2,1)S(1)}, u32[]{:S(2)}, u32[]{:S(2)}) async-start(bf16[16,24,128]{2,1,0:T(8,128)(2,1)} %get-tuple-element.56), calls=%async_computation.1 | async-start | bytes 196608 | tf_op jit(solution)/shard_map/all_to_all | solution.py:679
  42.8 7.4 %copy-start.6 = (bf16[2,2,4096]{2,1,0:T(2,128)(2,1)S(1)}, bf16[2,2,4096]{2,1,0:T(2,128)(2,1)}, u32[]{:S(2)}) copy-start(bf16[2,2,4096]{2,1,0:T(2,128)(2,1)} %new_gate.1) | copy-start | bytes 98308
  42.9 7.4 %copy-start.7 = (f32[4096]{0:T(1024)S(1)}, f32[4096]{0:T(1024)}, u32[]{:S(2)}) copy-start(f32[4096]{0:T(1024)} %param.33) | copy-start | bytes 49156

commit v5 on v4

--- a/solution.py
+++ b/solution.py
@@ -604,7 +604,7 @@
         cost_estimate=cost(4),
         name="before",
     )(lengths, step_bias, decay_log, skip_gain, conv_hidden, hidden_pre, step_raw)
-    early = (1, 2)
+    early = (1, 3, 6)
     recv, sums, *held = lax.optimization_barrier(
         (recv, before[-1], *(kept[m] for m in early))
     )

time: 52.4 us -> 51.3 us (0.979)
  starting transfers between devices: 24.8 us -> 23.7 us
    ppermute x7, waiting for transfers between devices: 2.37 us -> 4.76 us  [local(): lax.ppermute(kept[m], 'tensor', [(i, i ^ m) for i in range(chips)])]
    all_to_all x1, waiting for transfers between devices: 2.28 us -> 0.01 us  [local(): recv = lax.all_to_all(send, AXES, split_axis=0, concat_axis=0, tiled=True)]
    all_to_all x1, starting transfers between devices: 5.27 us -> 3.52 us  [local(): fin_got = lax.all_to_all(fin, AXES, split_axis=0, concat_axis=0, tiled=True)]
    ppermute x7, starting transfers between devices: 11.9 us -> 12.5 us  [local(): lax.ppermute(kept[m], 'tensor', [(i, i ^ m) for i in range(chips)])]
  transfers between devices with their start and end apart: 11 -> 11, of which waited for: 4 -> 3; matrix products, arithmetic and copies ran while one was open for 0% -> 0% of each run, Pallas kernels for 24% -> 25%
where the time goes in v5:
time: 51.3 us; the launch traced here: 51 us
  starting transfers between devices  23.7 us (46%)
  Pallas kernels  17.9 us (35%)
  waiting for transfers between devices  7.75 us (15%)
  between operations  0.86 us (2%)
  local copies, waits for them, and re-layouts  0.71 us (1%)
    ppermute x7, starting transfers between devices, local(): lax.ppermute(kept[m], 'tensor', [(i, i ^ m) for i in range(chips)])  12.5 us
    all_to_all x1, starting transfers between devices, local(): recv = lax.all_to_all(send, AXES, split_axis=0, concat_axis=0, tiled=True)  7.53 us
    pallas_call x1, Pallas kernels, local(): pl.pallas_call(main_kernel, grid=(1,), out_shape=(jax.ShapeDtypeStruct((p...  5.16 us
    ppermute x7, waiting for transfers between devices, local(): lax.ppermute(kept[m], 'tensor', [(i, i ^ m) for i in range(chips)])  4.76 us
    pallas_call x1, Pallas kernels, local(): pl.pallas_call(cache_kernel, out_shape=(jax.ShapeDtypeStruct((page_table....  4.32 us
    all_to_all x1, starting transfers between devices, local(): fin_got = lax.all_to_all(fin, AXES, split_axis=0, concat_axis=0, tiled=True)  3.52 us
    all_to_all x1, waiting for transfers between devices, local(): fin_got = lax.all_to_all(fin, AXES, split_axis=0, concat_axis=0, tiled=True)  2.99 us
    pallas_call x1, Pallas kernels, local(): pl.pallas_call(before_kernel, out_shape=(jax.ShapeDtypeStruct((prompts, s...  2.34 us
  transfers between devices with their start and end apart: 11, of which 3 were waited for; matrix products, arithmetic and copies ran while one was open for 0% of the time, Pallas kernels for 25%

profile of v5, /device:TPU:0, one launch (start us, length us, event | category | flops | bytes accessed | tf_op | source)
XLA Modules:
  0.0 51.0 jit_solution(11467908534153396481)
XLA Ops:
  0.6 0.0 copy-start.2
  0.6 2.1 %pack.1 = bf16[16,80,128]{2,1,0:T(8,128)(2,1)} custom-call(bf16[1,64,2048]{2,1,0:T(8,128)(2,1)} %coeff.2, bf16[2,2,4096]{2,1,0:T(2,128)(2,1)} %hidden_in.1, bf16[2,2,2048]{2,1,0:T(2,128)(2,1)} %coeff_new_in.1, f32[2,2,64]{2,1,0:T(2,128)} %step_in.1), custom_call_target="tpu_custom_call" | custom-call | tf_op jit(solution)/shard_map/pack/pallas_call | solution.py:563
  2.8 0.0 copy-start
  2.8 7.5 %all-to-all-start = ((bf16[16,80,128]{2,1,0:T(8,128)(2,1)}), bf16[16,80,128]{2,1,0:T(8,128)(2,1)S(1)}, u32[]{:S(2)}, u32[]{:S(2)}) async-start(bf16[16,80,128]{2,1,0:T(8,128)(2,1)} %pack.1), calls=%async_computation | async-start | bytes 655360 | tf_op jit(solution)/shard_map/all_to_all | solution.py:576
  10.3 0.0 copy-start.10
  10.3 0.0 copy-done.2
  10.4 0.6 %copy-done.10 = s32[16,1]{0,1:T(1,128)S(1)} copy-done((s32[16,1]{0,1:T(1,128)S(1)}, s32[16,1]{0,1:T(1,128)}, u32[]{:S(2)}) %copy-start.10) | copy-done | bytes 88
  11.0 0.8 %pack_cache.1 = (bf16[2,128,128]{2,1,0:T(8,128)(2,1)S(1)}, bf16[2,128,128]{2,1,0:T(8,128)(2,1)S(1)}, bf16[2,128,128]{2,1,0:T(8,128)(2,1)S(1)}, bf16[2,128,128]{2...) custom-call(s32[16]{0:T(128)S(1)} %bitcast.3, ...), custom_call_target="tpu_custom_call" | custom-call | bytes 10500000 | tf_op jit(solution)/shard_map/pack_cache/pallas_call | solution.py:578
  11.8 2.0 %collective-permute-start = (bf16[2,128,128]{2,1,0:T(8,128)(2,1)S(1)}, bf16[2,128,128]{2,1,0:T(8,128)(2,1)S(1)}, u32[]{:S(2)}, u32[]{:S(2)}) collective-permute-start(bf16[2,128,128]{2,1,0:T(8,128)(2,1)S(1)} %get-tuple-element.40), channel_id=1, source_target_pairs={{0,2},{2,0},{4,6},{6,4},{8,10},{10,8},{12,14},{14,12},{1,3},{3,1},... | collective-permute-start | bytes 196616 | tf_op jit(solution)/shard_map/ppermute | solution.py:589
  13.8 1.5 %collective-permute-start.1 = (bf16[2,128,128]{2,1,0:T(8,128)(2,1)S(1)}, bf16[2,128,128]{2,1,0:T(8,128)(2,1)S(1)}, u32[]{:S(2)}, u32[]{:S(2)}) collective-permute-start(bf16[2,128,128]{2,1,0:T(8,128)(2,1)S(1)} %get-tuple-element.41), channel_id=1, source_target_pairs={{0,6},{2,4},{4,2},{6,0},{8,14},{10,12},{12,10},{14,8},{1,7},{3,5},... | collective-permute-start | bytes 196616 | tf_op jit(solution)/shard_map/ppermute | solution.py:589
  15.3 2.4 %collective-permute-start.2 = (bf16[2,128,128]{2,1,0:T(8,128)(2,1)S(1)}, bf16[2,128,128]{2,1,0:T(8,128)(2,1)S(1)}, u32[]{:S(2)}, u32[]{:S(2)}) collective-permute-start(bf16[2,128,128]{2,1,0:T(8,128)(2,1)S(1)} %get-tuple-element.42), channel_id=1, source_target_pairs={{0,12},{2,14},{4,8},{6,10},{8,4},{10,6},{12,0},{14,2},{1,13},{3,15... | collective-permute-start | bytes 196616 | tf_op jit(solution)/shard_map/ppermute | solution.py:589
  17.7 0.0 copy-done
  17.7 0.0 copy-done.3
  17.7 0.0 copy-done.5
  17.7 0.0 copy-done.14
  17.8 2.3 %before.1 = (bf16[16,64,256]{2,1,0:T(8,128)(2,1)S(1)}, f32[3,16,256]{2,1,0:T(8,128)S(1)}, f32[8,256]{1,0:T(8,128)S(1)}, f32[4,16,128]{2,1,0:T(8,128)S(1)}, f32[4,16,128]{2,1,0:T(8,128)S(1)}) custom-call(s32[16]{0:T(128)S(1)} %copy-done.11, f32[64]{0:T(128)S(1)} %copy-done.12, f32[64]{0:T(128)S(1)} %copy-done.13, f32[64]{0:T(128)S(1)} %copy-done.14, ...), custom_call_target="tpu_custom_call" | custom-call | bytes 14000000 | tf_op jit(solution)/shard_map/before/pallas_call | solution.py:592
  20.1 0.0 collective-permute-done.refs_1_
  20.1 0.0 collective-permute-done.1.refs_3_
  20.1 3.4 %collective-permute-done.2.refs_6_ = bf16[2,128,128]{2,1,0:T(8,128)(2,1)S(1)} collective-permute-done((bf16[2,128,128]{2,1,0:T(8,128)(2,1)S(1)}, bf16[2,128,128]{2,1,0:T(8,128)(2,1)S(1)}, u32[]{:S(2)}, u32[]{:S(2)}) %collective-permute-start.2) | collective-permute-done | bytes 65568 | tf_op jit(solution)/shard_map/ppermute | solution.py:589
  23.5 0.0 all-to-all-done.recv.new_ref
  23.5 1.4 %coeff.3.mine = bf16[16,80,128]{2,1,0:T(8,128)(2,1)S(1)} custom-call(s32[16]{0:T(128)S(1)} %bitcast.4, s32[16]{0:T(128)S(1)} %copy-done.11, bf16[4,2048]{1,0:T(4,128)(2,1)S(1)} %copy-done.9, bf16[16,80,128]{2,1,0:T(8,128)(2,1)S(1)} %all-to-all-done.recv.new_ref), custom_call_target="tpu_custom_call" | custom-call | bytes 7000000 | tf_op jit(solution)/shard_map/coeff/pallas_call | solution.py:615
  24.9 0.1 collective-permute-start.3
  25.0 1.3 %collective-permute-start.4 = (bf16[2,128,128]{2,1,0:T(8,128)(2,1)S(1)}, bf16[2,128,128]{2,1,0:T(8,128)(2,1)S(1)}, u32[]{:S(2)}, u32[]{:S(2)}) collective-permute-start(bf16[2,128,128]{2,1,0:T(8,128)(2,1)S(1)} %get-tuple-element.52), channel_id=1, source_target_pairs={{0,4},{2,6},{4,0},{6,2},{8,12},{10,14},{12,8},{14,10},{1,5},{3,7},... | collective-permute-start | bytes 196616 | tf_op jit(solution)/shard_map/ppermute | solution.py:589
  26.3 0.9 %collective-permute-start.5 = (bf16[2,128,128]{2,1,0:T(8,128)(2,1)S(1)}, bf16[2,128,128]{2,1,0:T(8,128)(2,1)S(1)}, u32[]{:S(2)}, u32[]{:S(2)}) collective-permute-start(bf16[2,128,128]{2,1,0:T(8,128)(2,1)S(1)} %get-tuple-element.54), channel_id=1, source_target_pairs={{0,8},{2,10},{4,12},{6,14},{8,0},{10,2},{12,4},{14,6},{1,9},{3,11}... | collective-permute-start | bytes 196616 | tf_op jit(solution)/shard_map/ppermute | solution.py:589
  27.2 2.9 %collective-permute-start.6 = (bf16[2,128,128]{2,1,0:T(8,128)(2,1)S(1)}, bf16[2,128,128]{2,1,0:T(8,128)(2,1)S(1)}, u32[]{:S(2)}, u32[]{:S(2)}) collective-permute-start(bf16[2,128,128]{2,1,0:T(8,128)(2,1)S(1)} %get-tuple-element.55), channel_id=1, source_target_pairs={{0,10},{2,8},{4,14},{6,12},{8,2},{10,0},{12,6},{14,4},{1,11},{3,9}... | collective-permute-start | bytes 196616 | tf_op jit(solution)/shard_map/ppermute | solution.py:589
  30.1 1.5 %collective-permute-start.7 = (bf16[2,128,128]{2,1,0:T(8,128)(2,1)S(1)}, bf16[2,128,128]{2,1,0:T(8,128)(2,1)S(1)}, u32[]{:S(2)}, u32[]{:S(2)}) collective-permute-start(bf16[2,128,128]{2,1,0:T(8,128)(2,1)S(1)} %get-tuple-element.57), channel_id=1, source_target_pairs={{0,14},{2,12},{4,10},{6,8},{8,6},{10,4},{12,2},{14,0},{1,15},{3,13... | collective-permute-start | bytes 196616 | tf_op jit(solution)/shard_map/ppermute | solution.py:589
  31.6 0.0 collective-permute-done.3.other
  31.6 0.0 copy-done.1
  31.6 5.2 %main.1 = (f32[16,64,256]{2,1,0:T(8,128)S(1)}, bf16[16,24,128]{2,1,0:T(8,128)(2,1)}) custom-call(s32[16]{0:T(128)S(1)} %bitcast.5, s32[16]{0:T(128)S(1)} %copy-done.11, bf16[4,4096]{1,0:T(4,128)(2,1)S(1)} %copy-done.3, bf16[16,80,128]{2,1,0:T(8,128)(2,1)S(1)} %coeff.3.mine, bf16[16,80,128]{2,1,0:T(8,128)(2,1)S(1)} %collective-permute-done.3.other, ...), custom_call_target="tpu_custom_call" | custom-call | bytes 35000000 | tf_op jit(solution)/shard_map/main/pallas_call | solution.py:634
  36.8 0.0 collective-permute-done.4.refs_2_
  36.8 0.0 collective-permute-done.5.refs_4_
  36.8 1.4 %collective-permute-done.6.refs_5_ = bf16[2,128,128]{2,1,0:T(8,128)(2,1)S(1)} collective-permute-done((bf16[2,128,128]{2,1,0:T(8,128)(2,1)S(1)}, bf16[2,128,128]{2,1,0:T(8,128)(2,1)S(1)}, u32[]{:S(2)}, u32[]{:S(2)}) %collective-permute-start.6) | collective-permute-done | bytes 65568 | tf_op jit(solution)/shard_map/ppermute | solution.py:589
  38.2 0.0 collective-permute-done.7.refs_7_
  38.2 0.0 copy-start.4
  38.2 0.0 copy-start.8
  38.2 0.0 copy-start.15
  38.2 0.1 collective-permute-start.8
  38.3 3.5 %all-to-all-start.1 = ((bf16[16,24,128]{2,1,0:T(8,128)(2,1)}), bf16[16,24,128]{2,1,0:T(8,128)(2,1)S(1)}, u32[]{:S(2)}, u32[]{:S(2)}) async-start(bf16[16,24,128]{2,1,0:T(8,128)(2,1)} %get-tuple-element.58), calls=%async_computation.1 | async-start | bytes 196608 | tf_op jit(solution)/shard_map/all_to_all | solution.py:679
  41.8 0.0 copy-start.6
  41.8 0.0 collective-permute-done.8.crossed
  41.8 0.0 copy-done.4
  41.9 0.0 copy-done.8
  41.9 0.0 copy-done.15
  41.9 0.0 copy-start.7
  41.9 4.3 %cache.3 = (bf16[8,16,2048]{2,1,0:T(8,128)(2,1)}, bf16[2,2,8192]{2,1,0:T(2,128)(2,1)}) custom-call(s32[16]{0:T(128)S(1)} %bitcast.6, s32[16]{0:T(128)S(1)} %copy-done.11, s32[1,8]{1,0:T(1,128)S(1)} %copy-done.15, bf16[2,2,8192]{2,1,0:T(2,128)(2,1)S(1)} %copy-done.4, bf16[2,2,2048]{2,1,0:T(2,128)(2,1)S(1)} %copy-done.8, ...), custom_call_target="tpu_custom_call" | custom-call | bytes 17500000 | tf_op jit(solution)/shard_map/cache/pallas_call | solution.py:681
  46.2 3.0 %all-to-all-done.1.fin = bf16[16,24,128]{2,1,0:T(8,128)(2,1)S(1)} async-done(((bf16[16,24,128]{2,1,0:T(8,128)(2,1)}), bf16[16,24,128]{2,1,0:T(8,128)(2,1)S(1)}, u32[]{:S(2)}, u32[]{:S(2)}) %all-to-all-start.1) | async-done | bytes 98336 | tf_op jit(solution)/shard_map/all_to_all | solution.py:679
  49.2 0.0 copy-done.7
  49.2 1.8 %final.1 = (bf16[16,64,256]{2,1,0:T(8,128)(2,1)}, bf16[2,2,4096]{2,1,0:T(2,128)(2,1)}) custom-call(s32[16]{0:T(128)S(1)} %bitcast.7, s32[16]{0:T(128)S(1)} %copy-done.11, f32[1,4096]{1,0:T(1,128)S(1)} %bitcast.2, bf16[16,24,128]{2,1,0:T(8,128)(2,1)S(1)} %all-to-all-done.1.fin, f32[16,64,256]{2,1,0:T(8,128)S(1)} %get-tuple-element.69.gated, ...), custom_call_target="tpu_custom_call" | custom-call | tf_op jit(solution)/shard_map/final/pallas_call | solution.py:696
  (14 shorter events, 0.0 us)
Async XLA Ops:
  0.6 9.7 %copy-start.2 = (bf16[16,4,2048]{2,1,0:T(4,128)(2,1)S(1)}, bf16[16,4,2048]{2,1,0:T(4,128)(2,1)}, u32[]{:S(2)}) copy-start(bf16[16,4,2048]{2,1,0:T(4,128)(2,1)} %cache.2) | copy-start | bytes 786436
  2.8 14.9 %copy-start = (bf16[16,64,256]{2,1,0:T(8,128)(2,1)S(1)}, bf16[16,64,256]{2,1,0:T(8,128)(2,1)}, u32[]{:S(2)}) copy-start(bf16[16,64,256]{2,1,0:T(8,128)(2,1)} %hidden.1) | copy-start | bytes 1572868
  2.8 20.7 %all-to-all-start = ((bf16[16,80,128]{2,1,0:T(8,128)(2,1)}), bf16[16,80,128]{2,1,0:T(8,128)(2,1)S(1)}, u32[]{:S(2)}, u32[]{:S(2)}) async-start(bf16[16,80,128]{2,1,0:T(8,128)(2,1)} %pack.1), calls=%async_computation | async-start | bytes 655360 | tf_op jit(solution)/shard_map/all_to_all | solution.py:576
  10.3 0.7 %copy-start.10 = (s32[16,1]{0,1:T(1,128)S(1)}, s32[16,1]{0,1:T(1,128)}, u32[]{:S(2)}) copy-start(s32[16,1]{0,1:T(1,128)} %param.26) | copy-start | bytes 196
  11.0 6.7 %copy-start.3 = (bf16[4,4096]{1,0:T(4,128)(2,1)S(1)}, bf16[4,4096]{1,0:T(4,128)(2,1)}, u32[]{:S(2)}) copy-start(bf16[4,4096]{1,0:T(4,128)(2,1)} %taps_ref.5) | copy-start | bytes 98308
  11.0 6.7 %copy-start.5 = (f32[4,16,64]{2,1,0:T(8,128)S(1)}, f32[4,16,64]{2,1,0:T(8,128)}, u32[]{:S(2)}) copy-start(f32[4,16,64]{2,1,0:T(8,128)} %step.1) | copy-start | bytes 49156
  11.8 8.3 %collective-permute-start = (bf16[2,128,128]{2,1,0:T(8,128)(2,1)S(1)}, bf16[2,128,128]{2,1,0:T(8,128)(2,1)S(1)}, u32[]{:S(2)}, u32[]{:S(2)}) collective-permute-start(bf16[2,128,128]{2,1,0:T(8,128)(2,1)S(1)} %get-tuple-element.40), channel_id=1, source_target_pairs={{0,2},{2,0},{4,6},{6,4},{8,10},{10,8},{12,14},{14,12},{1,3},{3,1},... | collective-permute-start | bytes 196616 | tf_op jit(solution)/shard_map/ppermute | solution.py:589
  13.8 3.9 %copy-start.14 = (f32[64]{0:T(128)S(1)}, f32[64]{0:T(128)}, u32[]{:S(2)}) copy-start(f32[64]{0:T(128)} %skip.1) | copy-start | bytes 772
  13.8 3.9 %copy-start.11 = (s32[16]{0:T(128)S(1)}, s32[16]{0:T(128)}, u32[]{:S(2)}) copy-start(s32[16]{0:T(128)} %lengths.9) | copy-start | bytes 196
  13.8 3.9 %copy-start.12 = (f32[64]{0:T(128)S(1)}, f32[64]{0:T(128)}, u32[]{:S(2)}) copy-start(f32[64]{0:T(128)} %bias.1) | copy-start | bytes 772
  13.8 3.9 %copy-start.13 = (f32[64]{0:T(128)S(1)}, f32[64]{0:T(128)}, u32[]{:S(2)}) copy-start(f32[64]{0:T(128)} %decay.1) | copy-start | bytes 772
  13.8 6.3 %collective-permute-start.1 = (bf16[2,128,128]{2,1,0:T(8,128)(2,1)S(1)}, bf16[2,128,128]{2,1,0:T(8,128)(2,1)S(1)}, u32[]{:S(2)}, u32[]{:S(2)}) collective-permute-start(bf16[2,128,128]{2,1,0:T(8,128)(2,1)S(1)} %get-tuple-element.41), channel_id=1, source_target_pairs={{0,6},{2,4},{4,2},{6,0},{8,14},{10,12},{12,10},{14,8},{1,7},{3,5},... | collective-permute-start | bytes 196616 | tf_op jit(solution)/shard_map/ppermute | solution.py:589
  15.3 8.2 %copy-start.9 = (bf16[4,2048]{1,0:T(4,128)(2,1)S(1)}, bf16[4,2048]{1,0:T(4,128)(2,1)}, u32[]{:S(2)}) copy-start(bf16[4,2048]{1,0:T(4,128)(2,1)} %taps_ref.4) | copy-start | bytes 49156
  15.3 16.3 %copy-start.1 = (bf16[16,64,256]{2,1,0:T(8,128)(2,1)S(1)}, bf16[16,64,256]{2,1,0:T(8,128)(2,1)}, u32[]{:S(2)}) copy-start(bf16[16,64,256]{2,1,0:T(8,128)(2,1)} %gate.1) | copy-start | bytes 1572868
  15.3 8.1 %collective-permute-start.2 = (bf16[2,128,128]{2,1,0:T(8,128)(2,1)S(1)}, bf16[2,128,128]{2,1,0:T(8,128)(2,1)S(1)}, u32[]{:S(2)}, u32[]{:S(2)}) collective-permute-start(bf16[2,128,128]{2,1,0:T(8,128)(2,1)S(1)} %get-tuple-element.42), channel_id=1, source_target_pairs={{0,12},{2,14},{4,8},{6,10},{8,4},{10,6},{12,0},{14,2},{1,13},{3,15... | collective-permute-start | bytes 196616 | tf_op jit(solution)/shard_map/ppermute | solution.py:589
  24.9 6.7 %collective-permute-start.3 = (bf16[16,80,128]{2,1,0:T(8,128)(2,1)S(1)}, bf16[16,80,128]{2,1,0:T(8,128)(2,1)S(1)}, u32[]{:S(2)}, u32[]{:S(2)}) collective-permute-start(bf16[16,80,128]{2,1,0:T(8,128)(2,1)S(1)} %coeff.3.mine), channel_id=1, source_target_pairs={{0,1},{1,0},{2,3},{3,2},{4,5},{5,4},{6,7},{7,6},{8,9},{9,8},{10,11... | collective-permute-start | bytes 983048 | tf_op jit(solution)/shard_map/ppermute | solution.py:631
  25.0 11.8 %collective-permute-start.4 = (bf16[2,128,128]{2,1,0:T(8,128)(2,1)S(1)}, bf16[2,128,128]{2,1,0:T(8,128)(2,1)S(1)}, u32[]{:S(2)}, u32[]{:S(2)}) collective-permute-start(bf16[2,128,128]{2,1,0:T(8,128)(2,1)S(1)} %get-tuple-element.52), channel_id=1, source_target_pairs={{0,4},{2,6},{4,0},{6,2},{8,12},{10,14},{12,8},{14,10},{1,5},{3,7},... | collective-permute-start | bytes 196616 | tf_op jit(solution)/shard_map/ppermute | solution.py:589
  26.3 10.5 %collective-permute-start.5 = (bf16[2,128,128]{2,1,0:T(8,128)(2,1)S(1)}, bf16[2,128,128]{2,1,0:T(8,128)(2,1)S(1)}, u32[]{:S(2)}, u32[]{:S(2)}) collective-permute-start(bf16[2,128,128]{2,1,0:T(8,128)(2,1)S(1)} %get-tuple-element.54), channel_id=1, source_target_pairs={{0,8},{2,10},{4,12},{6,14},{8,0},{10,2},{12,4},{14,6},{1,9},{3,11}... | collective-permute-start | bytes 196616 | tf_op jit(solution)/shard_map/ppermute | solution.py:589
  27.2 10.9 %collective-permute-start.6 = (bf16[2,128,128]{2,1,0:T(8,128)(2,1)S(1)}, bf16[2,128,128]{2,1,0:T(8,128)(2,1)S(1)}, u32[]{:S(2)}, u32[]{:S(2)}) collective-permute-start(bf16[2,128,128]{2,1,0:T(8,128)(2,1)S(1)} %get-tuple-element.55), channel_id=1, source_target_pairs={{0,10},{2,8},{4,14},{6,12},{8,2},{10,0},{12,6},{14,4},{1,11},{3,9}... | collective-permute-start | bytes 196616 | tf_op jit(solution)/shard_map/ppermute | solution.py:589
  30.1 8.0 %collective-permute-start.7 = (bf16[2,128,128]{2,1,0:T(8,128)(2,1)S(1)}, bf16[2,128,128]{2,1,0:T(8,128)(2,1)S(1)}, u32[]{:S(2)}, u32[]{:S(2)}) collective-permute-start(bf16[2,128,128]{2,1,0:T(8,128)(2,1)S(1)} %get-tuple-element.57), channel_id=1, source_target_pairs={{0,14},{2,12},{4,10},{6,8},{8,6},{10,4},{12,2},{14,0},{1,15},{3,13... | collective-permute-start | bytes 196616 | tf_op jit(solution)/shard_map/ppermute | solution.py:589
  38.2 3.7 %copy-start.4 = (bf16[2,2,8192]{2,1,0:T(2,128)(2,1)S(1)}, bf16[2,2,8192]{2,1,0:T(2,128)(2,1)}, u32[]{:S(2)}) copy-start(bf16[2,2,8192]{2,1,0:T(2,128)(2,1)} %query.1) | copy-start | bytes 196612
  38.2 3.7 %copy-start.8 = (bf16[2,2,2048]{2,1,0:T(2,128)(2,1)S(1)}, bf16[2,2,2048]{2,1,0:T(2,128)(2,1)}, u32[]{:S(2)}) copy-start(bf16[2,2,2048]{2,1,0:T(2,128)(2,1)} %cache_new.1) | copy-start | bytes 49156
  38.2 3.7 %copy-start.15 = (s32[1,8]{1,0:T(1,128)S(1)}, s32[1,8]{1,0:T(1,128)}, u32[]{:S(2)}) copy-start(s32[1,8]{1,0:T(1,128)} %pages.1) | copy-start | bytes 100
  38.2 3.6 %collective-permute-start.8 = (bf16[8,128,128]{2,1,0:T(8,128)(2,1)S(1)}, bf16[8,128,128]{2,1,0:T(8,128)(2,1)S(1)}, u32[]{:S(2)}, u32[]{:S(2)}) collective-permute-start(bf16[8,128,128]{2,1,0:T(8,128)(2,1)S(1)} %stack.1), channel_id=1, source_target_pairs={{0,1},{1,0},{2,3},{3,2},{4,5},{5,4},{6,7},{7,6},{8,9},{9,8},{10,11... | collective-permute-start | bytes 786440 | tf_op jit(solution)/shard_map/ppermute | solution.py:678
  38.3 10.9 %all-to-all-start.1 = ((bf16[16,24,128]{2,1,0:T(8,128)(2,1)}), bf16[16,24,128]{2,1,0:T(8,128)(2,1)S(1)}, u32[]{:S(2)}, u32[]{:S(2)}) async-start(bf16[16,24,128]{2,1,0:T(8,128)(2,1)} %get-tuple-element.58), calls=%async_computation.1 | async-start | bytes 196608 | tf_op jit(solution)/shard_map/all_to_all | solution.py:679
  41.8 7.4 %copy-start.6 = (bf16[2,2,4096]{2,1,0:T(2,128)(2,1)S(1)}, bf16[2,2,4096]{2,1,0:T(2,128)(2,1)}, u32[]{:S(2)}) copy-start(bf16[2,2,4096]{2,1,0:T(2,128)(2,1)} %new_gate.1) | copy-start | bytes 98308
  41.9 7.3 %copy-start.7 = (f32[4096]{0:T(1024)S(1)}, f32[4096]{0:T(1024)}, u32[]{:S(2)}) copy-start(f32[4096]{0:T(1024)} %param.33) | copy-start | bytes 49156

commit v6 on v5

--- a/solution.py
+++ b/solution.py
@@ -211,7 +211,7 @@
         out[r] = conv(rows, taps)
         return carry
 
-    lax.fori_loop(0, prompts, one, 0, unroll=4)
+    lax.fori_loop(0, prompts, one, 0, unroll=8)
 
 
 def before_kernel(
@@ -301,7 +301,7 @@
             rows_ref[i, pl.ds(r, 1), :] = jnp.concatenate([low, high], axis=1)
         return carry
 
-    lax.fori_loop(0, prompts, fetch, 0, unroll=4)
+    lax.fori_loop(0, prompts, fetch, 0, unroll=8)
     raws = [tail_ref[0], tail_ref[1], tail_ref[2], rows_ref[0], rows_ref[1]]
     for i in range(2):
         total = sum(raws[i + k] * taps[k : k + 1] for k in range(CONVK))
@@ -374,7 +374,7 @@
         square = jnp.sum(gated * gated, axis=1, keepdims=True)
         return jnp.where(column_of == r, square, squares)
 
-    squares = lax.fori_loop(0, prompts, one, jnp.zeros((span, LANES), F32), unroll=4)
+    squares = lax.fori_loop(0, prompts, one, jnp.zeros((span, LANES), F32), unroll=8)
     turned = squares.T
     half = prompts // 2
     packed = jnp.concatenate([turned[0:half, :], turned[half:prompts, :]], axis=1)
@@ -585,10 +585,10 @@
         cost_estimate=cost(3),
         name="pack_cache",
     )(owners, cache_rows)
-    kept = [kept[0]] + [
-        lax.ppermute(kept[m], "tensor", [(i, i ^ m) for i in range(chips)])
-        for m in range(1, chips)
-    ]
+    kept = list(kept)
+    first = (1, 3, 6, 7, 5, 4, 2)
+    for m in (*first, *range(len(first) + 1, chips)):
+        kept[m] = lax.ppermute(kept[m], "tensor", [(i, i ^ m) for i in range(chips)])
     before = pl.pallas_call(
         before_kernel,
         out_shape=(

time: 51.3 us -> 51.3 us (level)
  no operation moved by 1% of the time
where the time goes in v6:
time: 51.3 us; the launch traced here: 50.9 us
  starting transfers between devices  23.7 us (46%)
  Pallas kernels  17.8 us (35%)
  waiting for transfers between devices  7.91 us (15%)
  between operations  0.86 us (2%)
  local copies, waits for them, and re-layouts  0.71 us (1%)
    ppermute x7, starting transfers between devices, local(): lax.ppermute(kept[m], 'tensor', [(i, i ^ m) for i in range(chips)])  12.5 us
    all_to_all x1, starting transfers between devices, local(): recv = lax.all_to_all(send, AXES, split_axis=0, concat_axis=0, tiled=True)  7.53 us
    pallas_call x1, Pallas kernels, local(): pl.pallas_call(main_kernel, grid=(1,), out_shape=(jax.ShapeDtypeStruct((p...  5.01 us
    ppermute x7, waiting for transfers between devices, local(): lax.ppermute(kept[m], 'tensor', [(i, i ^ m) for i in range(chips)])  4.91 us
    pallas_call x1, Pallas kernels, local(): pl.pallas_call(cache_kernel, out_shape=(jax.ShapeDtypeStruct((page_table....  4.32 us
    all_to_all x1, starting transfers between devices, local(): fin_got = lax.all_to_all(fin, AXES, split_axis=0, concat_axis=0, tiled=True)  3.52 us
    all_to_all x1, waiting for transfers between devices, local(): fin_got = lax.all_to_all(fin, AXES, split_axis=0, concat_axis=0, tiled=True)  2.99 us
    pallas_call x1, Pallas kernels, local(): pl.pallas_call(before_kernel, out_shape=(jax.ShapeDtypeStruct((prompts, s...  2.34 us
  transfers between devices with their start and end apart: 11, of which 3 were waited for; matrix products, arithmetic and copies ran while one was open for 0% of the time, Pallas kernels for 25%

profile of v6, /device:TPU:0, one launch (start us, length us, event | category | flops | bytes accessed | tf_op | source)
XLA Modules:
  0.0 50.9 jit_solution(9213319652866921936)
XLA Ops:
  0.6 0.0 copy-start.2
  0.6 2.1 %pack.1 = bf16[16,80,128]{2,1,0:T(8,128)(2,1)} custom-call(bf16[1,64,2048]{2,1,0:T(8,128)(2,1)} %coeff.2, bf16[2,2,4096]{2,1,0:T(2,128)(2,1)} %hidden_in.1, bf16[2,2,2048]{2,1,0:T(2,128)(2,1)} %coeff_new_in.1, f32[2,2,64]{2,1,0:T(2,128)} %step_in.1), custom_call_target="tpu_custom_call" | custom-call | tf_op jit(solution)/shard_map/pack/pallas_call | solution.py:563
  2.8 0.0 copy-start
  2.8 7.5 %all-to-all-start = ((bf16[16,80,128]{2,1,0:T(8,128)(2,1)}), bf16[16,80,128]{2,1,0:T(8,128)(2,1)S(1)}, u32[]{:S(2)}, u32[]{:S(2)}) async-start(bf16[16,80,128]{2,1,0:T(8,128)(2,1)} %pack.1), calls=%async_computation | async-start | bytes 655360 | tf_op jit(solution)/shard_map/all_to_all | solution.py:576
  10.3 0.0 copy-start.10
  10.3 0.0 copy-done.2
  10.4 0.6 %copy-done.10 = s32[16,1]{0,1:T(1,128)S(1)} copy-done((s32[16,1]{0,1:T(1,128)S(1)}, s32[16,1]{0,1:T(1,128)}, u32[]{:S(2)}) %copy-start.10) | copy-done | bytes 88
  11.0 0.8 %pack_cache.1 = (bf16[2,128,128]{2,1,0:T(8,128)(2,1)S(1)}, bf16[2,128,128]{2,1,0:T(8,128)(2,1)S(1)}, bf16[2,128,128]{2,1,0:T(8,128)(2,1)S(1)}, bf16[2,128,128]{2...) custom-call(s32[16]{0:T(128)S(1)} %bitcast.3, ...), custom_call_target="tpu_custom_call" | custom-call | bytes 10500000 | tf_op jit(solution)/shard_map/pack_cache/pallas_call | solution.py:578
  11.8 2.0 %collective-permute-start = (bf16[2,128,128]{2,1,0:T(8,128)(2,1)S(1)}, bf16[2,128,128]{2,1,0:T(8,128)(2,1)S(1)}, u32[]{:S(2)}, u32[]{:S(2)}) collective-permute-start(bf16[2,128,128]{2,1,0:T(8,128)(2,1)S(1)} %get-tuple-element.40), channel_id=1, source_target_pairs={{0,2},{2,0},{4,6},{6,4},{8,10},{10,8},{12,14},{14,12},{1,3},{3,1},... | collective-permute-start | bytes 196616 | tf_op jit(solution)/shard_map/ppermute | solution.py:591
  13.8 1.5 %collective-permute-start.1 = (bf16[2,128,128]{2,1,0:T(8,128)(2,1)S(1)}, bf16[2,128,128]{2,1,0:T(8,128)(2,1)S(1)}, u32[]{:S(2)}, u32[]{:S(2)}) collective-permute-start(bf16[2,128,128]{2,1,0:T(8,128)(2,1)S(1)} %get-tuple-element.41), channel_id=1, source_target_pairs={{0,6},{2,4},{4,2},{6,0},{8,14},{10,12},{12,10},{14,8},{1,7},{3,5},... | collective-permute-start | bytes 196616 | tf_op jit(solution)/shard_map/ppermute | solution.py:591
  15.3 2.4 %collective-permute-start.2 = (bf16[2,128,128]{2,1,0:T(8,128)(2,1)S(1)}, bf16[2,128,128]{2,1,0:T(8,128)(2,1)S(1)}, u32[]{:S(2)}, u32[]{:S(2)}) collective-permute-start(bf16[2,128,128]{2,1,0:T(8,128)(2,1)S(1)} %get-tuple-element.42), channel_id=1, source_target_pairs={{0,12},{2,14},{4,8},{6,10},{8,4},{10,6},{12,0},{14,2},{1,13},{3,15... | collective-permute-start | bytes 196616 | tf_op jit(solution)/shard_map/ppermute | solution.py:591
  17.7 0.0 copy-done
  17.7 0.0 copy-done.3
  17.7 0.0 copy-done.5
  17.7 0.0 copy-done.14
  17.7 0.0 copy-done.11
  17.7 0.0 copy-done.12
  17.8 2.3 %before.1 = (bf16[16,64,256]{2,1,0:T(8,128)(2,1)S(1)}, f32[3,16,256]{2,1,0:T(8,128)S(1)}, f32[8,256]{1,0:T(8,128)S(1)}, f32[4,16,128]{2,1,0:T(8,128)S(1)}, f32[4,16,128]{2,1,0:T(8,128)S(1)}) custom-call(s32[16]{0:T(128)S(1)} %copy-done.11, f32[64]{0:T(128)S(1)} %copy-done.12, f32[64]{0:T(128)S(1)} %copy-done.13, f32[64]{0:T(128)S(1)} %copy-done.14, ...), custom_call_target="tpu_custom_call" | custom-call | bytes 14000000 | tf_op jit(solution)/shard_map/before/pallas_call | solution.py:592
  20.1 0.0 collective-permute-done.refs_1_
  20.1 0.0 collective-permute-done.1.refs_3_
  20.1 3.4 %collective-permute-done.2.refs_6_ = bf16[2,128,128]{2,1,0:T(8,128)(2,1)S(1)} collective-permute-done((bf16[2,128,128]{2,1,0:T(8,128)(2,1)S(1)}, bf16[2,128,128]{2,1,0:T(8,128)(2,1)S(1)}, u32[]{:S(2)}, u32[]{:S(2)}) %collective-permute-start.2) | collective-permute-done | bytes 65568 | tf_op jit(solution)/shard_map/ppermute | solution.py:591
  23.5 0.0 all-to-all-done.recv.new_ref
  23.5 1.4 %coeff.3.mine = bf16[16,80,128]{2,1,0:T(8,128)(2,1)S(1)} custom-call(s32[16]{0:T(128)S(1)} %bitcast.4, s32[16]{0:T(128)S(1)} %copy-done.11, bf16[4,2048]{1,0:T(4,128)(2,1)S(1)} %copy-done.9, bf16[16,80,128]{2,1,0:T(8,128)(2,1)S(1)} %all-to-all-done.recv.new_ref), custom_call_target="tpu_custom_call" | custom-call | bytes 7000000 | tf_op jit(solution)/shard_map/coeff/pallas_call | solution.py:615
  24.9 0.1 collective-permute-start.3
  24.9 1.3 %collective-permute-start.4 = (bf16[2,128,128]{2,1,0:T(8,128)(2,1)S(1)}, bf16[2,128,128]{2,1,0:T(8,128)(2,1)S(1)}, u32[]{:S(2)}, u32[]{:S(2)}) collective-permute-start(bf16[2,128,128]{2,1,0:T(8,128)(2,1)S(1)} %get-tuple-element.52), channel_id=1, source_target_pairs={{0,4},{2,6},{4,0},{6,2},{8,12},{10,14},{12,8},{14,10},{1,5},{3,7},... | collective-permute-start | bytes 196616 | tf_op jit(solution)/shard_map/ppermute | solution.py:591
  26.3 0.9 %collective-permute-start.5 = (bf16[2,128,128]{2,1,0:T(8,128)(2,1)S(1)}, bf16[2,128,128]{2,1,0:T(8,128)(2,1)S(1)}, u32[]{:S(2)}, u32[]{:S(2)}) collective-permute-start(bf16[2,128,128]{2,1,0:T(8,128)(2,1)S(1)} %get-tuple-element.54), channel_id=1, source_target_pairs={{0,8},{2,10},{4,12},{6,14},{8,0},{10,2},{12,4},{14,6},{1,9},{3,11}... | collective-permute-start | bytes 196616 | tf_op jit(solution)/shard_map/ppermute | solution.py:591
  27.2 2.9 %collective-permute-start.6 = (bf16[2,128,128]{2,1,0:T(8,128)(2,1)S(1)}, bf16[2,128,128]{2,1,0:T(8,128)(2,1)S(1)}, u32[]{:S(2)}, u32[]{:S(2)}) collective-permute-start(bf16[2,128,128]{2,1,0:T(8,128)(2,1)S(1)} %get-tuple-element.55), channel_id=1, source_target_pairs={{0,10},{2,8},{4,14},{6,12},{8,2},{10,0},{12,6},{14,4},{1,11},{3,9}... | collective-permute-start | bytes 196616 | tf_op jit(solution)/shard_map/ppermute | solution.py:591
  30.1 1.5 %collective-permute-start.7 = (bf16[2,128,128]{2,1,0:T(8,128)(2,1)S(1)}, bf16[2,128,128]{2,1,0:T(8,128)(2,1)S(1)}, u32[]{:S(2)}, u32[]{:S(2)}) collective-permute-start(bf16[2,128,128]{2,1,0:T(8,128)(2,1)S(1)} %get-tuple-element.57), channel_id=1, source_target_pairs={{0,14},{2,12},{4,10},{6,8},{8,6},{10,4},{12,2},{14,0},{1,15},{3,13... | collective-permute-start | bytes 196616 | tf_op jit(solution)/shard_map/ppermute | solution.py:591
  31.6 0.0 collective-permute-done.3.other
  31.6 5.0 %main.1 = (f32[16,64,256]{2,1,0:T(8,128)S(1)}, bf16[16,24,128]{2,1,0:T(8,128)(2,1)}) custom-call(s32[16]{0:T(128)S(1)} %bitcast.5, s32[16]{0:T(128)S(1)} %copy-done.11, bf16[4,4096]{1,0:T(4,128)(2,1)S(1)} %copy-done.3, bf16[16,80,128]{2,1,0:T(8,128)(2,1)S(1)} %coeff.3.mine, bf16[16,80,128]{2,1,0:T(8,128)(2,1)S(1)} %collective-permute-done.3.other, ...), custom_call_target="tpu_custom_call" | custom-call | bytes 35000000 | tf_op jit(solution)/shard_map/main/pallas_call | solution.py:634
  36.6 0.0 collective-permute-done.4.refs_2_
  36.6 0.0 collective-permute-done.5.refs_4_
  36.6 1.5 %collective-permute-done.6.refs_5_ = bf16[2,128,128]{2,1,0:T(8,128)(2,1)S(1)} collective-permute-done((bf16[2,128,128]{2,1,0:T(8,128)(2,1)S(1)}, bf16[2,128,128]{2,1,0:T(8,128)(2,1)S(1)}, u32[]{:S(2)}, u32[]{:S(2)}) %collective-permute-start.6) | collective-permute-done | bytes 65568 | tf_op jit(solution)/shard_map/ppermute | solution.py:591
  38.1 0.0 collective-permute-done.7.refs_7_
  38.1 0.0 copy-start.4
  38.1 0.0 copy-start.8
  38.2 0.0 copy-start.15
  38.2 0.1 collective-permute-start.8
  38.2 3.5 %all-to-all-start.1 = ((bf16[16,24,128]{2,1,0:T(8,128)(2,1)}), bf16[16,24,128]{2,1,0:T(8,128)(2,1)S(1)}, u32[]{:S(2)}, u32[]{:S(2)}) async-start(bf16[16,24,128]{2,1,0:T(8,128)(2,1)} %get-tuple-element.58), calls=%async_computation.1 | async-start | bytes 196608 | tf_op jit(solution)/shard_map/all_to_all | solution.py:679
  41.8 0.0 copy-start.6
  41.8 0.0 collective-permute-done.8.crossed
  41.8 0.0 copy-done.4
  41.8 0.0 copy-done.8
  41.8 0.0 copy-done.15
  41.8 0.0 copy-start.7
  41.8 4.3 %cache.3 = (bf16[8,16,2048]{2,1,0:T(8,128)(2,1)}, bf16[2,2,8192]{2,1,0:T(2,128)(2,1)}) custom-call(s32[16]{0:T(128)S(1)} %bitcast.6, s32[16]{0:T(128)S(1)} %copy-done.11, s32[1,8]{1,0:T(1,128)S(1)} %copy-done.15, bf16[2,2,8192]{2,1,0:T(2,128)(2,1)S(1)} %copy-done.4, bf16[2,2,2048]{2,1,0:T(2,128)(2,1)S(1)} %copy-done.8, ...), custom_call_target="tpu_custom_call" | custom-call | bytes 17500000 | tf_op jit(solution)/shard_map/cache/pallas_call | solution.py:681
  46.2 3.0 %all-to-all-done.1.fin = bf16[16,24,128]{2,1,0:T(8,128)(2,1)S(1)} async-done(((bf16[16,24,128]{2,1,0:T(8,128)(2,1)}), bf16[16,24,128]{2,1,0:T(8,128)(2,1)S(1)}, u32[]{:S(2)}, u32[]{:S(2)}) %all-to-all-start.1) | async-done | bytes 98336 | tf_op jit(solution)/shard_map/all_to_all | solution.py:679
  49.2 1.8 %final.1 = (bf16[16,64,256]{2,1,0:T(8,128)(2,1)}, bf16[2,2,4096]{2,1,0:T(2,128)(2,1)}) custom-call(s32[16]{0:T(128)S(1)} %bitcast.7, s32[16]{0:T(128)S(1)} %copy-done.11, f32[1,4096]{1,0:T(1,128)S(1)} %bitcast.2, bf16[16,24,128]{2,1,0:T(8,128)(2,1)S(1)} %all-to-all-done.1.fin, f32[16,64,256]{2,1,0:T(8,128)S(1)} %get-tuple-element.69.gated, ...), custom_call_target="tpu_custom_call" | custom-call | tf_op jit(solution)/shard_map/final/pallas_call | solution.py:696
  (14 shorter events, 0.0 us)
Async XLA Ops:
  0.6 9.7 %copy-start.2 = (bf16[16,4,2048]{2,1,0:T(4,128)(2,1)S(1)}, bf16[16,4,2048]{2,1,0:T(4,128)(2,1)}, u32[]{:S(2)}) copy-start(bf16[16,4,2048]{2,1,0:T(4,128)(2,1)} %cache.2) | copy-start | bytes 786436
  2.8 14.9 %copy-start = (bf16[16,64,256]{2,1,0:T(8,128)(2,1)S(1)}, bf16[16,64,256]{2,1,0:T(8,128)(2,1)}, u32[]{:S(2)}) copy-start(bf16[16,64,256]{2,1,0:T(8,128)(2,1)} %hidden.1) | copy-start | bytes 1572868
  2.8 20.7 %all-to-all-start = ((bf16[16,80,128]{2,1,0:T(8,128)(2,1)}), bf16[16,80,128]{2,1,0:T(8,128)(2,1)S(1)}, u32[]{:S(2)}, u32[]{:S(2)}) async-start(bf16[16,80,128]{2,1,0:T(8,128)(2,1)} %pack.1), calls=%async_computation | async-start | bytes 655360 | tf_op jit(solution)/shard_map/all_to_all | solution.py:576
  10.3 0.7 %copy-start.10 = (s32[16,1]{0,1:T(1,128)S(1)}, s32[16,1]{0,1:T(1,128)}, u32[]{:S(2)}) copy-start(s32[16,1]{0,1:T(1,128)} %param.26) | copy-start | bytes 196
  11.0 6.7 %copy-start.3 = (bf16[4,4096]{1,0:T(4,128)(2,1)S(1)}, bf16[4,4096]{1,0:T(4,128)(2,1)}, u32[]{:S(2)}) copy-start(bf16[4,4096]{1,0:T(4,128)(2,1)} %taps_ref.5) | copy-start | bytes 98308
  11.0 6.7 %copy-start.5 = (f32[4,16,64]{2,1,0:T(8,128)S(1)}, f32[4,16,64]{2,1,0:T(8,128)}, u32[]{:S(2)}) copy-start(f32[4,16,64]{2,1,0:T(8,128)} %step.1) | copy-start | bytes 49156
  11.8 8.3 %collective-permute-start = (bf16[2,128,128]{2,1,0:T(8,128)(2,1)S(1)}, bf16[2,128,128]{2,1,0:T(8,128)(2,1)S(1)}, u32[]{:S(2)}, u32[]{:S(2)}) collective-permute-start(bf16[2,128,128]{2,1,0:T(8,128)(2,1)S(1)} %get-tuple-element.40), channel_id=1, source_target_pairs={{0,2},{2,0},{4,6},{6,4},{8,10},{10,8},{12,14},{14,12},{1,3},{3,1},... | collective-permute-start | bytes 196616 | tf_op jit(solution)/shard_map/ppermute | solution.py:591
  13.8 3.9 %copy-start.14 = (f32[64]{0:T(128)S(1)}, f32[64]{0:T(128)}, u32[]{:S(2)}) copy-start(f32[64]{0:T(128)} %skip.1) | copy-start | bytes 772
  13.8 3.9 %copy-start.11 = (s32[16]{0:T(128)S(1)}, s32[16]{0:T(128)}, u32[]{:S(2)}) copy-start(s32[16]{0:T(128)} %lengths.9) | copy-start | bytes 196
  13.8 3.9 %copy-start.12 = (f32[64]{0:T(128)S(1)}, f32[64]{0:T(128)}, u32[]{:S(2)}) copy-start(f32[64]{0:T(128)} %bias.1) | copy-start | bytes 772
  13.8 3.9 %copy-start.13 = (f32[64]{0:T(128)S(1)}, f32[64]{0:T(128)}, u32[]{:S(2)}) copy-start(f32[64]{0:T(128)} %decay.1) | copy-start | bytes 772
  13.8 6.3 %collective-permute-start.1 = (bf16[2,128,128]{2,1,0:T(8,128)(2,1)S(1)}, bf16[2,128,128]{2,1,0:T(8,128)(2,1)S(1)}, u32[]{:S(2)}, u32[]{:S(2)}) collective-permute-start(bf16[2,128,128]{2,1,0:T(8,128)(2,1)S(1)} %get-tuple-element.41), channel_id=1, source_target_pairs={{0,6},{2,4},{4,2},{6,0},{8,14},{10,12},{12,10},{14,8},{1,7},{3,5},... | collective-permute-start | bytes 196616 | tf_op jit(solution)/shard_map/ppermute | solution.py:591
  15.3 8.2 %copy-start.9 = (bf16[4,2048]{1,0:T(4,128)(2,1)S(1)}, bf16[4,2048]{1,0:T(4,128)(2,1)}, u32[]{:S(2)}) copy-start(bf16[4,2048]{1,0:T(4,128)(2,1)} %taps_ref.4) | copy-start | bytes 49156
  15.3 16.2 %copy-start.1 = (bf16[16,64,256]{2,1,0:T(8,128)(2,1)S(1)}, bf16[16,64,256]{2,1,0:T(8,128)(2,1)}, u32[]{:S(2)}) copy-start(bf16[16,64,256]{2,1,0:T(8,128)(2,1)} %gate.1) | copy-start | bytes 1572868
  15.3 8.1 %collective-permute-start.2 = (bf16[2,128,128]{2,1,0:T(8,128)(2,1)S(1)}, bf16[2,128,128]{2,1,0:T(8,128)(2,1)S(1)}, u32[]{:S(2)}, u32[]{:S(2)}) collective-permute-start(bf16[2,128,128]{2,1,0:T(8,128)(2,1)S(1)} %get-tuple-element.42), channel_id=1, source_target_pairs={{0,12},{2,14},{4,8},{6,10},{8,4},{10,6},{12,0},{14,2},{1,13},{3,15... | collective-permute-start | bytes 196616 | tf_op jit(solution)/shard_map/ppermute | solution.py:591
  24.9 6.7 %collective-permute-start.3 = (bf16[16,80,128]{2,1,0:T(8,128)(2,1)S(1)}, bf16[16,80,128]{2,1,0:T(8,128)(2,1)S(1)}, u32[]{:S(2)}, u32[]{:S(2)}) collective-permute-start(bf16[16,80,128]{2,1,0:T(8,128)(2,1)S(1)} %coeff.3.mine), channel_id=1, source_target_pairs={{0,1},{1,0},{2,3},{3,2},{4,5},{5,4},{6,7},{7,6},{8,9},{9,8},{10,11... | collective-permute-start | bytes 983048 | tf_op jit(solution)/shard_map/ppermute | solution.py:631
  24.9 11.6 %collective-permute-start.4 = (bf16[2,128,128]{2,1,0:T(8,128)(2,1)S(1)}, bf16[2,128,128]{2,1,0:T(8,128)(2,1)S(1)}, u32[]{:S(2)}, u32[]{:S(2)}) collective-permute-start(bf16[2,128,128]{2,1,0:T(8,128)(2,1)S(1)} %get-tuple-element.52), channel_id=1, source_target_pairs={{0,4},{2,6},{4,0},{6,2},{8,12},{10,14},{12,8},{14,10},{1,5},{3,7},... | collective-permute-start | bytes 196616 | tf_op jit(solution)/shard_map/ppermute | solution.py:591
  26.3 10.3 %collective-permute-start.5 = (bf16[2,128,128]{2,1,0:T(8,128)(2,1)S(1)}, bf16[2,128,128]{2,1,0:T(8,128)(2,1)S(1)}, u32[]{:S(2)}, u32[]{:S(2)}) collective-permute-start(bf16[2,128,128]{2,1,0:T(8,128)(2,1)S(1)} %get-tuple-element.54), channel_id=1, source_target_pairs={{0,8},{2,10},{4,12},{6,14},{8,0},{10,2},{12,4},{14,6},{1,9},{3,11}... | collective-permute-start | bytes 196616 | tf_op jit(solution)/shard_map/ppermute | solution.py:591
  27.2 10.9 %collective-permute-start.6 = (bf16[2,128,128]{2,1,0:T(8,128)(2,1)S(1)}, bf16[2,128,128]{2,1,0:T(8,128)(2,1)S(1)}, u32[]{:S(2)}, u32[]{:S(2)}) collective-permute-start(bf16[2,128,128]{2,1,0:T(8,128)(2,1)S(1)} %get-tuple-element.55), channel_id=1, source_target_pairs={{0,10},{2,8},{4,14},{6,12},{8,2},{10,0},{12,6},{14,4},{1,11},{3,9}... | collective-permute-start | bytes 196616 | tf_op jit(solution)/shard_map/ppermute | solution.py:591
  30.1 8.0 %collective-permute-start.7 = (bf16[2,128,128]{2,1,0:T(8,128)(2,1)S(1)}, bf16[2,128,128]{2,1,0:T(8,128)(2,1)S(1)}, u32[]{:S(2)}, u32[]{:S(2)}) collective-permute-start(bf16[2,128,128]{2,1,0:T(8,128)(2,1)S(1)} %get-tuple-element.57), channel_id=1, source_target_pairs={{0,14},{2,12},{4,10},{6,8},{8,6},{10,4},{12,2},{14,0},{1,15},{3,13... | collective-permute-start | bytes 196616 | tf_op jit(solution)/shard_map/ppermute | solution.py:591
  38.1 3.7 %copy-start.4 = (bf16[2,2,8192]{2,1,0:T(2,128)(2,1)S(1)}, bf16[2,2,8192]{2,1,0:T(2,128)(2,1)}, u32[]{:S(2)}) copy-start(bf16[2,2,8192]{2,1,0:T(2,128)(2,1)} %query.1) | copy-start | bytes 196612
  38.1 3.7 %copy-start.8 = (bf16[2,2,2048]{2,1,0:T(2,128)(2,1)S(1)}, bf16[2,2,2048]{2,1,0:T(2,128)(2,1)}, u32[]{:S(2)}) copy-start(bf16[2,2,2048]{2,1,0:T(2,128)(2,1)} %cache_new.1) | copy-start | bytes 49156
  38.2 3.7 %copy-start.15 = (s32[1,8]{1,0:T(1,128)S(1)}, s32[1,8]{1,0:T(1,128)}, u32[]{:S(2)}) copy-start(s32[1,8]{1,0:T(1,128)} %pages.1) | copy-start | bytes 100
  38.2 3.6 %collective-permute-start.8 = (bf16[8,128,128]{2,1,0:T(8,128)(2,1)S(1)}, bf16[8,128,128]{2,1,0:T(8,128)(2,1)S(1)}, u32[]{:S(2)}, u32[]{:S(2)}) collective-permute-start(bf16[8,128,128]{2,1,0:T(8,128)(2,1)S(1)} %stack.1), channel_id=1, source_target_pairs={{0,1},{1,0},{2,3},{3,2},{4,5},{5,4},{6,7},{7,6},{8,9},{9,8},{10,11... | collective-permute-start | bytes 786440 | tf_op jit(solution)/shard_map/ppermute | solution.py:678
  38.2 10.9 %all-to-all-start.1 = ((bf16[16,24,128]{2,1,0:T(8,128)(2,1)}), bf16[16,24,128]{2,1,0:T(8,128)(2,1)S(1)}, u32[]{:S(2)}, u32[]{:S(2)}) async-start(bf16[16,24,128]{2,1,0:T(8,128)(2,1)} %get-tuple-element.58), calls=%async_computation.1 | async-start | bytes 196608 | tf_op jit(solution)/shard_map/all_to_all | solution.py:679
  41.8 7.4 %copy-start.6 = (bf16[2,2,4096]{2,1,0:T(2,128)(2,1)S(1)}, bf16[2,2,4096]{2,1,0:T(2,128)(2,1)}, u32[]{:S(2)}) copy-start(bf16[2,2,4096]{2,1,0:T(2,128)(2,1)} %new_gate.1) | copy-start | bytes 98308
  41.8 7.3 %copy-start.7 = (f32[4096]{0:T(1024)S(1)}, f32[4096]{0:T(1024)}, u32[]{:S(2)}) copy-start(f32[4096]{0:T(1024)} %param.33) | copy-start | bytes 49156
